TPU v7x, 32 devices: a whole 2x2x4 slice. The times are simulated.
32 devices in a mesh: parts: 2 (over y), wide: 4 (over x, core), narrow: 4 (over z).
Axes of the slice: x: 2, y: 2, z: 4, core: 2. Of those that a mesh axis runs over, the one named last changes fastest.
Arguments:
- hist_events: bfloat16 [8, 2048, 512], P(('parts', 'wide'), 'narrow'), parts along dimension 0, may hold values from -6 to 6
- query_events: bfloat16 [8, 1024, 512], P(('parts', 'wide'), 'narrow'), parts along dimension 0, may hold values from -6 to 6
- hist_lengths: int32 [8], P(('parts', 'wide')), parts along dimension 0, may hold values from 512 to 2048
- time_buckets: int32 [8, 2048], P(('parts', 'wide'), 'narrow'), parts along dimension 0, may hold values from 0 to 127
- w_key: bfloat16 [512, 1024], replicated, may hold values from -0.25 to 0.25
- w_query: bfloat16 [512, 1024], replicated, may hold values from -0.25 to 0.25
- bias_table: bfloat16 [128, 8], replicated, may hold values from -3 to 3
- out_gain: float32 [512], replicated, may hold values from 0.1 to 1.9
- w_out: bfloat16 [512, 512], replicated, may hold values from -0.25 to 0.25
Outputs:
- layer_out: bfloat16 [8, 1024, 512], P(('parts', 'wide'), 'narrow'), parts along dimension 0
There are 2 independent parts, one for each index of `parts`. A program takes and returns all parts, laid end to end along the dimension named above; an argument that names none is the same for every part. Nothing has to cross between parts.
All inputs are finite; a program needn't handle non-finite values.
Results may differ from a plain program's by a relative error of at most 0.0048.
Values may be sent and summed in bfloat16 or wider, within the bound.
No kernel may reach another device: no remote copies, remote signals or barrier semaphores. Data moves between devices by JAX's collectives and lax.ppermute only.
A program may use at most 128 MiB of HBM per device.

v0:
```python
import math

import jax
import jax.numpy as jnp
from jax import lax
from jax.sharding import PartitionSpec as P

HEADS = 8


def attend(
    query_states, key_states, value_states, bias_keys, positions, length, shard_rows, keep_below
):
    q_rows = query_states.shape[0]
    key_rows = key_states.shape[0]
    head_size = key_states.shape[1] // HEADS
    score_scale = 1.0 / math.sqrt(head_size)
    block_rows = 128
    blocks = key_rows // block_rows
    query_heads = query_states.reshape(q_rows, HEADS, head_size)
    key_blocks = key_states.reshape(blocks, block_rows, HEADS, head_size)
    value_blocks = value_states.reshape(blocks, block_rows, HEADS, head_size)
    bias_blocks = bias_keys.reshape(blocks, block_rows, HEADS)
    position_blocks = positions.reshape(blocks, block_rows)

    def absorb_block(running, item):
        key_block, value_block, bias_block, position = item
        live_rows = (position < length) & (position % shard_rows < keep_below)
        scores = jnp.einsum(
            "qhd,khd->hqk", query_heads, key_block, preferred_element_type=jnp.float32
        )
        scores = scores * score_scale + bias_block.astype(jnp.float32).T[:, None, :]
        live = live_rows.astype(jnp.float32)
        weights = (jax.nn.silu(scores) * live[None, None, :]).astype(jnp.bfloat16)
        contrib = jnp.einsum(
            "hqk,khd->qhd", weights, value_block, preferred_element_type=jnp.float32
        )
        return (running + contrib, None)

    running, _ = lax.scan(
        absorb_block,
        jnp.zeros((q_rows, HEADS, head_size), jnp.float32),
        (key_blocks, value_blocks, bias_blocks, position_blocks),
    )
    return running


def on_device(
    hist_events,
    query_events,
    hist_lengths,
    time_buckets,
    w_key,
    w_query,
    bias_table,
    out_gain,
    w_out,
):
    history = hist_events[0]
    queries_in = query_events[0]
    length = hist_lengths[0]
    buckets = time_buckets[0]
    width = history.shape[1]
    shard_rows = history.shape[0]
    key_value = jnp.dot(history, w_key, preferred_element_type=jnp.float32)
    key_states = jax.nn.silu(key_value[:, :width]).astype(jnp.bfloat16)
    value_states = key_value[:, width:].astype(jnp.bfloat16)
    query_gate = jnp.dot(queries_in, w_query, preferred_element_type=jnp.float32)
    query_states = jax.nn.silu(query_gate[:, :width]).astype(jnp.bfloat16)
    gate_states = jax.nn.silu(query_gate[:, width:])
    onehot = (buckets[:, None] == jnp.arange(bias_table.shape[0], dtype=jnp.int32)[None, :]).astype(
        jnp.bfloat16
    )
    bias_keys = jnp.dot(onehot, bias_table, preferred_element_type=jnp.float32).astype(jnp.bfloat16)
    keep_below = jnp.int32(shard_rows)
    own_positions = lax.axis_index("narrow") * shard_rows + jnp.arange(shard_rows, dtype=jnp.int32)
    piece_rows = lax.all_gather(query_states, "narrow", axis=0, tiled=True)
    running = attend(
        piece_rows,
        key_states,
        value_states,
        bias_keys,
        own_positions,
        length,
        shard_rows,
        keep_below,
    )
    terms = running.reshape(piece_rows.shape[0], width)
    attended = lax.psum_scatter(terms, "narrow", scatter_dimension=0, tiled=True)
    center = jnp.mean(attended, axis=-1, keepdims=True)
    spread = jnp.mean(jnp.square(attended - center), axis=-1, keepdims=True)
    normed = (attended - center) * lax.rsqrt(spread + 1e-05)
    mixed = (normed * out_gain * gate_states).astype(jnp.bfloat16)
    result = queries_in.astype(jnp.float32) + jnp.dot(
        mixed, w_out, preferred_element_type=jnp.float32
    )
    return result.astype(jnp.bfloat16)[None]


def solution(mesh):
    in_specs = (
        P(("parts", "wide"), "narrow", None),
        P(("parts", "wide"), "narrow", None),
        P(("parts", "wide")),
        P(("parts", "wide"), "narrow"),
        P(),
        P(),
        P(),
        P(),
        P(),
    )
    out_specs = P(("parts", "wide"), "narrow", None)
    return jax.shard_map(
        on_device, mesh=mesh, in_specs=in_specs, out_specs=out_specs, check_vma=False
    )
```

profile of v0, /device:TPU:1, one launch (start us, length us, event | category | flops | bytes accessed | tf_op | source)
XLA Modules:
  0.0 116.6 jit_solution(13096410062211780048)
XLA Ops:
  6.5 1.8 %fusion.23 = f32[256,1024]{1,0:T(8,128)S(1)} fusion(bf16[512,1024]{1,0:T(8,128)(2,1)} %param.16, bf16[1,256,512]{2,1,0:T(8,128)(2,1)} %param.12), kind=kOutput, calls=%fused_computation.36 | convolution fusion | flops 268435456 | bytes 2359296 | tf_op jit(solution)/shard_map/dot_general | solution.py:68
  8.4 1.0 copy-done.1
  9.4 0.8 multiply_convert_fusion.2
  10.3 1.8 %fusion.21 = f32[512,1024]{1,0:T(8,128)S(1)} fusion(bf16[512,1024]{1,0:T(8,128)(2,1)S(1)} %copy-done, bf16[1,512,512]{2,1,0:T(8,128)(2,1)} %param.11), kind=kOutput, calls=%fused_computation.31 | convolution fusion | flops 536870912 | bytes 3670016 | tf_op jit(solution)/shard_map/dot_general | solution.py:65
  12.1 0.9 slice.26
  13.0 2.4 %reshape.63 = bf16[4,128,8,64]{3,2,1,0:T(8,128)(2,1)} reshape(bf16[512,512]{1,0:T(8,128)(2,1)} %slice.26) | data formatting | bytes 1048576 | tf_op jit(solution)/shard_map/reshape | solution.py:22
  15.3 2.5 %copy.19 = bf16[4,128,8,64]{1,3,2,0:T(8,128)(2,1)} copy(bf16[4,128,8,64]{3,2,1,0:T(8,128)(2,1)} %reshape.63) | data formatting | bytes 1048576
  17.8 1.1 multiply_convert_fusion
  18.9 1.7 %reshape.64 = bf16[4,128,8,64]{3,2,1,0:T(8,128)(2,1)S(1)} reshape(bf16[512,512]{1,0:T(8,128)(2,1)} %multiply_convert_fusion) | data formatting | bytes 1048576 | tf_op jit(solution)/shard_map/reshape | solution.py:21
  20.6 1.4 %copy.20 = bf16[4,128,8,64]{1,3,2,0:T(8,128)(2,1)} copy(bf16[4,128,8,64]{3,2,1,0:T(8,128)(2,1)S(1)} %reshape.64) | data formatting | bytes 1048576
  22.2 18.0 %all-gather.2.cloned.1.call-done = bf16[1024,512]{1,0:T(8,128)(2,1)} async-done(((bf16[256,512]{1,0:T(8,128)(2,1)}), bf16[1024,512]{1,0:T(8,128)(2,1)}) %all-gather.2.cloned.1.call-update) | async-done | bytes 1048592 | tf_op jit(solution)/shard_map/all_gather | solution.py:77
  40.3 2.3 %copy.18 = bf16[1024,512]{0,1:T(8,128)(2,1)} copy(bf16[1024,512]{1,0:T(8,128)(2,1)} %all-gather.2.cloned.1.call-done) | data formatting | bytes 2097152 | tf_op jit(solution)/shard_map/all_gather | solution.py:77
  42.5 17.2 %while.13 = (s32[]{:T(128)}, f32[1024,8,64]{0,2,1:T(8,128)S(1)}, bf16[4,128,8,64]{1,3,2,0:T(8,128)(2,1)}, bf16[4,128,8,64]{1,3,2,0:T(8,128)(2,1)}, bf16[1024,8,6...) while((s32[]{:T(128)}, f32[1024,8,64]{0,2,1:T(8,128)S(1)}, ...), condition=%wide.region_1.2_spmd.clone, body=%wide.region_0.1_spmd.clone.sunk | while | flops 277875584 | bytes 5517947 | solution.py:40
  43.2 3.6 %bitcast_add_fusion.2 = f32[1024,8,64]{0,2,1:T(8,128)S(1)} fusion(f32[1024,8,64]{0,2,1:T(8,128)S(1)} %get-tuple-element.227, bf16[1024,8,64]{0,2,1:T(8,128)(2,1)} %get-tuple-element.240, f32[128]{0:T(128)S(1)} %and_convert_fusion.2, f32[8,128]{1,0:T(8,128)S(1)} %convert_bitcast_fusion.2, pred[]{:T(512)S(6)} %compare.4, ...), kind=kOutput, calls=%fused_computation.7.clone.1 | convolution fusion | flops 277872640 | bytes 5510657 | tf_op jit(solution)/shard_map/while/body/eval_jaxpr/hqk,khd->qhd/dot_general | solution.py:35
  46.8 0.7 and_convert_fusion.2
  47.5 3.6 %bitcast_add_fusion.2 = f32[1024,8,64]{0,2,1:T(8,128)S(1)} fusion(f32[1024,8,64]{0,2,1:T(8,128)S(1)} %get-tuple-element.227, bf16[1024,8,64]{0,2,1:T(8,128)(2,1)} %get-tuple-element.240, f32[128]{0:T(128)S(1)} %and_convert_fusion.2, f32[8,128]{1,0:T(8,128)S(1)} %convert_bitcast_fusion.2, pred[]{:T(512)S(6)} %compare.4, ...), kind=kOutput, calls=%fused_computation.7.clone.1 | convolution fusion | flops 277872640 | bytes 5510657 | tf_op jit(solution)/shard_map/while/body/eval_jaxpr/hqk,khd->qhd/dot_general | solution.py:35
  51.2 0.7 and_convert_fusion.2
  51.9 3.6 %bitcast_add_fusion.2 = f32[1024,8,64]{0,2,1:T(8,128)S(1)} fusion(f32[1024,8,64]{0,2,1:T(8,128)S(1)} %get-tuple-element.227, bf16[1024,8,64]{0,2,1:T(8,128)(2,1)} %get-tuple-element.240, f32[128]{0:T(128)S(1)} %and_convert_fusion.2, f32[8,128]{1,0:T(8,128)S(1)} %convert_bitcast_fusion.2, pred[]{:T(512)S(6)} %compare.4, ...), kind=kOutput, calls=%fused_computation.7.clone.1 | convolution fusion | flops 277872640 | bytes 5510657 | tf_op jit(solution)/shard_map/while/body/eval_jaxpr/hqk,khd->qhd/dot_general | solution.py:35
  56.2 3.6 %bitcast_add_fusion.2 = f32[1024,8,64]{0,2,1:T(8,128)S(1)} fusion(f32[1024,8,64]{0,2,1:T(8,128)S(1)} %get-tuple-element.227, bf16[1024,8,64]{0,2,1:T(8,128)(2,1)} %get-tuple-element.240, f32[128]{0:T(128)S(1)} %and_convert_fusion.2, f32[8,128]{1,0:T(8,128)S(1)} %convert_bitcast_fusion.2, pred[]{:T(512)S(6)} %compare.4, ...), kind=kOutput, calls=%fused_computation.7.clone.1 | convolution fusion | flops 277872640 | bytes 5510657 | tf_op jit(solution)/shard_map/while/body/eval_jaxpr/hqk,khd->qhd/dot_general | solution.py:35
  59.8 1.9 %copy.21 = f32[1024,512]{1,0:T(8,128)} copy(f32[1024,512]{0,1:T(8,128)S(1)} %bitcast.73) | data formatting | bytes 4194304 | tf_op jit(solution)/shard_map/reshape | solution.py:88
  61.7 43.5 %reduce-scatter.2.cloned.1.call-done = f32[256,512]{1,0:T(8,128)} async-done(((f32[1024,512]{1,0:T(8,128)}), f32[256,512]{1,0:T(8,128)}) %reduce-scatter.2.cloned.1.call-update) | async-done | bytes 524304 | tf_op jit(solution)/shard_map/reduce_scatter | solution.py:89
  105.2 1.2 reduce_sum.18
  106.3 1.2 %multiply_reduce_fusion = f32[256]{0:T(256)S(1)} fusion(f32[256,512]{1,0:T(8,128)} %reduce-scatter.2.cloned.1.call-done, f32[256]{0:T(256)S(1)} %broadcast_multiply_fusion), kind=kLoop, calls=%fused_computation.34 | loop fusion | flops 392960 | bytes 526336 | tf_op jit(solution)/shard_map/reduce_sum | solution.py:91
  107.6 2.1 %fusion.19 = bf16[1,256,512]{2,1,0:T(8,128)(2,1)} fusion(bf16[512,512]{1,0:T(8,128)(2,1)S(1)} %copy-done.5, f32[256,1024]{1,0:T(8,128)S(1)} %copy-done.2, f32[256,512]{1,0:T(8,128)} %reduce-scatter.2.cloned.1.call-done, bf16[1,256,512]{2,1,0:T(8,128)(2,1)S(1)} %copy-done.4, f32[512]{0:T(512)S(1)} %copy-done.8, f32[256]{0:T(256)S(1)} %add_rsqrt_fusion, ...), kind=kOutput, calls=%fused_computation.26 | convolution fusion | flops 135790592 | bytes 2101248 | tf_op jit(solution)/shard_map/dot_general | solution.py:94
  (32 shorter events, 1.7 us)
Async XLA Ops:
  6.5 3.8 %copy-start = (bf16[512,1024]{1,0:T(8,128)(2,1)S(1)}, bf16[512,1024]{1,0:T(8,128)(2,1)}, u32[]{:S(2)}) copy-start(bf16[512,1024]{1,0:T(8,128)(2,1)} %param.15) | copy-start | bytes 3145732
  6.5 33.7 %all-gather.2.cloned.1.call-start = ((), (), s32[]{:S(2)}) async-start(), calls=%async_computation.1 | async-start | bytes 1310720 | tf_op jit(solution)/shard_map/all_gather | solution.py:77
  8.4 1.0 copy-start.1
  10.2 94.9 %reduce-scatter.2.cloned.1.call-start = ((), (), s32[]{:S(2)}) async-start(), calls=%async_computation.2 | async-start | bytes 2621440 | tf_op jit(solution)/shard_map/reduce_scatter | solution.py:89
  17.8 4.1 %copy-start.6 = (bf16[128,8]{0,1:T(8,128)(2,1)S(1)}, bf16[128,8]{0,1:T(8,128)(2,1)}, u32[]{:S(2)}) copy-start(bf16[128,8]{0,1:T(8,128)(2,1)} %param.17) | copy-start | bytes 6148
  17.8 4.1 %copy-start.7 = (s32[1,512]{1,0:T(1,128)S(1)}, s32[1,512]{1,0:T(1,128)}, u32[]{:S(2)}) copy-start(s32[1,512]{1,0:T(1,128)} %param.14) | copy-start | bytes 6148
  22.0 20.6 %copy-start.3 = (f32[1024,8,64]{0,2,1:T(8,128)S(1)}, f32[1024,8,64]{0,2,1:T(8,128)}, u32[]{:S(2)}) copy-start(f32[1024,8,64]{0,2,1:T(8,128)} %custom-call) | copy-start | bytes 6291460
  61.7 45.9 %copy-start.2 = (f32[256,1024]{1,0:T(8,128)S(1)}, f32[256,1024]{1,0:T(8,128)}, u32[]{:S(2)}) copy-start(f32[256,1024]{1,0:T(8,128)} %copy-done.1) | copy-start | bytes 3145732
  61.7 45.9 %copy-start.4 = (bf16[1,256,512]{2,1,0:T(8,128)(2,1)S(1)}, bf16[1,256,512]{2,1,0:T(8,128)(2,1)}, u32[]{:S(2)}) copy-start(bf16[1,256,512]{2,1,0:T(8,128)(2,1)} %param.12) | copy-start | bytes 786436
  61.7 46.0 %copy-start.5 = (bf16[512,512]{1,0:T(8,128)(2,1)S(1)}, bf16[512,512]{1,0:T(8,128)(2,1)}, u32[]{:S(2)}) copy-start(bf16[512,512]{1,0:T(8,128)(2,1)} %param.19) | copy-start | bytes 1572868
  61.7 46.0 %copy-start.8 = (f32[512]{0:T(512)S(1)}, f32[512]{0:T(512)}, u32[]{:S(2)}) copy-start(f32[512]{0:T(512)} %param.18) | copy-start | bytes 6148
Sparse Core Ops, SparseCore 0:
  10.4 29.8 all-gather.1
  61.8 43.3 reduce-scatter.1
where the time goes:
time: 118 us; the launch traced here: 117 us
  waiting for transfers between devices  61.5 us (52%)
  matrix products  20.4 us (17%)
  local copies, waits for them, and re-layouts  14 us (12%)
  between operations  13.5 us (11%)
  other arithmetic  7.03 us (6%)
    reduce_scatter x1, waiting for transfers between devices, on_device(): lax.psum_scatter(terms, 'narrow', scatter_dimension=0, tiled=True)  43.5 us
    all_gather x1, waiting for transfers between devices, on_device(): piece_rows = lax.all_gather(query_states, 'narrow', axis=0, tiled=True)  18 us
    dot_general x4, matrix products, absorb_block(): jnp.einsum('hqk,khd->qhd', weights, value_block, preferred_element_type=j...  14.4 us
    unnamed x20, local copies, waits for them, and re-layouts  4.9 us
    convert_element_type x4, other arithmetic, absorb_block(): live = live_rows.astype(jnp.float32)  2.65 us
    reshape x1, local copies, waits for them, and re-layouts, attend(): value_blocks = value_states.reshape(blocks, block_rows, HEADS, head_size)  2.37 us
  transfers between devices with their start and end apart: 2, of which 2 were waited for; matrix products, arithmetic and copies ran while one was open for 10% of the time, Pallas kernels for 0%

commit v1 on v0

v1 whole, which is shorter than its diff:
```python
import functools
import math

import jax
import jax.numpy as jnp
from jax import lax
from jax.experimental import pallas as pl
from jax.experimental.pallas import tpu as pltpu
from jax.sharding import PartitionSpec as P

LANES = 128


def silu(x):
    half = 0.5 * x
    return half + half * jnp.tanh(half)


def pick(index, table):
    value = jnp.int32(table[0])
    for i, entry in enumerate(table[1:], 1):
        value = jnp.where(index == i, jnp.int32(entry), value)
    return value


def dot(a, b, dims=((1,), (0,))):
    return lax.dot_general(a, b, (dims, ((), ())), preferred_element_type=jnp.float32)


def project_queries(own_ref, other_ref, w_ref, states_ref, gates_ref, *, scale):
    rows, width = own_ref.shape
    both = dot(own_ref[...], w_ref[...])
    states_ref[:rows] = (silu(both[:, :width]).astype(jnp.bfloat16) * scale).astype(jnp.bfloat16)
    gates_ref[...] = silu(both[:, width:])
    other = dot(other_ref[...], w_ref[:, :width])
    states_ref[rows:] = (silu(other).astype(jnp.bfloat16) * scale).astype(jnp.bfloat16)


def attend(
    length_ref, *refs, heads, owners, offset, shard_rows, first, chosen
):
    refs = list(refs)
    hist = refs.pop(0)[...]
    buckets = refs.pop(0)[...]
    place = lax.axis_index("narrow")
    if chosen is not None:
        take_own = pick(place, chosen) == 1
        hist = jnp.where(take_own, refs.pop(0)[...], hist)
        buckets = jnp.where(take_own, refs.pop(0)[...], buckets)
    w_ref, table_ref, states_ref = refs[:3]
    out_ref = refs[-1]
    total_ref = None if first else refs[3]

    rows, width = hist.shape
    head_size = width // heads
    per_block = LANES // head_size
    q_rows = states_ref.shape[0]
    q_block = min(256, q_rows)

    start = pick(place, owners) * shard_rows + offset
    live = (start + lax.broadcasted_iota(jnp.int32, (rows, 1), 0) < length_ref[0]).astype(jnp.float32)
    key_value = dot(hist, w_ref[...])
    keys = silu(key_value[:, :width]).astype(jnp.bfloat16)
    values = (key_value[:, width:] * live).astype(jnp.bfloat16)

    size = table_ref.shape[0]
    hot = lax.broadcasted_iota(jnp.int32, (size, rows), 0) == buckets
    table = jnp.concatenate(
        [table_ref[...] * 0.5, jnp.zeros((size, LANES - heads), jnp.bfloat16)], axis=1
    ).astype(jnp.bfloat16)
    bias = dot(hot.astype(jnp.bfloat16), table, ((0,), (0,))).astype(jnp.bfloat16)

    lane = lax.broadcasted_iota(jnp.int32, (1, LANES), 1)
    for block in range(width // LANES):
        cols = slice(block * LANES, (block + 1) * LANES)
        keys_bias = jnp.concatenate([keys[:, cols], bias], axis=1)
        parts = []
        for j in range(per_block):
            mask = ((lane // head_size) == j).astype(jnp.bfloat16)
            pointer = jnp.broadcast_to(
                (lane == block * per_block + j).astype(jnp.bfloat16), (q_block, LANES)
            )
            parts.append((mask, pointer, values[:, cols] * mask))
        for at in range(0, q_rows, q_block):
            queries = states_ref[at : at + q_block, cols]
            total = None
            for mask, pointer, value in parts:
                scores = dot(
                    jnp.concatenate([queries * mask, pointer], axis=1), keys_bias, ((1,), (1,))
                )
                weights = (scores + scores * jnp.tanh(scores)).astype(jnp.bfloat16)
                term = dot(weights, value)
                total = term if total is None else total + term
            if not first:
                total = total + total_ref[at : at + q_block, cols]
            out_ref[at : at + q_block, cols] = total.astype(out_ref.dtype)


def finish(total_ref, other_ref, gates_ref, gain_ref, w_ref, events_ref, out_ref):
    attended = total_ref[...] + other_ref[...].astype(jnp.float32)
    center = jnp.mean(attended, axis=-1, keepdims=True)
    away = attended - center
    spread = jnp.mean(away * away, axis=-1, keepdims=True)
    normed = away * lax.rsqrt(spread + 1e-05)
    mixed = (normed * gain_ref[...] * gates_ref[...]).astype(jnp.bfloat16)
    out_ref[...] = (events_ref[...].astype(jnp.float32) + dot(mixed, w_ref[...])).astype(jnp.bfloat16)


VMEM = pl.BlockSpec(memory_space=pltpu.VMEM)
SMEM = pl.BlockSpec(memory_space=pltpu.SMEM)
PARAMS = pltpu.CompilerParams(vmem_limit_bytes=40 * 1024 * 1024)


def routes(n):
    half = n // 2
    rank = [z if z < half else n - 1 - z for z in range(n)]

    def shard(z, step):
        own_half = (z < half) == (rank[z] % 2 == 0)
        at = (rank[z] + step) % half
        return at if own_half else n - 1 - at

    sources = []
    for step in range(half):
        row = []
        for z in range(n):
            source = shard(z, step)
            row.append(source if z < half else n - 1 - shard(n - 1 - z, step))
        sources.append(row)
    return rank, sources


def on_device(
    hist_events, query_events, hist_lengths, time_buckets, w_key, w_query, bias_table, out_gain, w_out, *, n
):
    history, queries_in, buckets = hist_events[0], query_events[0], time_buckets
    shard_rows, width = history.shape
    q_rows = queries_in.shape[0]
    heads = bias_table.shape[1]
    scale = 0.5 / math.sqrt(width // heads)
    rank, sources = routes(n)
    swap = [(z, z ^ 1) for z in range(n)]

    def send(x, step):
        pairs = [(source, z) for z, source in enumerate(sources[step]) if source != z]
        return lax.ppermute(x, "narrow", pairs)

    pieces = []
    for step in range(n // 2):
        parts = 2 if step == n // 2 - 1 else 1
        size = shard_rows // parts
        for part in range(parts):
            at = part * size
            pieces.append((step, at, size))
    received = [
        (send(history[at : at + size], step), send(buckets[:, at : at + size], step))
        for step, at, size in pieces
    ]
    other_queries = lax.ppermute(queries_in, "narrow", swap)

    states, gates = pl.pallas_call(
        functools.partial(project_queries, scale=scale),
        out_shape=(
            jax.ShapeDtypeStruct((2 * q_rows, width), jnp.bfloat16),
            jax.ShapeDtypeStruct((q_rows, width), jnp.float32),
        ),
        in_specs=[VMEM] * 3,
        out_specs=[VMEM] * 2,
        compiler_params=PARAMS,
        name="project_queries",
    )(queries_in, other_queries, w_query)

    def absorb(index, states, total, dtype, name):
        step, at, size = pieces[index]
        operands = [hist_lengths, *received[index]]
        chosen = None
        if step == 0:
            chosen = [int(sources[0][z] == z) for z in range(n)]
            operands += [history, buckets]
        operands += [w_key, bias_table, states]
        if total is not None:
            operands.append(total)
        body = functools.partial(
            attend,
            heads=heads,
            owners=sources[step],
            offset=at,
            shard_rows=shard_rows,
            first=total is None,
            chosen=chosen,
        )
        return pl.pallas_call(
            body,
            out_shape=jax.ShapeDtypeStruct((states.shape[0], width), dtype),
            in_specs=[SMEM] + [VMEM] * (len(operands) - 1),
            out_specs=VMEM,
            compiler_params=PARAMS,
            name=name,
        )(*operands)

    total = None
    for index in range(len(pieces) - 1):
        total = absorb(index, states, total, jnp.float32, f"attend_piece{index}")
    last = len(pieces) - 1
    theirs = absorb(last, states[q_rows:], total[q_rows:], jnp.bfloat16, "attend_theirs")
    theirs = lax.ppermute(theirs, "narrow", swap)
    own = absorb(last, states[:q_rows], total[:q_rows], jnp.float32, "attend_own")
    result = pl.pallas_call(
        finish,
        out_shape=jax.ShapeDtypeStruct((q_rows, width), jnp.bfloat16),
        in_specs=[VMEM] * 6,
        out_specs=VMEM,
        compiler_params=PARAMS,
        name="finish",
    )(own, theirs, gates, out_gain[None], w_out, queries_in)
    return result[None]


def solution(mesh):
    in_specs = (
        P(("parts", "wide"), "narrow", None),
        P(("parts", "wide"), "narrow", None),
        P(("parts", "wide")),
        P(("parts", "wide"), "narrow"),
        P(),
        P(),
        P(),
        P(),
        P(),
    )
    out_specs = P(("parts", "wide"), "narrow", None)
    return jax.shard_map(
        functools.partial(on_device, n=mesh.shape["narrow"]),
        mesh=mesh,
        in_specs=in_specs,
        out_specs=out_specs,
        check_vma=False,
    )
```

time: 118 us -> 47.9 us (0.41)
  the two profiles are of different devices: /device:TPU:1 before, /device:TPU:0 now
where the time goes in v1:
time: 47.9 us; the launch traced here: 47.7 us
  starting transfers between devices  27.1 us (57%)
  Pallas kernels  11 us (23%)
  waiting for transfers between devices  5.6 us (12%)
  local copies, waits for them, and re-layouts  3.11 us (6%)
  between operations  0.8 us (2%)
    ppermute x1, starting transfers between devices, on_device(): theirs = lax.ppermute(theirs, 'narrow', swap)  14.8 us
    pallas_call x4, Pallas kernels, absorb(): pl.pallas_call(body, out_shape=jax.ShapeDtypeStruct((states.shape[0], wid...  9.11 us
    ppermute x6, starting transfers between devices, send(): return lax.ppermute(x, 'narrow', pairs)  6.4 us
    ppermute x1, starting transfers between devices, on_device(): other_queries = lax.ppermute(queries_in, 'narrow', swap)  5.91 us
    ppermute x1, waiting for transfers between devices, on_device(): theirs = lax.ppermute(theirs, 'narrow', swap)  3.62 us
    ppermute x1, waiting for transfers between devices, on_device(): other_queries = lax.ppermute(queries_in, 'narrow', swap)  1.97 us
    unnamed x19, local copies, waits for them, and re-layouts  1.94 us
    pallas_call x1, Pallas kernels, on_device(): pl.pallas_call(finish, out_shape=jax.ShapeDtypeStruct((q_rows, width), jn...  1.23 us
  transfers between devices with their start and end apart: 8, of which 2 were waited for; matrix products, arithmetic and copies ran while one was open for 3% of the time, Pallas kernels for 17%

profile of v1, /device:TPU:0, one launch (start us, length us, event | category | flops | bytes accessed | tf_op | source)
XLA Modules:
  0.0 47.7 jit_solution(2602978221914998408)
XLA Ops:
  0.0 0.8 %collective-permute-start.6 = (s32[1,512]{1,0:T(1,128)}, s32[1,512]{1,0:T(1,128)S(1)}, u32[]{:S(2)}, u32[]{:S(2)}) collective-permute-start(s32[1,512]{1,0:T(1,128)} %refs_3_.4), channel_id=1, source_target_pairs={{2,1},{1,2},{6,5},{5,6},{10,9},{9,10},{14,13},{13,14},{18,17},{17,... | collective-permute-start | bytes 6152 | tf_op jit(solution)/shard_map/ppermute | solution.py:146
  0.8 5.9 %collective-permute-start.2 = (bf16[256,512]{1,0:T(8,128)(2,1)}, bf16[256,512]{1,0:T(8,128)(2,1)S(1)}, u32[]{:S(2)}, u32[]{:S(2)}) collective-permute-start(bf16[256,512]{1,0:T(8,128)(2,1)} %bitcast.10), channel_id=1, source_target_pairs={{0,1},{1,0},{2,3},{3,2},{4,5},{5,4},{6,7},{7,6},{8,9},{9,8},{10,11... | collective-permute-start | bytes 786440 | tf_op jit(solution)/shard_map/ppermute | solution.py:159
  6.7 0.7 %collective-permute-start.5 = (bf16[512,512]{1,0:T(8,128)(2,1)}, bf16[512,512]{1,0:T(8,128)(2,1)S(1)}, u32[]{:S(2)}, u32[]{:S(2)}) collective-permute-start(bf16[512,512]{1,0:T(8,128)(2,1)} %bitcast.8), channel_id=1, source_target_pairs={{2,1},{1,2},{6,5},{5,6},{10,9},{9,10},{14,13},{13,14},{18,17},{17,... | collective-permute-start | bytes 1572872 | tf_op jit(solution)/shard_map/ppermute | solution.py:146
  7.4 1.1 %slice_bitcast_fusion = (bf16[256,512]{1,0:T(8,128)(2,1)S(1)}, bf16[256,512]{1,0:T(8,128)(2,1)S(1)}) fusion(bf16[1,512,512]{2,1,0:T(8,128)(2,1)} %param.9), kind=kLoop, calls=%fused_computation | loop fusion | bytes 1048576 | tf_op jit(solution)/shard_map/slice | solution.py:156
  8.5 2.8 %collective-permute-start.3 = (bf16[256,512]{1,0:T(8,128)(2,1)S(1)}, bf16[256,512]{1,0:T(8,128)(2,1)S(1)}, u32[]{:S(2)}, u32[]{:S(2)}) collective-permute-start(bf16[256,512]{1,0:T(8,128)(2,1)S(1)} %get-tuple-element.13), channel_id=1, source_target_pairs={{1,0},{3,1},{0,2},{2,3},{5,4},{7,5},{4,6},{6,7},{9,8},{11,9},{8,10... | collective-permute-start | bytes 786440 | tf_op jit(solution)/shard_map/ppermute | solution.py:146
  11.2 0.1 collective-permute-start.4
  12.0 0.1 copy.12.refs_5_.refs_3_
  12.1 2.0 %collective-permute-done.2.other_ref = bf16[256,512]{1,0:T(8,128)(2,1)S(1)} collective-permute-done((bf16[256,512]{1,0:T(8,128)(2,1)}, bf16[256,512]{1,0:T(8,128)(2,1)S(1)}, u32[]{:S(2)}, u32[]{:S(2)}) %collective-permute-start.2) | collective-permute-done | bytes 262176 | tf_op jit(solution)/shard_map/ppermute | solution.py:159
  14.1 1.9 %collective-permute-start.1 = (s32[1,256]{1,0:T(1,128)S(1)}, s32[1,256]{1,0:T(1,128)S(1)}, u32[]{:S(2)}, u32[]{:S(2)}) collective-permute-start(s32[1,256]{1,0:T(1,128)S(1)} %get-tuple-element.16), channel_id=1, source_target_pairs={{1,0},{3,1},{0,2},{2,3},{5,4},{7,5},{4,6},{6,7},{9,8},{11,9},{8,10... | collective-permute-start | bytes 3080 | tf_op jit(solution)/shard_map/ppermute | solution.py:146
  16.0 0.9 %copy-done.3 = bf16[1,256,512]{2,1,0:T(8,128)(2,1)S(1)} copy-done((bf16[1,256,512]{2,1,0:T(8,128)(2,1)S(1)}, bf16[1,256,512]{2,1,0:T(8,128)(2,1)}, u32[]{:S(2)}) %copy-start.3) | copy-done | bytes 262168
  17.0 0.7 %project_queries.1 = (bf16[512,512]{1,0:T(8,128)(2,1)S(1)}, f32[256,512]{1,0:T(8,128)S(1)}) custom-call(bf16[256,512]{1,0:T(8,128)(2,1)S(1)} %bitcast.11, bf16[256,512]{1,0:T(8,128)(2,1)S(1)} %collective-permute-done.2.other_ref, bf16[512,1024]{1,0:T(8,128)(2,1)S(1)} %copy-done.2), custom_call_target="tpu_custom_call" | custom-call | tf_op jit(solution)/shard_map/project_queries/pallas_call | solution.py:161
  17.7 0.0 copy-start.1
  17.8 0.1 collective-permute-start
  17.9 0.8 %copy-done.1 = bf16[1,512,512]{2,1,0:T(8,128)(2,1)S(1)} copy-done((bf16[1,512,512]{2,1,0:T(8,128)(2,1)S(1)}, bf16[1,512,512]{2,1,0:T(8,128)(2,1)}, u32[]{:S(2)}) %copy-start.1) | copy-done | bytes 524312
  18.7 3.7 %attend_piece0.1.refs_5_ = f32[512,512]{1,0:T(8,128)S(1)} custom-call(s32[1]{0:T(128)S(6)} %copy.14.length_ref, bf16[512,512]{1,0:T(8,128)(2,1)S(1)} %collective-permute-done.5.refs_0_, s32[1,512]{1,0:T(1,128)S(1)} %collective-permute-done.6.refs_1_, bf16[512,512]{1,0:T(8,128)(2,1)S(1)} %bitcast.9, s32[1,512]{1,0:T(1,128)S(1)} %copy-done.6, ...), custom_call_target="tpu_custom_call" | custom-call | tf_op jit(solution)/shard_map/attend_piece0/pallas_call | solution.py:192
  22.5 0.0 collective-permute-done.3.refs_0_
  22.5 2.4 %attend_piece1.1 = f32[512,512]{1,0:T(8,128)S(1)} custom-call(s32[1]{0:T(128)S(6)} %copy.14.length_ref, bf16[256,512]{1,0:T(8,128)(2,1)S(1)} %collective-permute-done.3.refs_0_, s32[1,256]{1,0:T(1,128)S(1)} %collective-permute-done.4.refs_1_, bf16[512,1024]{1,0:T(8,128)(2,1)S(1)} %copy-done, bf16[128,8]{1,0:T(8,128)(2,1)S(1)} %copy.12.refs_5_.refs_3_, ...), custom_call_target="tpu_custom_call" | custom-call | tf_op jit(solution)/shard_map/attend_piece1/pallas_call | solution.py:192
  24.9 0.1 fusion
  25.0 1.5 %attend_theirs.1 = bf16[256,512]{1,0:T(8,128)(2,1)S(1)} custom-call(s32[1]{0:T(128)S(6)} %copy.14.length_ref, bf16[256,512]{1,0:T(8,128)(2,1)S(1)} %collective-permute-done.refs_0_, s32[1,256]{1,0:T(1,128)S(1)} %collective-permute-done.1.refs_1_, bf16[512,1024]{1,0:T(8,128)(2,1)S(1)} %copy-done, bf16[128,8]{1,0:T(8,128)(2,1)S(1)} %copy.12.refs_5_.refs_3_, ...), custom_call_target="tpu_custom_call" | custom-call | tf_op jit(solution)/shard_map/attend_theirs/pallas_call | solution.py:192
  26.5 14.8 %collective-permute-start.7 = (bf16[256,512]{1,0:T(8,128)(2,1)S(1)}, bf16[256,512]{1,0:T(8,128)(2,1)S(1)}, u32[]{:S(2)}, u32[]{:S(2)}) collective-permute-start(bf16[256,512]{1,0:T(8,128)(2,1)S(1)} %attend_theirs.1), channel_id=1, source_target_pairs={{0,1},{1,0},{2,3},{3,2},{4,5},{5,4},{6,7},{7,6},{8,9},{9,8},{10,11... | collective-permute-start | bytes 786440 | tf_op jit(solution)/shard_map/ppermute | solution.py:206
  41.3 1.5 %attend_own.1.total_ref = f32[256,512]{1,0:T(8,128)S(1)} custom-call(s32[1]{0:T(128)S(6)} %copy.14.length_ref, bf16[256,512]{1,0:T(8,128)(2,1)S(1)} %collective-permute-done.refs_0_, s32[1,256]{1,0:T(1,128)S(1)} %collective-permute-done.1.refs_1_, bf16[512,1024]{1,0:T(8,128)(2,1)S(1)} %copy-done, bf16[128,8]{1,0:T(8,128)(2,1)S(1)} %copy.12.refs_5_.refs_3_, ...), custom_call_target="tpu_custom_call" | custom-call | tf_op jit(solution)/shard_map/attend_own/pallas_call | solution.py:192
  42.8 0.0 copy-start.7
  42.8 3.6 %collective-permute-done.7.other_ref = bf16[256,512]{1,0:T(8,128)(2,1)S(1)} collective-permute-done((bf16[256,512]{1,0:T(8,128)(2,1)S(1)}, bf16[256,512]{1,0:T(8,128)(2,1)S(1)}, u32[]{:S(2)}, u32[]{:S(2)}) %collective-permute-start.7) | collective-permute-done | bytes 262176 | tf_op jit(solution)/shard_map/ppermute | solution.py:206
  46.4 1.2 %finish.1 = bf16[256,512]{1,0:T(8,128)(2,1)} custom-call(f32[256,512]{1,0:T(8,128)S(1)} %attend_own.1.total_ref, bf16[256,512]{1,0:T(8,128)(2,1)S(1)} %collective-permute-done.7.other_ref, f32[256,512]{1,0:T(8,128)S(1)} %get-tuple-element.8.gates_ref, f32[1,512]{1,0:T(1,128)S(1)} %bitcast.13, bf16[512,512]{1,0:T(8,128)(2,1)S(1)} %copy-done.5, ...), custom_call_target="tpu_custom_call" | custom-call | tf_op jit(solution)/shard_map/finish/pallas_call | solution.py:208
  (21 shorter events, 0.1 us)
Async XLA Ops:
  0.0 16.0 %copy-start.2 = (bf16[512,1024]{1,0:T(8,128)(2,1)S(1)}, bf16[512,1024]{1,0:T(8,128)(2,1)}, u32[]{:S(2)}) copy-start(bf16[512,1024]{1,0:T(8,128)(2,1)} %w_ref.2) | copy-start | bytes 3145732
  0.0 17.8 %collective-permute-start.6 = (s32[1,512]{1,0:T(1,128)}, s32[1,512]{1,0:T(1,128)S(1)}, u32[]{:S(2)}, u32[]{:S(2)}) collective-permute-start(s32[1,512]{1,0:T(1,128)} %refs_3_.4), channel_id=1, source_target_pairs={{2,1},{1,2},{6,5},{5,6},{10,9},{9,10},{14,13},{13,14},{18,17},{17,... | collective-permute-start | bytes 6152 | tf_op jit(solution)/shard_map/ppermute | solution.py:146
  0.8 13.3 %collective-permute-start.2 = (bf16[256,512]{1,0:T(8,128)(2,1)}, bf16[256,512]{1,0:T(8,128)(2,1)S(1)}, u32[]{:S(2)}, u32[]{:S(2)}) collective-permute-start(bf16[256,512]{1,0:T(8,128)(2,1)} %bitcast.10), channel_id=1, source_target_pairs={{0,1},{1,0},{2,3},{3,2},{4,5},{5,4},{6,7},{7,6},{8,9},{9,8},{10,11... | collective-permute-start | bytes 786440 | tf_op jit(solution)/shard_map/ppermute | solution.py:159
  6.7 11.2 %collective-permute-start.5 = (bf16[512,512]{1,0:T(8,128)(2,1)}, bf16[512,512]{1,0:T(8,128)(2,1)S(1)}, u32[]{:S(2)}, u32[]{:S(2)}) collective-permute-start(bf16[512,512]{1,0:T(8,128)(2,1)} %bitcast.8), channel_id=1, source_target_pairs={{2,1},{1,2},{6,5},{5,6},{10,9},{9,10},{14,13},{13,14},{18,17},{17,... | collective-permute-start | bytes 1572872 | tf_op jit(solution)/shard_map/ppermute | solution.py:146
  7.4 3.8 %copy-start.6 = (s32[1,512]{1,0:T(1,128)S(1)}, s32[1,512]{1,0:T(1,128)}, u32[]{:S(2)}) copy-start(s32[1,512]{1,0:T(1,128)} %refs_3_.4) | copy-start | bytes 6148
  8.5 14.0 %collective-permute-start.3 = (bf16[256,512]{1,0:T(8,128)(2,1)S(1)}, bf16[256,512]{1,0:T(8,128)(2,1)S(1)}, u32[]{:S(2)}, u32[]{:S(2)}) collective-permute-start(bf16[256,512]{1,0:T(8,128)(2,1)S(1)} %get-tuple-element.13), channel_id=1, source_target_pairs={{1,0},{3,1},{0,2},{2,3},{5,4},{7,5},{4,6},{6,7},{9,8},{11,9},{8,10... | collective-permute-start | bytes 786440 | tf_op jit(solution)/shard_map/ppermute | solution.py:146
  11.2 0.7 %copy-start.8 = (bf16[128,8]{0,1:T(8,128)(2,1)S(1)}, bf16[128,8]{0,1:T(8,128)(2,1)}, u32[]{:S(2)}) copy-start(bf16[128,8]{0,1:T(8,128)(2,1)} %param.15) | copy-start | bytes 6148
  11.2 11.2 %collective-permute-start.4 = (s32[1,256]{1,0:T(1,128)S(1)}, s32[1,256]{1,0:T(1,128)S(1)}, u32[]{:S(2)}, u32[]{:S(2)}) collective-permute-start(s32[1,256]{1,0:T(1,128)S(1)} %get-tuple-element.15), channel_id=1, source_target_pairs={{1,0},{3,1},{0,2},{2,3},{5,4},{7,5},{4,6},{6,7},{9,8},{11,9},{8,10... | collective-permute-start | bytes 3080 | tf_op jit(solution)/shard_map/ppermute | solution.py:146
  14.1 3.8 %copy-start = (bf16[512,1024]{1,0:T(8,128)(2,1)S(1)}, bf16[512,1024]{1,0:T(8,128)(2,1)}, u32[]{:S(2)}) copy-start(bf16[512,1024]{1,0:T(8,128)(2,1)} %refs_2_.5) | copy-start | bytes 3145732
  14.1 10.9 %collective-permute-start.1 = (s32[1,256]{1,0:T(1,128)S(1)}, s32[1,256]{1,0:T(1,128)S(1)}, u32[]{:S(2)}, u32[]{:S(2)}) collective-permute-start(s32[1,256]{1,0:T(1,128)S(1)} %get-tuple-element.16), channel_id=1, source_target_pairs={{1,0},{3,1},{0,2},{2,3},{5,4},{7,5},{4,6},{6,7},{9,8},{11,9},{8,10... | collective-permute-start | bytes 3080 | tf_op jit(solution)/shard_map/ppermute | solution.py:146
  16.0 1.0 %copy-start.3 = (bf16[1,256,512]{2,1,0:T(8,128)(2,1)S(1)}, bf16[1,256,512]{2,1,0:T(8,128)(2,1)}, u32[]{:S(2)}) copy-start(bf16[1,256,512]{2,1,0:T(8,128)(2,1)} %param.10) | copy-start | bytes 786436
  17.7 1.0 %copy-start.1 = (bf16[1,512,512]{2,1,0:T(8,128)(2,1)S(1)}, bf16[1,512,512]{2,1,0:T(8,128)(2,1)}, u32[]{:S(2)}) copy-start(bf16[1,512,512]{2,1,0:T(8,128)(2,1)} %param.9) | copy-start | bytes 1572868
  17.8 7.2 %collective-permute-start = (bf16[256,512]{1,0:T(8,128)(2,1)S(1)}, bf16[256,512]{1,0:T(8,128)(2,1)S(1)}, u32[]{:S(2)}, u32[]{:S(2)}) collective-permute-start(bf16[256,512]{1,0:T(8,128)(2,1)S(1)} %get-tuple-element.14), channel_id=1, source_target_pairs={{1,0},{3,1},{0,2},{2,3},{5,4},{7,5},{4,6},{6,7},{9,8},{11,9},{8,10... | collective-permute-start | bytes 786440 | tf_op jit(solution)/shard_map/ppermute | solution.py:146
  26.5 19.9 %collective-permute-start.7 = (bf16[256,512]{1,0:T(8,128)(2,1)S(1)}, bf16[256,512]{1,0:T(8,128)(2,1)S(1)}, u32[]{:S(2)}, u32[]{:S(2)}) collective-permute-start(bf16[256,512]{1,0:T(8,128)(2,1)S(1)} %attend_theirs.1), channel_id=1, source_target_pairs={{0,1},{1,0},{2,3},{3,2},{4,5},{5,4},{6,7},{7,6},{8,9},{9,8},{10,11... | collective-permute-start | bytes 786440 | tf_op jit(solution)/shard_map/ppermute | solution.py:206
  41.3 5.1 %copy-start.4 = (bf16[1,256,512]{2,1,0:T(8,128)(2,1)S(1)}, bf16[1,256,512]{2,1,0:T(8,128)(2,1)}, u32[]{:S(2)}) copy-start(bf16[1,256,512]{2,1,0:T(8,128)(2,1)} %param.10) | copy-start | bytes 786436
  41.3 5.1 %copy-start.5 = (bf16[512,512]{1,0:T(8,128)(2,1)S(1)}, bf16[512,512]{1,0:T(8,128)(2,1)}, u32[]{:S(2)}) copy-start(bf16[512,512]{1,0:T(8,128)(2,1)} %w_ref.3) | copy-start | bytes 1572868
  42.8 3.6 %copy-start.7 = (f32[512]{0:T(512)S(1)}, f32[512]{0:T(512)}, u32[]{:S(2)}) copy-start(f32[512]{0:T(512)} %param.16) | copy-start | bytes 6148

commit v2 on v1

--- a/solution.py
+++ b/solution.py
@@ -37,34 +37,39 @@
 
 
 def attend(
-    length_ref, *refs, heads, owners, offset, shard_rows, first, chosen
+    length_ref, *refs, heads, owners, at, rows, q_at, q_rows, shard_rows, first, chosen
 ):
     refs = list(refs)
-    hist = refs.pop(0)[...]
-    buckets = refs.pop(0)[...]
+    hist_ref = refs.pop(0)
+    hist = hist_ref[:rows]
+    width = hist.shape[1]
     place = lax.axis_index("narrow")
     if chosen is not None:
+        labels_ref, own_ref, own_labels_ref = refs.pop(0), refs.pop(0), refs.pop(0)
+        from_row, from_col = labels_ref.shape[0] - 16 + at // width, at % width
+        labels = labels_ref[:, from_col : from_col + rows].astype(jnp.float32)
+        labels = labels[from_row : from_row + 1].astype(jnp.int32)
         take_own = pick(place, chosen) == 1
-        hist = jnp.where(take_own, refs.pop(0)[...], hist)
-        buckets = jnp.where(take_own, refs.pop(0)[...], buckets)
+        hist = jnp.where(take_own, own_ref[at : at + rows], hist)
+        labels = jnp.where(take_own, own_labels_ref[:, at : at + rows], labels)
+    else:
+        labels = refs.pop(0)[...]
     w_ref, table_ref, states_ref = refs[:3]
     out_ref = refs[-1]
     total_ref = None if first else refs[3]
 
-    rows, width = hist.shape
     head_size = width // heads
     per_block = LANES // head_size
-    q_rows = states_ref.shape[0]
     q_block = min(256, q_rows)
 
-    start = pick(place, owners) * shard_rows + offset
+    start = pick(place, owners) * shard_rows + at
     live = (start + lax.broadcasted_iota(jnp.int32, (rows, 1), 0) < length_ref[0]).astype(jnp.float32)
     key_value = dot(hist, w_ref[...])
     keys = silu(key_value[:, :width]).astype(jnp.bfloat16)
     values = (key_value[:, width:] * live).astype(jnp.bfloat16)
 
     size = table_ref.shape[0]
-    hot = lax.broadcasted_iota(jnp.int32, (size, rows), 0) == buckets
+    hot = lax.broadcasted_iota(jnp.int32, (size, rows), 0) == labels
     table = jnp.concatenate(
         [table_ref[...] * 0.5, jnp.zeros((size, LANES - heads), jnp.bfloat16)], axis=1
     ).astype(jnp.bfloat16)
@@ -81,8 +86,8 @@
                 (lane == block * per_block + j).astype(jnp.bfloat16), (q_block, LANES)
             )
             parts.append((mask, pointer, values[:, cols] * mask))
-        for at in range(0, q_rows, q_block):
-            queries = states_ref[at : at + q_block, cols]
+        for q in range(0, q_rows, q_block):
+            queries = states_ref[q_at + q : q_at + q + q_block, cols]
             total = None
             for mask, pointer, value in parts:
                 scores = dot(
@@ -92,8 +97,8 @@
                 term = dot(weights, value)
                 total = term if total is None else total + term
             if not first:
-                total = total + total_ref[at : at + q_block, cols]
-            out_ref[at : at + q_block, cols] = total.astype(out_ref.dtype)
+                total = total + total_ref[q_at + q : q_at + q + q_block, cols]
+            out_ref[q : q + q_block, cols] = total.astype(out_ref.dtype)
 
 
 def finish(total_ref, other_ref, gates_ref, gain_ref, w_ref, events_ref, out_ref):
@@ -108,7 +113,7 @@
 
 VMEM = pl.BlockSpec(memory_space=pltpu.VMEM)
 SMEM = pl.BlockSpec(memory_space=pltpu.SMEM)
-PARAMS = pltpu.CompilerParams(vmem_limit_bytes=40 * 1024 * 1024)
+PARAMS = pltpu.CompilerParams(vmem_limit_bytes=16 * 1024 * 1024)
 
 
 def routes(n):
@@ -128,6 +133,14 @@
             row.append(source if z < half else n - 1 - shard(n - 1 - z, step))
         sources.append(row)
     return rank, sources
+
+
+def cost(flops, *arrays):
+    return pl.CostEstimate(
+        flops=flops,
+        bytes_accessed=sum(a.size * a.dtype.itemsize for a in arrays),
+        transcendentals=0,
+    )
 
 
 def on_device(
@@ -145,18 +158,20 @@
         pairs = [(source, z) for z, source in enumerate(sources[step]) if source != z]
         return lax.ppermute(x, "narrow", pairs)
 
-    pieces = []
-    for step in range(n // 2):
-        parts = 2 if step == n // 2 - 1 else 1
-        size = shard_rows // parts
-        for part in range(parts):
-            at = part * size
-            pieces.append((step, at, size))
-    received = [
-        (send(history[at : at + size], step), send(buckets[:, at : at + size], step))
-        for step, at, size in pieces
-    ]
-    other_queries = lax.ppermute(queries_in, "narrow", swap)
+    half = shard_rows // 2
+    pieces = [(step, 0, shard_rows) for step in range(1, n // 2)] + [(0, 0, half), (0, half, half)]
+    received = {step: [send(history, step)] for step in range(1, n // 2)}
+    tail = 16 * width
+    bucket_rows = jnp.pad(buckets[0].astype(jnp.bfloat16), (0, tail - shard_rows)).reshape(16, width)
+    head = jnp.concatenate([history[:half], bucket_rows])
+    rest = history[half:]
+    queries_out, labels, head, rest = lax.optimization_barrier((queries_in, buckets, head, rest))
+    other_queries = lax.ppermute(queries_out, "narrow", swap)
+    for step in range(1, n // 2):
+        received[step].append(send(labels, step))
+    head = send(head, 0)
+    rest, received[1][0] = lax.optimization_barrier((rest, received[1][0]))
+    rest = send(rest, 0)
 
     states, gates = pl.pallas_call(
         functools.partial(project_queries, scale=scale),
@@ -167,16 +182,19 @@
         in_specs=[VMEM] * 3,
         out_specs=[VMEM] * 2,
         compiler_params=PARAMS,
+        cost_estimate=cost(6 * q_rows * width * width, queries_in, w_query),
         name="project_queries",
     )(queries_in, other_queries, w_query)
 
-    def absorb(index, states, total, dtype, name):
+    def absorb(index, total, dtype, q_at, q_count, name):
         step, at, size = pieces[index]
-        operands = [hist_lengths, *received[index]]
+        operands = [hist_lengths]
         chosen = None
         if step == 0:
             chosen = [int(sources[0][z] == z) for z in range(n)]
-            operands += [history, buckets]
+            operands += [rest if at else head, head, history, buckets]
+        else:
+            operands += received[step]
         operands += [w_key, bias_table, states]
         if total is not None:
             operands.append(total)
@@ -184,33 +202,38 @@
             attend,
             heads=heads,
             owners=sources[step],
-            offset=at,
+            at=at,
+            rows=size,
+            q_at=q_at,
+            q_rows=q_count,
             shard_rows=shard_rows,
             first=total is None,
             chosen=chosen,
         )
         return pl.pallas_call(
             body,
-            out_shape=jax.ShapeDtypeStruct((states.shape[0], width), dtype),
+            out_shape=jax.ShapeDtypeStruct((q_count, width), dtype),
             in_specs=[SMEM] + [VMEM] * (len(operands) - 1),
             out_specs=VMEM,
             compiler_params=PARAMS,
+            cost_estimate=cost(64 * q_count * size * width, *operands),
             name=name,
         )(*operands)
 
     total = None
     for index in range(len(pieces) - 1):
-        total = absorb(index, states, total, jnp.float32, f"attend_piece{index}")
+        total = absorb(index, total, jnp.float32, 0, 2 * q_rows, f"attend_piece{index}")
     last = len(pieces) - 1
-    theirs = absorb(last, states[q_rows:], total[q_rows:], jnp.bfloat16, "attend_theirs")
+    theirs = absorb(last, total, jnp.bfloat16, q_rows, q_rows, "attend_theirs")
     theirs = lax.ppermute(theirs, "narrow", swap)
-    own = absorb(last, states[:q_rows], total[:q_rows], jnp.float32, "attend_own")
+    own = absorb(last, total, jnp.float32, 0, q_rows, "attend_own")
     result = pl.pallas_call(
         finish,
         out_shape=jax.ShapeDtypeStruct((q_rows, width), jnp.bfloat16),
         in_specs=[VMEM] * 6,
         out_specs=VMEM,
         compiler_params=PARAMS,
+        cost_estimate=cost(2 * q_rows * width * width, own, w_out),
         name="finish",
     )(own, theirs, gates, out_gain[None], w_out, queries_in)
     return result[None]

time: 47.9 us -> 41 us (0.86)
  starting transfers between devices: 27.1 us -> 11.7 us
  waiting for transfers between devices: 5.6 us -> 13.3 us
  other arithmetic: 0 us -> 1.42 us
    ppermute x1, starting transfers between devices: 14.8 us -> 4.72 us  [on_device(): theirs = lax.ppermute(theirs, 'narrow', swap)]
    ppermute x1, waiting for transfers between devices: 1.97 us -> 10.1 us  [on_device(): other_queries = lax.ppermute(queries_out, 'narrow', swap)]
    ppermute x1, starting transfers between devices: 5.91 us -> 0.01 us  [on_device(): other_queries = lax.ppermute(queries_out, 'narrow', swap)]
    unnamed x19, local copies, waits for them, and re-layouts: 1.94 us -> 0.84 us
    concatenate x0 -> x1, other arithmetic: none -> 0.72 us  [on_device(): head = jnp.concatenate([history[:half], bucket_rows])]
    convert_element_type x0 -> x1, other arithmetic: none -> 0.7 us  [on_device(): buckets[0].astype(jnp.bfloat16)]
    slice x4 -> x1, local copies, waits for them, and re-layouts: 1.18 us -> 1.76 us  [on_device(): rest = history[half:]]
    ppermute x6 -> x4, starting transfers between devices: 6.4 us -> 6.96 us  [send(): return lax.ppermute(x, 'narrow', pairs)]
  transfers between devices with their start and end apart: 8 -> 6, of which waited for: 2 -> 2; matrix products, arithmetic and copies ran while one was open for 3% -> 8% of each run, Pallas kernels for 17% -> 20%
where the time goes in v2:
time: 41 us; the launch traced here: 40.8 us
  waiting for transfers between devices  13.3 us (32%)
  starting transfers between devices  11.7 us (29%)
  Pallas kernels  11 us (27%)
  local copies, waits for them, and re-layouts  2.64 us (6%)
  other arithmetic  1.42 us (3%)
  between operations  0.81 us (2%)
    ppermute x1, waiting for transfers between devices, on_device(): other_queries = lax.ppermute(queries_out, 'narrow', swap)  10.1 us
    pallas_call x4, Pallas kernels, absorb(): pl.pallas_call(body, out_shape=jax.ShapeDtypeStruct((q_count, width), dty...  9.1 us
    ppermute x4, starting transfers between devices, send(): return lax.ppermute(x, 'narrow', pairs)  6.96 us
    ppermute x1, starting transfers between devices, on_device(): theirs = lax.ppermute(theirs, 'narrow', swap)  4.72 us
    ppermute x1, waiting for transfers between devices, on_device(): theirs = lax.ppermute(theirs, 'narrow', swap)  3.16 us
    slice x1, local copies, waits for them, and re-layouts, on_device(): rest = history[half:]  1.76 us
    pallas_call x1, Pallas kernels, on_device(): pl.pallas_call(finish, out_shape=jax.ShapeDtypeStruct((q_rows, width), jn...  1.22 us
    unnamed x19, local copies, waits for them, and re-layouts  0.84 us
  transfers between devices with their start and end apart: 6, of which 2 were waited for; matrix products, arithmetic and copies ran while one was open for 8% of the time, Pallas kernels for 20%

profile of v2, /device:TPU:0, one launch (start us, length us, event | category | flops | bytes accessed | tf_op | source)
XLA Modules:
  0.0 40.8 jit_solution(11417082404221358133)
XLA Ops:
  0.0 4.0 %collective-permute-start = (bf16[512,512]{1,0:T(8,128)(2,1)}, bf16[512,512]{1,0:T(8,128)(2,1)S(1)}, u32[]{:S(2)}, u32[]{:S(2)}) collective-permute-start(bf16[512,512]{1,0:T(8,128)(2,1)} %bitcast.11), channel_id=1, source_target_pairs={{1,0},{3,1},{0,2},{2,3},{5,4},{7,5},{4,6},{6,7},{9,8},{11,9},{8,10... | collective-permute-start | bytes 1572872 | tf_op jit(solution)/shard_map/ppermute | solution.py:159
  4.0 1.8 %slice_bitcast_fusion = (bf16[256,512]{1,0:T(8,128)(2,1)}, bf16[256,512]{1,0:T(8,128)(2,1)S(1)}) fusion(bf16[1,512,512]{2,1,0:T(8,128)(2,1)} %param.9), kind=kLoop, calls=%fused_computation.1 | loop fusion | bytes 1048576 | tf_op jit(solution)/shard_map/slice | solution.py:167
  5.8 0.7 %convert_reduce_fusion = bf16[512]{0:T(512)(128)(2,1)S(1)} fusion(s32[1,512]{1,0:T(1,128)} %refs_3_.6), kind=kLoop, calls=%fused_computation.3 | loop fusion | flops 512 | bytes 3072 | tf_op jit(solution)/shard_map/convert_element_type | solution.py:165
  6.5 0.0 copy-start.1
  6.6 0.0 copy-start.8
  6.6 0.7 %pad_maximum_fusion = bf16[272,512]{1,0:T(8,128)(2,1)} fusion(bf16[16,512]{1,0:T(8,128)(2,1)S(1)} %reshape.6, bf16[256,512]{1,0:T(8,128)(2,1)S(1)} %get-tuple-element.22), kind=kLoop, calls=%fused_computation | loop fusion | flops 557056 | bytes 557056 | tf_op jit(solution)/shard_map/concatenate | solution.py:166
  7.3 0.2 copy-done.1
  7.5 0.4 %copy-done.4 = s32[1,512]{1,0:T(1,128)S(1)} copy-done((s32[1,512]{1,0:T(1,128)S(1)}, s32[1,512]{1,0:T(1,128)}, u32[]{:S(2)}) %copy-start.4) | copy-done | bytes 2072
  8.0 1.6 %collective-permute-start.4 = (s32[1,512]{1,0:T(1,128)S(1)}, s32[1,512]{1,0:T(1,128)S(1)}, u32[]{:S(2)}, u32[]{:S(2)}) collective-permute-start(s32[1,512]{1,0:T(1,128)S(1)} %copy-done.4), channel_id=1, source_target_pairs={{1,0},{3,1},{0,2},{2,3},{5,4},{7,5},{4,6},{6,7},{9,8},{11,9},{8,10... | collective-permute-start | bytes 6152 | tf_op jit(solution)/shard_map/ppermute | solution.py:159
  9.6 0.7 %collective-permute-start.2 = (bf16[272,512]{1,0:T(8,128)(2,1)}, bf16[272,512]{1,0:T(8,128)(2,1)S(1)}, u32[]{:S(2)}, u32[]{:S(2)}) collective-permute-start(bf16[272,512]{1,0:T(8,128)(2,1)} %pad_maximum_fusion), channel_id=1, source_target_pairs={{2,1},{1,2},{6,5},{5,6},{10,9},{9,10},{14,13},{13,14},{18,17},{17,... | collective-permute-start | bytes 835592 | tf_op jit(solution)/shard_map/ppermute | solution.py:159
  10.9 0.1 copy.12.refs_3_.refs_5_
  11.0 10.1 %collective-permute-done.3.other_ref = bf16[256,512]{1,0:T(8,128)(2,1)S(1)} collective-permute-done((bf16[256,512]{1,0:T(8,128)(2,1)S(1)}, bf16[256,512]{1,0:T(8,128)(2,1)S(1)}, u32[]{:S(2)}, u32[]{:S(2)}) %collective-permute-start.3) | collective-permute-done | bytes 262176 | tf_op jit(solution)/shard_map/ppermute | solution.py:169
  21.1 0.7 %project_queries.1 = (bf16[512,512]{1,0:T(8,128)(2,1)S(1)}, f32[256,512]{1,0:T(8,128)S(1)}) custom-call(bf16[256,512]{1,0:T(8,128)(2,1)S(1)} %bitcast.9, bf16[256,512]{1,0:T(8,128)(2,1)S(1)} %collective-permute-done.3.other_ref, bf16[512,1024]{1,0:T(8,128)(2,1)S(1)} %copy-done), custom_call_target="tpu_custom_call" | custom-call | flops 402653184 | bytes 1310720 | tf_op jit(solution)/shard_map/project_queries/pallas_call | solution.py:176
  21.8 0.7 %collective-permute-start.1 = (bf16[256,512]{1,0:T(8,128)(2,1)S(1)}, bf16[256,512]{1,0:T(8,128)(2,1)S(1)}, u32[]{:S(2)}, u32[]{:S(2)}) collective-permute-start(bf16[256,512]{1,0:T(8,128)(2,1)S(1)} %copy-done.7), channel_id=1, source_target_pairs={{2,1},{1,2},{6,5},{5,6},{10,9},{9,10},{14,13},{13,14},{18,17},{17,... | collective-permute-start | bytes 786440 | tf_op jit(solution)/shard_map/ppermute | solution.py:159
  22.5 0.0 copy-start.2
  22.6 3.7 %attend_piece0.1.refs_7_ = f32[512,512]{1,0:T(8,128)S(1)} custom-call(s32[1]{0:T(128)S(6)} %copy.14.length_ref, bf16[512,512]{1,0:T(8,128)(2,1)S(1)} %collective-permute-done.refs_0_, s32[1,512]{1,0:T(1,128)S(1)} %collective-permute-done.4.refs_1_, bf16[512,1024]{1,0:T(8,128)(2,1)S(1)} %copy-done.6, bf16[128,8]{1,0:T(8,128)(2,1)S(1)} %copy.12.refs_3_.refs_5_, ...), custom_call_target="tpu_custom_call" | custom-call | flops 8589934592 | bytes 2101252 | tf_op jit(solution)/shard_map/attend_piece0/pallas_call | solution.py:213
  26.3 2.4 %attend_piece1.1.refs_7_ = f32[512,512]{1,0:T(8,128)S(1)} custom-call(s32[1]{0:T(128)S(6)} %copy.14.length_ref, bf16[272,512]{1,0:T(8,128)(2,1)S(1)} %collective-permute-done.2.refs_0_.refs_1_, bf16[272,512]{1,0:T(8,128)(2,1)S(1)} %collective-permute-done.2.refs_0_.refs_1_, bf16[512,512]{1,0:T(8,128)(2,1)S(1)} %bitcast.12, s32[1,512]{1,0:T(1,128)S(1)} %copy-done.4, ...), custom_call_target="tpu_custom_call" | custom-call | flops 4294967296 | bytes 3706884 | tf_op jit(solution)/shard_map/attend_piece1/pallas_call | solution.py:213
  28.7 1.5 %attend_theirs.1 = bf16[256,512]{1,0:T(8,128)(2,1)S(1)} custom-call(s32[1]{0:T(128)S(6)} %copy.14.length_ref, bf16[256,512]{1,0:T(8,128)(2,1)S(1)} %collective-permute-done.1.refs_0_, bf16[272,512]{1,0:T(8,128)(2,1)S(1)} %collective-permute-done.2.refs_0_.refs_1_, bf16[512,512]{1,0:T(8,128)(2,1)S(1)} %bitcast.13, s32[1,512]{1,0:T(1,128)S(1)} %copy-done.4, ...), custom_call_target="tpu_custom_call" | custom-call | flops 2147483648 | bytes 3690500 | tf_op jit(solution)/shard_map/attend_theirs/pallas_call | solution.py:213
  30.2 0.0 copy-start.3
  30.2 4.7 %collective-permute-start.5 = (bf16[256,512]{1,0:T(8,128)(2,1)S(1)}, bf16[256,512]{1,0:T(8,128)(2,1)S(1)}, u32[]{:S(2)}, u32[]{:S(2)}) collective-permute-start(bf16[256,512]{1,0:T(8,128)(2,1)S(1)} %attend_theirs.1), channel_id=1, source_target_pairs={{0,1},{1,0},{2,3},{3,2},{4,5},{5,4},{6,7},{7,6},{8,9},{9,8},{10,11... | collective-permute-start | bytes 786440 | tf_op jit(solution)/shard_map/ppermute | solution.py:228
  35.0 1.5 %attend_own.1.total_ref = f32[256,512]{1,0:T(8,128)S(1)} custom-call(s32[1]{0:T(128)S(6)} %copy.14.length_ref, bf16[256,512]{1,0:T(8,128)(2,1)S(1)} %collective-permute-done.1.refs_0_, bf16[272,512]{1,0:T(8,128)(2,1)S(1)} %collective-permute-done.2.refs_0_.refs_1_, bf16[512,512]{1,0:T(8,128)(2,1)S(1)} %bitcast.14, s32[1,512]{1,0:T(1,128)S(1)} %copy-done.4, ...), custom_call_target="tpu_custom_call" | custom-call | flops 2147483648 | bytes 3690500 | tf_op jit(solution)/shard_map/attend_own/pallas_call | solution.py:213
  36.4 0.0 copy-start.5
  36.5 3.2 %collective-permute-done.5.other_ref = bf16[256,512]{1,0:T(8,128)(2,1)S(1)} collective-permute-done((bf16[256,512]{1,0:T(8,128)(2,1)S(1)}, bf16[256,512]{1,0:T(8,128)(2,1)S(1)}, u32[]{:S(2)}, u32[]{:S(2)}) %collective-permute-start.5) | collective-permute-done | bytes 262176 | tf_op jit(solution)/shard_map/ppermute | solution.py:228
  39.6 1.2 %finish.1 = bf16[256,512]{1,0:T(8,128)(2,1)} custom-call(f32[256,512]{1,0:T(8,128)S(1)} %attend_own.1.total_ref, bf16[256,512]{1,0:T(8,128)(2,1)S(1)} %collective-permute-done.5.other_ref, f32[256,512]{1,0:T(8,128)S(1)} %get-tuple-element.20.gates_ref, f32[1,512]{1,0:T(1,128)S(1)} %bitcast.15, bf16[512,512]{1,0:T(8,128)(2,1)S(1)} %copy-done.3, ...), custom_call_target="tpu_custom_call" | custom-call | flops 134217728 | bytes 1048576 | tf_op jit(solution)/shard_map/finish/pallas_call | solution.py:230
  (18 shorter events, 0.1 us)
Async XLA Ops:
  0.0 21.1 %copy-start = (bf16[512,1024]{1,0:T(8,128)(2,1)S(1)}, bf16[512,1024]{1,0:T(8,128)(2,1)}, u32[]{:S(2)}) copy-start(bf16[512,1024]{1,0:T(8,128)(2,1)} %w_ref.2) | copy-start | bytes 3145732
  0.0 21.8 %collective-permute-start = (bf16[512,512]{1,0:T(8,128)(2,1)}, bf16[512,512]{1,0:T(8,128)(2,1)S(1)}, u32[]{:S(2)}, u32[]{:S(2)}) collective-permute-start(bf16[512,512]{1,0:T(8,128)(2,1)} %bitcast.11), channel_id=1, source_target_pairs={{1,0},{3,1},{0,2},{2,3},{5,4},{7,5},{4,6},{6,7},{9,8},{11,9},{8,10... | collective-permute-start | bytes 1572872 | tf_op jit(solution)/shard_map/ppermute | solution.py:159
  6.5 1.0 %copy-start.1 = (bf16[1,256,512]{2,1,0:T(8,128)(2,1)S(1)}, bf16[1,256,512]{2,1,0:T(8,128)(2,1)}, u32[]{:S(2)}) copy-start(bf16[1,256,512]{2,1,0:T(8,128)(2,1)} %param.10) | copy-start | bytes 786436
  6.6 4.3 %copy-start.8 = (bf16[128,8]{0,1:T(8,128)(2,1)S(1)}, bf16[128,8]{0,1:T(8,128)(2,1)}, u32[]{:S(2)}) copy-start(bf16[128,8]{0,1:T(8,128)(2,1)} %param.15) | copy-start | bytes 6148
  7.3 0.7 %copy-start.4 = (s32[1,512]{1,0:T(1,128)S(1)}, s32[1,512]{1,0:T(1,128)}, u32[]{:S(2)}) copy-start(s32[1,512]{1,0:T(1,128)} %refs_3_.6) | copy-start | bytes 6148
  7.3 15.2 %copy-start.6 = (bf16[512,1024]{1,0:T(8,128)(2,1)S(1)}, bf16[512,1024]{1,0:T(8,128)(2,1)}, u32[]{:S(2)}) copy-start(bf16[512,1024]{1,0:T(8,128)(2,1)} %refs_4_.5) | copy-start | bytes 3145732
  7.5 13.6 %collective-permute-start.3 = (bf16[256,512]{1,0:T(8,128)(2,1)S(1)}, bf16[256,512]{1,0:T(8,128)(2,1)S(1)}, u32[]{:S(2)}, u32[]{:S(2)}) collective-permute-start(bf16[256,512]{1,0:T(8,128)(2,1)S(1)} %bitcast.8), channel_id=1, source_target_pairs={{0,1},{1,0},{2,3},{3,2},{4,5},{5,4},{6,7},{7,6},{8,9},{9,8},{10,11... | collective-permute-start | bytes 786440 | tf_op jit(solution)/shard_map/ppermute | solution.py:169
  8.0 14.6 %collective-permute-start.4 = (s32[1,512]{1,0:T(1,128)S(1)}, s32[1,512]{1,0:T(1,128)S(1)}, u32[]{:S(2)}, u32[]{:S(2)}) collective-permute-start(s32[1,512]{1,0:T(1,128)S(1)} %copy-done.4), channel_id=1, source_target_pairs={{1,0},{3,1},{0,2},{2,3},{5,4},{7,5},{4,6},{6,7},{9,8},{11,9},{8,10... | collective-permute-start | bytes 6152 | tf_op jit(solution)/shard_map/ppermute | solution.py:159
  9.6 16.8 %collective-permute-start.2 = (bf16[272,512]{1,0:T(8,128)(2,1)}, bf16[272,512]{1,0:T(8,128)(2,1)S(1)}, u32[]{:S(2)}, u32[]{:S(2)}) collective-permute-start(bf16[272,512]{1,0:T(8,128)(2,1)} %pad_maximum_fusion), channel_id=1, source_target_pairs={{2,1},{1,2},{6,5},{5,6},{10,9},{9,10},{14,13},{13,14},{18,17},{17,... | collective-permute-start | bytes 835592 | tf_op jit(solution)/shard_map/ppermute | solution.py:159
  11.0 10.8 %copy-start.7 = (bf16[256,512]{1,0:T(8,128)(2,1)S(1)}, bf16[256,512]{1,0:T(8,128)(2,1)}, u32[]{:S(2)}) copy-start(bf16[256,512]{1,0:T(8,128)(2,1)} %get-tuple-element.14) | copy-start | bytes 786436
  21.8 6.9 %collective-permute-start.1 = (bf16[256,512]{1,0:T(8,128)(2,1)S(1)}, bf16[256,512]{1,0:T(8,128)(2,1)S(1)}, u32[]{:S(2)}, u32[]{:S(2)}) collective-permute-start(bf16[256,512]{1,0:T(8,128)(2,1)S(1)} %copy-done.7), channel_id=1, source_target_pairs={{2,1},{1,2},{6,5},{5,6},{10,9},{9,10},{14,13},{13,14},{18,17},{17,... | collective-permute-start | bytes 786440 | tf_op jit(solution)/shard_map/ppermute | solution.py:159
  22.5 3.8 %copy-start.2 = (bf16[1,512,512]{2,1,0:T(8,128)(2,1)S(1)}, bf16[1,512,512]{2,1,0:T(8,128)(2,1)}, u32[]{:S(2)}) copy-start(bf16[1,512,512]{2,1,0:T(8,128)(2,1)} %param.9) | copy-start | bytes 1572868
  30.2 9.4 %copy-start.3 = (bf16[512,512]{1,0:T(8,128)(2,1)S(1)}, bf16[512,512]{1,0:T(8,128)(2,1)}, u32[]{:S(2)}) copy-start(bf16[512,512]{1,0:T(8,128)(2,1)} %w_ref.3) | copy-start | bytes 1572868
  30.2 9.4 %collective-permute-start.5 = (bf16[256,512]{1,0:T(8,128)(2,1)S(1)}, bf16[256,512]{1,0:T(8,128)(2,1)S(1)}, u32[]{:S(2)}, u32[]{:S(2)}) collective-permute-start(bf16[256,512]{1,0:T(8,128)(2,1)S(1)} %attend_theirs.1), channel_id=1, source_target_pairs={{0,1},{1,0},{2,3},{3,2},{4,5},{5,4},{6,7},{7,6},{8,9},{9,8},{10,11... | collective-permute-start | bytes 786440 | tf_op jit(solution)/shard_map/ppermute | solution.py:228
  36.4 3.2 %copy-start.5 = (f32[512]{0:T(512)S(1)}, f32[512]{0:T(512)}, u32[]{:S(2)}) copy-start(f32[512]{0:T(512)} %param.16) | copy-start | bytes 6148

commit v3 on v2

v3 whole, which is shorter than its diff:
```python
import functools
import math

import jax
import jax.numpy as jnp
from jax import lax
from jax.experimental import pallas as pl
from jax.experimental.pallas import tpu as pltpu
from jax.sharding import PartitionSpec as P

SPAN = 256


def silu(x):
    half = 0.5 * x
    return half + half * jnp.tanh(half)


def pick(index, table):
    value = jnp.int32(table[0])
    for i, entry in enumerate(table[1:], 1):
        value = jnp.where(index == i, jnp.int32(entry), value)
    return value


def dot(a, b, dims=((1,), (0,))):
    return lax.dot_general(a, b, (dims, ((), ())), preferred_element_type=jnp.float32)


def project_gates(events_ref, w_ref, w_key_ref, gates_ref):
    del w_key_ref
    width = events_ref.shape[1]
    gates_ref[...] = silu(dot(events_ref[...], w_ref[:, width:]))


def pack(history_ref, labels_ref, head_ref, rest_ref, sems):
    half, width = rest_ref.shape
    copies = [
        pltpu.make_async_copy(history_ref.at[:half], head_ref.at[:half], sems.at[0]),
        pltpu.make_async_copy(history_ref.at[half:], rest_ref, sems.at[1]),
    ]
    for copy in copies:
        copy.start()
    labels = labels_ref[...].astype(jnp.float32)
    for i, at in enumerate(range(0, labels.shape[1], width)):
        part = labels[:, at : at + width]
        row = half + 16 * i
        head_ref[row : row + 16, : part.shape[1]] = jnp.broadcast_to(
            part, (16, part.shape[1])
        ).astype(jnp.bfloat16)
    for copy in copies:
        copy.wait()


def attend(length_ref, *refs, heads, parts, owners, chosen, shard_rows, first, raw, keep, scale):
    refs = list(refs)
    kept_ref = refs.pop() if keep else None
    out_ref = refs.pop()
    total_ref = None if first else refs.pop()
    w_query_ref = refs.pop() if raw else None
    w_ref, table_ref, states_ref = refs[-3:]
    states = states_ref[...]
    if raw:
        states = silu(dot(states, w_query_ref[:, : states.shape[1]])).astype(jnp.bfloat16)
        states = (states * scale).astype(jnp.bfloat16)
    if keep:
        kept_ref[...] = states
    place = lax.axis_index("narrow")
    owner = pick(place, owners)
    total = total_ref
    for at, rows in parts:
        if chosen is None:
            hist_ref, labels_ref = refs[:2]
            hist, labels = hist_ref[at : at + rows], labels_ref[:, at : at + rows]
            width = hist.shape[1]
        else:
            take_own = pick(place, chosen) == 1
            hist_ref, own_ref = refs.pop(0), refs.pop(0)
            hist = jnp.where(take_own, own_ref[:rows], hist_ref[:rows])
            width = hist.shape[1]
            labels_ref, own_labels_ref = refs.pop(0), refs.pop(0)
            where = (
                slice(shard_rows // 2 + 16 * (at // width), shard_rows // 2 + 16 * (at // width) + 16),
                slice(at % width, at % width + rows),
            )
            labels = jnp.where(take_own, own_labels_ref[where], labels_ref[where])
            labels = labels.astype(jnp.float32)[:1].astype(jnp.int32)
        head_size = width // heads
        per_span = SPAN // head_size
        q_rows = states.shape[0]
        start = owner * shard_rows + at
        row = start + lax.broadcasted_iota(jnp.int32, (rows, 1), 0)
        live = (row < length_ref[0]).astype(jnp.float32)
        key_value = dot(hist, w_ref[...])
        keys = silu(key_value[:, :width]).astype(jnp.bfloat16)
        values = (key_value[:, width:] * live).astype(jnp.bfloat16)

        hot = lax.broadcasted_iota(jnp.int32, (table_ref.shape[1], rows), 0) == labels
        bias = dot(table_ref[...], hot.astype(jnp.bfloat16)) * 0.5

        lane = lax.broadcasted_iota(jnp.int32, (1, SPAN), 1) // head_size
        for block in range(width // SPAN):
            cols = slice(block * SPAN, (block + 1) * SPAN)
            queries = states[:, cols]
            stack = [queries * (lane == j).astype(jnp.bfloat16) for j in range(per_span)]
            scores = dot(jnp.concatenate(stack, axis=0), keys[:, cols], ((1,), (1,)))
            weights = []
            for j in range(per_span):
                h = block * per_span + j
                s = scores[j * q_rows : (j + 1) * q_rows] + bias[h : h + 1]
                weights.append((s + s * jnp.tanh(s)).astype(jnp.bfloat16))
            mixed = dot(jnp.concatenate(weights, axis=0), values[:, cols])
            term = mixed[:q_rows]
            for j in range(1, per_span):
                term = jnp.where(lane == j, mixed[j * q_rows : (j + 1) * q_rows], term)
            if total is not None:
                term = term + total[:, cols]
            out_ref[:, cols] = term.astype(out_ref.dtype)
        total = out_ref


def finish(total_ref, other_ref, gates_ref, gain_ref, w_ref, events_ref, out_ref):
    attended = total_ref[...] + other_ref[...].astype(jnp.float32)
    center = jnp.mean(attended, axis=-1, keepdims=True)
    away = attended - center
    spread = jnp.mean(away * away, axis=-1, keepdims=True)
    normed = away * lax.rsqrt(spread + 1e-05)
    mixed = (normed * gain_ref[...] * gates_ref[...]).astype(jnp.bfloat16)
    out_ref[...] = (events_ref[...].astype(jnp.float32) + dot(mixed, w_ref[...])).astype(jnp.bfloat16)


VMEM = pl.BlockSpec(memory_space=pltpu.VMEM)
SMEM = pl.BlockSpec(memory_space=pltpu.SMEM)
PARAMS = pltpu.CompilerParams(vmem_limit_bytes=12 * 1024 * 1024)


def routes(n):
    half = n // 2
    rank = [z if z < half else n - 1 - z for z in range(n)]

    def shard(z, step):
        own_half = (z < half) == (rank[z] % 2 == 0)
        at = (rank[z] + step) % half
        return at if own_half else n - 1 - at

    sources = []
    for step in range(half):
        row = []
        for z in range(n):
            source = shard(z, step)
            row.append(source if z < half else n - 1 - shard(n - 1 - z, step))
        sources.append(row)
    return rank, sources


def cost(flops, *arrays):
    return pl.CostEstimate(
        flops=flops,
        bytes_accessed=sum(a.size * a.dtype.itemsize for a in arrays),
        transcendentals=0,
    )


def on_device(
    hist_events, query_events, hist_lengths, time_buckets, w_key, w_query, bias_table, out_gain, w_out, *, n
):
    history, queries_in, buckets = hist_events[0], query_events[0], time_buckets
    shard_rows, width = history.shape
    q_rows = queries_in.shape[0]
    heads = bias_table.shape[1]
    scale = 0.5 / math.sqrt(width // heads)
    rank, sources = routes(n)
    swap = [(z, z ^ 1) for z in range(n)]

    def send(x, step):
        pairs = [(source, z) for z, source in enumerate(sources[step]) if source != z]
        return lax.ppermute(x, "narrow", pairs)

    half = shard_rows // 2
    pieces = [(step, at, half) for step in range(n // 2) for at in (0, half)]
    received = {step: [send(history, step)] for step in range(1, n // 2)}
    label_rows = 16 * (-(-shard_rows // width))
    head, rest = pl.pallas_call(
        pack,
        out_shape=(
            jax.ShapeDtypeStruct((half + label_rows, width), jnp.bfloat16),
            jax.ShapeDtypeStruct((half, width), jnp.bfloat16),
        ),
        in_specs=[pl.BlockSpec(memory_space=pl.ANY), VMEM],
        out_specs=[VMEM] * 2,
        scratch_shapes=[pltpu.SemaphoreType.DMA((2,))],
        compiler_params=PARAMS,
        name="pack",
    )(history, buckets)
    queries_out, labels, head_own, rest_own = lax.optimization_barrier(
        (queries_in, buckets, head, rest)
    )
    other_queries = lax.ppermute(queries_out, "narrow", swap)
    for step in range(1, n // 2):
        received[step].append(send(labels, step))
    head = send(head_own, 0)

    gates = pl.pallas_call(
        project_gates,
        out_shape=jax.ShapeDtypeStruct((q_rows, width), jnp.float32),
        in_specs=[VMEM] * 3,
        out_specs=VMEM,
        compiler_params=PARAMS,
        cost_estimate=cost(2 * q_rows * width * width, queries_in, w_query),
        name="project_gates",
    )(queries_in, w_query, w_key)
    rest_own, gates = lax.optimization_barrier((rest_own, gates))
    rest = send(rest_own, 0)

    def absorb(states, indices, total, dtype, name, raw=False, keep=False):
        step = pieces[indices[0]][0]
        parts = [pieces[index][1:] for index in indices]
        operands = [hist_lengths]
        chosen = None
        for at, _ in parts:
            if step == 0:
                chosen = [int(sources[0][z] == z) for z in range(n)]
                operands += [rest if at else head, rest_own if at else head_own, head, head_own]
        if step:
            operands += received[step]
        operands += [w_key, bias_table.T, states]
        if raw:
            operands.append(w_query)
        if total is not None:
            operands.append(total)
        body = functools.partial(
            attend,
            heads=heads,
            parts=parts,
            owners=sources[step],
            chosen=chosen,
            shard_rows=shard_rows,
            first=total is None,
            raw=raw,
            keep=keep,
            scale=scale,
        )
        rows = sum(size for _, size in parts)
        shape = jax.ShapeDtypeStruct((q_rows, width), dtype)
        kept = jax.ShapeDtypeStruct((q_rows, width), jnp.bfloat16)
        return pl.pallas_call(
            body,
            out_shape=(shape, kept) if keep else shape,
            in_specs=[SMEM] + [VMEM] * (len(operands) - 1),
            out_specs=[VMEM] * 2 if keep else VMEM,
            compiler_params=PARAMS,
            cost_estimate=cost(64 * q_rows * rows * width, *operands),
            name=name,
        )(*operands)

    own = None
    for step in range(1, n // 2):
        own = absorb(
            queries_in, [2 * step, 2 * step + 1], own, jnp.float32, f"own_far{step}", raw=True
        )
    other_queries, own = lax.optimization_barrier((other_queries, own))
    theirs, other_states = absorb(
        other_queries, [2, 3], None, jnp.float32, "theirs_far1", raw=True, keep=True
    )
    for step in range(2, n // 2):
        theirs = absorb(other_states, [2 * step, 2 * step + 1], theirs, jnp.float32, f"theirs_far{step}")
    theirs = absorb(other_states, [0], theirs, jnp.float32, "theirs_near0")
    theirs = absorb(other_states, [1], theirs, jnp.bfloat16, "theirs_near1")
    theirs_sent, own, rest = lax.optimization_barrier((theirs, own, rest))
    theirs = lax.ppermute(theirs_sent, "narrow", swap)
    own = absorb(queries_in, [0, 1], own, jnp.float32, "own_near", raw=True)
    result = pl.pallas_call(
        finish,
        out_shape=jax.ShapeDtypeStruct((q_rows, width), jnp.bfloat16),
        in_specs=[VMEM] * 6,
        out_specs=VMEM,
        compiler_params=PARAMS,
        cost_estimate=cost(2 * q_rows * width * width, own, w_out),
        name="finish",
    )(own, theirs, gates, out_gain[None], w_out, queries_in)
    return result[None]


def solution(mesh):
    in_specs = (
        P(("parts", "wide"), "narrow", None),
        P(("parts", "wide"), "narrow", None),
        P(("parts", "wide")),
        P(("parts", "wide"), "narrow"),
        P(),
        P(),
        P(),
        P(),
        P(),
    )
    out_specs = P(("parts", "wide"), "narrow", None)
    return jax.shard_map(
        functools.partial(on_device, n=mesh.shape["narrow"]),
        mesh=mesh,
        in_specs=in_specs,
        out_specs=out_specs,
        check_vma=False,
    )
```

time: 41 us -> 38.7 us (0.944)
  waiting for transfers between devices: 13.3 us -> 10 us
  other arithmetic: 1.42 us -> 0 us
  local copies, waits for them, and re-layouts: 2.64 us -> 3.55 us
  starting transfers between devices: 11.7 us -> 12.4 us
  Pallas kernels: 11 us -> 11.6 us
    ppermute x1, waiting for transfers between devices: 10.1 us -> 2.06 us  [on_device(): other_queries = lax.ppermute(queries_out, 'narrow', swap)]
    ppermute x4, waiting for transfers between devices: 0.01 us -> 3.86 us  [send(): return lax.ppermute(x, 'narrow', pairs)]
    unnamed x19 -> x18, local copies, waits for them, and re-layouts: 0.84 us -> 3.55 us
    slice x1 -> x0, local copies, waits for them, and re-layouts: 1.76 us -> none  [on_device(): rest = history[half:]]
    ppermute x1, waiting for transfers between devices: 3.16 us -> 4.12 us  [on_device(): theirs = lax.ppermute(theirs_sent, 'narrow', swap)]
    concatenate x1 -> x0, other arithmetic: 0.72 us -> none  [on_device(): head = jnp.concatenate([history[:half], bucket_rows])]
    convert_element_type x1 -> x0, other arithmetic: 0.7 us -> none  [on_device(): buckets[0].astype(jnp.bfloat16)]
    pallas_call x5 -> x7, Pallas kernels: 9.79 us -> 10.4 us  [the longest x5 9.34 us: absorb(): pl.pallas_call(body, out_shape=(shape, kept) if keep else shape, in_specs...]
  transfers between devices with their start and end apart: 6 -> 6, of which waited for: 2 -> 3; matrix products, arithmetic and copies ran while one was open for 8% -> 0% of each run, Pallas kernels for 20% -> 24%
where the time goes in v3:
time: 38.7 us; the launch traced here: 38.4 us
  starting transfers between devices  12.4 us (32%)
  Pallas kernels  11.6 us (30%)
  waiting for transfers between devices  10 us (26%)
  local copies, waits for them, and re-layouts  3.55 us (9%)
  between operations  0.77 us (2%)
    pallas_call x5, Pallas kernels, absorb(): pl.pallas_call(body, out_shape=(shape, kept) if keep else shape, in_specs...  9.34 us
    ppermute x4, starting transfers between devices, send(): return lax.ppermute(x, 'narrow', pairs)  7.14 us
    ppermute x1, starting transfers between devices, on_device(): theirs = lax.ppermute(theirs_sent, 'narrow', swap)  4.82 us
    ppermute x1, waiting for transfers between devices, on_device(): theirs = lax.ppermute(theirs_sent, 'narrow', swap)  4.12 us
    ppermute x4, waiting for transfers between devices, send(): return lax.ppermute(x, 'narrow', pairs)  3.86 us
    unnamed x18, local copies, waits for them, and re-layouts  3.55 us
    ppermute x1, waiting for transfers between devices, on_device(): other_queries = lax.ppermute(queries_out, 'narrow', swap)  2.06 us
    pallas_call x1, Pallas kernels, on_device(): pl.pallas_call(finish, out_shape=jax.ShapeDtypeStruct((q_rows, width), jn...  1.22 us
  transfers between devices with their start and end apart: 6, of which 3 were waited for; matrix products, arithmetic and copies ran while one was open for 0% of the time, Pallas kernels for 24%

profile of v3, /device:TPU:0, one launch (start us, length us, event | category | flops | bytes accessed | tf_op | source)
XLA Modules:
  0.0 38.4 jit_solution(12196850296751153574)
XLA Ops:
  0.0 4.0 %collective-permute-start.2 = (bf16[512,512]{1,0:T(8,128)(2,1)}, bf16[512,512]{1,0:T(8,128)(2,1)S(1)}, u32[]{:S(2)}, u32[]{:S(2)}) collective-permute-start(bf16[512,512]{1,0:T(8,128)(2,1)} %bitcast.10), channel_id=1, source_target_pairs={{1,0},{3,1},{0,2},{2,3},{5,4},{7,5},{4,6},{6,7},{9,8},{11,9},{8,10... | collective-permute-start | bytes 1572872 | tf_op jit(solution)/shard_map/ppermute | solution.py:177
  4.0 1.1 %copy-done.5 = bf16[1,512,512]{2,1,0:T(8,128)(2,1)S(1)} copy-done((bf16[1,512,512]{2,1,0:T(8,128)(2,1)S(1)}, bf16[1,512,512]{2,1,0:T(8,128)(2,1)}, u32[]{:S(2)}) %copy-start.5) | copy-done | bytes 524312
  5.1 0.7 %pack.1 = (bf16[272,512]{1,0:T(8,128)(2,1)S(1)}, bf16[256,512]{1,0:T(8,128)(2,1)S(1)}) custom-call(bf16[512,512]{1,0:T(8,128)(2,1)S(1)} %bitcast.11, s32[1,512]{1,0:T(1,128)} %labels_ref.1), custom_call_target="tpu_custom_call" | custom-call | tf_op jit(solution)/shard_map/pack/pallas_call | solution.py:183
  5.9 1.6 %collective-permute-start.3 = (s32[1,512]{1,0:T(1,128)}, s32[1,512]{1,0:T(1,128)S(1)}, u32[]{:S(2)}, u32[]{:S(2)}) collective-permute-start(s32[1,512]{1,0:T(1,128)} %labels_ref.1), channel_id=1, source_target_pairs={{1,0},{3,1},{0,2},{2,3},{5,4},{7,5},{4,6},{6,7},{9,8},{11,9},{8,10... | collective-permute-start | bytes 6152 | tf_op jit(solution)/shard_map/ppermute | solution.py:177
  7.5 0.4 %collective-permute-start.4 = (bf16[256,512]{1,0:T(8,128)(2,1)S(1)}, bf16[256,512]{1,0:T(8,128)(2,1)S(1)}, u32[]{:S(2)}, u32[]{:S(2)}) collective-permute-start(bf16[256,512]{1,0:T(8,128)(2,1)S(1)} %bitcast.5), channel_id=1, source_target_pairs={{0,1},{1,0},{2,3},{3,2},{4,5},{5,4},{6,7},{7,6},{8,9},{9,8},{10,11... | collective-permute-start | bytes 786440 | tf_op jit(solution)/shard_map/ppermute | solution.py:198
  7.9 0.7 %collective-permute-start = (bf16[272,512]{1,0:T(8,128)(2,1)S(1)}, bf16[272,512]{1,0:T(8,128)(2,1)S(1)}, u32[]{:S(2)}, u32[]{:S(2)}) collective-permute-start(bf16[272,512]{1,0:T(8,128)(2,1)S(1)} %get-tuple-element.22.refs_1_.refs_3_.refs_7_), channel_id=1, source_target_pairs={{2,1},{1,2},{6,5},{5,6},{10,9},{9,10},{14,13},{13,14},{18,17},{17,... | collective-permute-start | bytes 835592 | tf_op jit(solution)/shard_map/ppermute | solution.py:177
  8.6 0.0 copy-start
  8.6 1.2 %copy-done = bf16[512,1024]{1,0:T(8,128)(2,1)S(1)} copy-done((bf16[512,1024]{1,0:T(8,128)(2,1)S(1)}, bf16[512,1024]{1,0:T(8,128)(2,1)}, u32[]{:S(2)}) %copy-start) | copy-done | bytes 1048600
  9.9 1.2 %copy-done.2 = bf16[512,1024]{1,0:T(8,128)(2,1)S(1)} copy-done((bf16[512,1024]{1,0:T(8,128)(2,1)S(1)}, bf16[512,1024]{1,0:T(8,128)(2,1)}, u32[]{:S(2)}) %copy-start.2) | copy-done | bytes 1048600
  11.1 0.3 project_gates.1.gates_ref
  11.4 0.0 copy-start.8
  11.4 0.8 %collective-permute-start.1 = (bf16[256,512]{1,0:T(8,128)(2,1)S(1)}, bf16[256,512]{1,0:T(8,128)(2,1)S(1)}, u32[]{:S(2)}, u32[]{:S(2)}) collective-permute-start(bf16[256,512]{1,0:T(8,128)(2,1)S(1)} %get-tuple-element.24.refs_1_.refs_5_), channel_id=1, source_target_pairs={{2,1},{1,2},{6,5},{5,6},{10,9},{9,10},{14,13},{13,14},{18,17},{17,... | collective-permute-start | bytes 786440 | tf_op jit(solution)/shard_map/ppermute | solution.py:177
  12.9 3.8 %collective-permute-done.3.refs_1_ = s32[1,512]{1,0:T(1,128)S(1)} collective-permute-done((s32[1,512]{1,0:T(1,128)}, s32[1,512]{1,0:T(1,128)S(1)}, u32[]{:S(2)}, u32[]{:S(2)}) %collective-permute-start.3) | collective-permute-done | bytes 2080 | tf_op jit(solution)/shard_map/ppermute | solution.py:177
  16.7 0.0 collective-permute-done.2.refs_0_
  16.7 2.3 %own_far1.1.refs_12_ = f32[256,512]{1,0:T(8,128)S(1)} custom-call(s32[1]{0:T(128)S(6)} %copy.10.length_ref, bf16[512,512]{1,0:T(8,128)(2,1)S(1)} %collective-permute-done.2.refs_0_, s32[1,512]{1,0:T(1,128)S(1)} %collective-permute-done.3.refs_1_, bf16[512,1024]{1,0:T(8,128)(2,1)S(1)} %copy-done.1, bf16[8,128]{1,0:T(8,128)(2,1)S(1)} %bitcast.13, ...), custom_call_target="tpu_custom_call" | custom-call | flops 4294967296 | bytes 2887684 | tf_op jit(solution)/shard_map/own_far1/pallas_call | solution.py:246
  19.1 2.1 %collective-permute-done.4.refs_4_ = bf16[256,512]{1,0:T(8,128)(2,1)S(1)} collective-permute-done((bf16[256,512]{1,0:T(8,128)(2,1)S(1)}, bf16[256,512]{1,0:T(8,128)(2,1)S(1)}, u32[]{:S(2)}, u32[]{:S(2)}) %collective-permute-start.4) | collective-permute-done | bytes 262176 | tf_op jit(solution)/shard_map/ppermute | solution.py:198
  21.1 2.4 %theirs_far1.1 = (f32[256,512]{1,0:T(8,128)S(1)}, bf16[256,512]{1,0:T(8,128)(2,1)S(1)}) custom-call(s32[1]{0:T(128)S(6)} %copy.10.length_ref, bf16[512,512]{1,0:T(8,128)(2,1)S(1)} %collective-permute-done.2.refs_0_, s32[1,512]{1,0:T(1,128)S(1)} %collective-permute-done.3.refs_1_, bf16[512,1024]{1,0:T(8,128)(2,1)S(1)} %copy-done.1, ...), custom_call_target="tpu_custom_call" | custom-call | flops 4294967296 | bytes 2887684 | tf_op jit(solution)/shard_map/theirs_far1/pallas_call | solution.py:246
  23.5 1.1 %theirs_near0.1.refs_7_ = f32[256,512]{1,0:T(8,128)S(1)} custom-call(s32[1]{0:T(128)S(6)} %copy.10.length_ref, bf16[272,512]{1,0:T(8,128)(2,1)S(1)} %collective-permute-done.refs_0_.refs_2_.refs_6_, bf16[272,512]{1,0:T(8,128)(2,1)S(1)} %get-tuple-element.22.refs_1_.refs_3_.refs_7_, bf16[272,512]{1,0:T(8,128)(2,1)S(1)} %collective-permute-done.refs_0_.refs_2_.refs_6_, ...), custom_call_target="tpu_custom_call" | custom-call | flops 2147483648 | bytes 2951172 | tf_op jit(solution)/shard_map/theirs_near0/pallas_call | solution.py:246
  24.7 1.2 %theirs_near1.1 = bf16[256,512]{1,0:T(8,128)(2,1)S(1)} custom-call(s32[1]{0:T(128)S(6)} %copy.10.length_ref, bf16[256,512]{1,0:T(8,128)(2,1)S(1)} %collective-permute-done.1.refs_0_.refs_4_, bf16[256,512]{1,0:T(8,128)(2,1)S(1)} %get-tuple-element.24.refs_1_.refs_5_, bf16[272,512]{1,0:T(8,128)(2,1)S(1)} %collective-permute-done.refs_0_.refs_2_.refs_6_, ...), custom_call_target="tpu_custom_call" | custom-call | flops 2147483648 | bytes 2918404 | tf_op jit(solution)/shard_map/theirs_near1/pallas_call | solution.py:246
  25.8 0.0 copy-start.6
  25.8 4.8 %collective-permute-start.5 = (bf16[256,512]{1,0:T(8,128)(2,1)S(1)}, bf16[256,512]{1,0:T(8,128)(2,1)S(1)}, u32[]{:S(2)}, u32[]{:S(2)}) collective-permute-start(bf16[256,512]{1,0:T(8,128)(2,1)S(1)} %theirs_near1.1), channel_id=1, source_target_pairs={{0,1},{1,0},{2,3},{3,2},{4,5},{5,4},{6,7},{7,6},{8,9},{9,8},{10,11... | collective-permute-start | bytes 786440 | tf_op jit(solution)/shard_map/ppermute | solution.py:270
  30.7 2.4 %own_near.1.total_ref = f32[256,512]{1,0:T(8,128)S(1)} custom-call(s32[1]{0:T(128)S(6)} %copy.10.length_ref, bf16[272,512]{1,0:T(8,128)(2,1)S(1)} %collective-permute-done.refs_0_.refs_2_.refs_6_, bf16[272,512]{1,0:T(8,128)(2,1)S(1)} %get-tuple-element.22.refs_1_.refs_3_.refs_7_, bf16[272,512]{1,0:T(8,128)(2,1)S(1)} %collective-permute-done.refs_0_.refs_2_.refs_6_, ...), custom_call_target="tpu_custom_call" | custom-call | flops 4294967296 | bytes 5081092 | tf_op jit(solution)/shard_map/own_near/pallas_call | solution.py:246
  33.0 4.1 %collective-permute-done.5.other_ref = bf16[256,512]{1,0:T(8,128)(2,1)S(1)} collective-permute-done((bf16[256,512]{1,0:T(8,128)(2,1)S(1)}, bf16[256,512]{1,0:T(8,128)(2,1)S(1)}, u32[]{:S(2)}, u32[]{:S(2)}) %collective-permute-start.5) | collective-permute-done | bytes 262176 | tf_op jit(solution)/shard_map/ppermute | solution.py:270
  37.2 1.2 %finish.1 = bf16[256,512]{1,0:T(8,128)(2,1)} custom-call(f32[256,512]{1,0:T(8,128)S(1)} %own_near.1.total_ref, bf16[256,512]{1,0:T(8,128)(2,1)S(1)} %collective-permute-done.5.other_ref, f32[256,512]{1,0:T(8,128)S(1)} %project_gates.1.gates_ref, f32[1,512]{1,0:T(1,128)S(1)} %bitcast.12, bf16[512,512]{1,0:T(8,128)(2,1)S(1)} %copy-done.6, ...), custom_call_target="tpu_custom_call" | custom-call | flops 134217728 | bytes 1048576 | tf_op jit(solution)/shard_map/finish/pallas_call | solution.py:272
  (14 shorter events, 0.0 us)
Async XLA Ops:
  0.0 7.5 %copy-start.4 = (bf16[1,256,512]{2,1,0:T(8,128)(2,1)S(1)}, bf16[1,256,512]{2,1,0:T(8,128)(2,1)}, u32[]{:S(2)}) copy-start(bf16[1,256,512]{2,1,0:T(8,128)(2,1)} %param.10) | copy-start | bytes 786436
  0.0 16.7 %collective-permute-start.2 = (bf16[512,512]{1,0:T(8,128)(2,1)}, bf16[512,512]{1,0:T(8,128)(2,1)S(1)}, u32[]{:S(2)}, u32[]{:S(2)}) collective-permute-start(bf16[512,512]{1,0:T(8,128)(2,1)} %bitcast.10), channel_id=1, source_target_pairs={{1,0},{3,1},{0,2},{2,3},{5,4},{7,5},{4,6},{6,7},{9,8},{11,9},{8,10... | collective-permute-start | bytes 1572872 | tf_op jit(solution)/shard_map/ppermute | solution.py:177
  4.0 1.1 %copy-start.5 = (bf16[1,512,512]{2,1,0:T(8,128)(2,1)S(1)}, bf16[1,512,512]{2,1,0:T(8,128)(2,1)}, u32[]{:S(2)}) copy-start(bf16[1,512,512]{2,1,0:T(8,128)(2,1)} %param.9) | copy-start | bytes 1572868
  5.9 10.9 %collective-permute-start.3 = (s32[1,512]{1,0:T(1,128)}, s32[1,512]{1,0:T(1,128)S(1)}, u32[]{:S(2)}, u32[]{:S(2)}) collective-permute-start(s32[1,512]{1,0:T(1,128)} %labels_ref.1), channel_id=1, source_target_pairs={{1,0},{3,1},{0,2},{2,3},{5,4},{7,5},{4,6},{6,7},{9,8},{11,9},{8,10... | collective-permute-start | bytes 6152 | tf_op jit(solution)/shard_map/ppermute | solution.py:177
  7.5 13.6 %collective-permute-start.4 = (bf16[256,512]{1,0:T(8,128)(2,1)S(1)}, bf16[256,512]{1,0:T(8,128)(2,1)S(1)}, u32[]{:S(2)}, u32[]{:S(2)}) collective-permute-start(bf16[256,512]{1,0:T(8,128)(2,1)S(1)} %bitcast.5), channel_id=1, source_target_pairs={{0,1},{1,0},{2,3},{3,2},{4,5},{5,4},{6,7},{7,6},{8,9},{9,8},{10,11... | collective-permute-start | bytes 786440 | tf_op jit(solution)/shard_map/ppermute | solution.py:198
  7.9 15.6 %collective-permute-start = (bf16[272,512]{1,0:T(8,128)(2,1)S(1)}, bf16[272,512]{1,0:T(8,128)(2,1)S(1)}, u32[]{:S(2)}, u32[]{:S(2)}) collective-permute-start(bf16[272,512]{1,0:T(8,128)(2,1)S(1)} %get-tuple-element.22.refs_1_.refs_3_.refs_7_), channel_id=1, source_target_pairs={{2,1},{1,2},{6,5},{5,6},{10,9},{9,10},{14,13},{13,14},{18,17},{17,... | collective-permute-start | bytes 835592 | tf_op jit(solution)/shard_map/ppermute | solution.py:177
  8.6 1.2 %copy-start = (bf16[512,1024]{1,0:T(8,128)(2,1)S(1)}, bf16[512,1024]{1,0:T(8,128)(2,1)}, u32[]{:S(2)}) copy-start(bf16[512,1024]{1,0:T(8,128)(2,1)} %refs_8_.1) | copy-start | bytes 3145732
  9.8 1.2 %copy-start.2 = (bf16[512,1024]{1,0:T(8,128)(2,1)S(1)}, bf16[512,1024]{1,0:T(8,128)(2,1)}, u32[]{:S(2)}) copy-start(bf16[512,1024]{1,0:T(8,128)(2,1)} %refs_11_.1) | copy-start | bytes 3145732
  11.1 5.7 %copy-start.1 = (bf16[512,1024]{1,0:T(8,128)(2,1)S(1)}, bf16[512,1024]{1,0:T(8,128)(2,1)}, u32[]{:S(2)}) copy-start(bf16[512,1024]{1,0:T(8,128)(2,1)} %refs_8_.1) | copy-start | bytes 3145732
  11.1 5.7 %copy-start.3 = (bf16[512,1024]{1,0:T(8,128)(2,1)S(1)}, bf16[512,1024]{1,0:T(8,128)(2,1)}, u32[]{:S(2)}) copy-start(bf16[512,1024]{1,0:T(8,128)(2,1)} %refs_11_.1) | copy-start | bytes 3145732
  11.4 5.3 %copy-start.8 = (bf16[128,8]{0,1:T(8,128)(2,1)S(1)}, bf16[128,8]{0,1:T(8,128)(2,1)}, u32[]{:S(2)}) copy-start(bf16[128,8]{0,1:T(8,128)(2,1)} %param.15) | copy-start | bytes 6148
  11.4 13.3 %collective-permute-start.1 = (bf16[256,512]{1,0:T(8,128)(2,1)S(1)}, bf16[256,512]{1,0:T(8,128)(2,1)S(1)}, u32[]{:S(2)}, u32[]{:S(2)}) collective-permute-start(bf16[256,512]{1,0:T(8,128)(2,1)S(1)} %get-tuple-element.24.refs_1_.refs_5_), channel_id=1, source_target_pairs={{2,1},{1,2},{6,5},{5,6},{10,9},{9,10},{14,13},{13,14},{18,17},{17,... | collective-permute-start | bytes 786440 | tf_op jit(solution)/shard_map/ppermute | solution.py:177
  25.8 11.3 %copy-start.6 = (bf16[512,512]{1,0:T(8,128)(2,1)S(1)}, bf16[512,512]{1,0:T(8,128)(2,1)}, u32[]{:S(2)}) copy-start(bf16[512,512]{1,0:T(8,128)(2,1)} %w_ref.3) | copy-start | bytes 1572868
  25.8 11.3 %collective-permute-start.5 = (bf16[256,512]{1,0:T(8,128)(2,1)S(1)}, bf16[256,512]{1,0:T(8,128)(2,1)S(1)}, u32[]{:S(2)}, u32[]{:S(2)}) collective-permute-start(bf16[256,512]{1,0:T(8,128)(2,1)S(1)} %theirs_near1.1), channel_id=1, source_target_pairs={{0,1},{1,0},{2,3},{3,2},{4,5},{5,4},{6,7},{7,6},{8,9},{9,8},{10,11... | collective-permute-start | bytes 786440 | tf_op jit(solution)/shard_map/ppermute | solution.py:270
  30.7 6.5 %copy-start.7 = (f32[512]{0:T(512)S(1)}, f32[512]{0:T(512)}, u32[]{:S(2)}) copy-start(f32[512]{0:T(512)} %param.16) | copy-start | bytes 6148

commit v4 on v3

--- a/solution.py
+++ b/solution.py
@@ -52,14 +52,16 @@
         copy.wait()
 
 
-def attend(length_ref, *refs, heads, parts, owners, chosen, shard_rows, first, raw, keep, scale):
+def attend(length_ref, *refs, heads, parts, owners, chosen, shard_rows, first, raw, keep, save, given, scale):
     refs = list(refs)
+    saved = [refs.pop() for _ in range(3)] if save else None
     kept_ref = refs.pop() if keep else None
     out_ref = refs.pop()
     total_ref = None if first else refs.pop()
     w_query_ref = refs.pop() if raw else None
-    w_ref, table_ref, states_ref = refs[-3:]
-    states = states_ref[...]
+    states = refs.pop()[...]
+    if not given:
+        table_ref, w_ref = refs.pop(), refs.pop()
     if raw:
         states = silu(dot(states, w_query_ref[:, : states.shape[1]])).astype(jnp.bfloat16)
         states = (states * scale).astype(jnp.bfloat16)
@@ -69,14 +71,21 @@
     owner = pick(place, owners)
     total = total_ref
     for at, rows in parts:
-        if chosen is None:
-            hist_ref, labels_ref = refs[:2]
+        if given:
+            keys_ref, values_ref, bias_ref = refs
+            keys, values = keys_ref[at : at + rows], values_ref[at : at + rows]
+            bias = bias_ref[:, at : at + rows]
+            width = keys.shape[1]
+        elif chosen is None:
+            hist_ref, labels_ref = refs
             hist, labels = hist_ref[at : at + rows], labels_ref[:, at : at + rows]
             width = hist.shape[1]
         else:
             take_own = pick(place, chosen) == 1
-            hist_ref, own_ref = refs.pop(0), refs.pop(0)
-            hist = jnp.where(take_own, own_ref[:rows], hist_ref[:rows])
+            hist = refs.pop(0)[:rows]
+            if at:
+                hist = jnp.where(lax.axis_index("wide") % 2 == 0, hist, refs.pop(0)[:rows])
+            hist = jnp.where(take_own, refs.pop(0)[:rows], hist)
             width = hist.shape[1]
             labels_ref, own_labels_ref = refs.pop(0), refs.pop(0)
             where = (
@@ -88,15 +97,19 @@
         head_size = width // heads
         per_span = SPAN // head_size
         q_rows = states.shape[0]
-        start = owner * shard_rows + at
-        row = start + lax.broadcasted_iota(jnp.int32, (rows, 1), 0)
-        live = (row < length_ref[0]).astype(jnp.float32)
-        key_value = dot(hist, w_ref[...])
-        keys = silu(key_value[:, :width]).astype(jnp.bfloat16)
-        values = (key_value[:, width:] * live).astype(jnp.bfloat16)
-
-        hot = lax.broadcasted_iota(jnp.int32, (table_ref.shape[1], rows), 0) == labels
-        bias = dot(table_ref[...], hot.astype(jnp.bfloat16)) * 0.5
+        if not given:
+            start = owner * shard_rows + at
+            row = start + lax.broadcasted_iota(jnp.int32, (rows, 1), 0)
+            live = (row < length_ref[0]).astype(jnp.float32)
+            key_value = dot(hist, w_ref[...])
+            keys = silu(key_value[:, :width]).astype(jnp.bfloat16)
+            values = (key_value[:, width:] * live).astype(jnp.bfloat16)
+            hot = lax.broadcasted_iota(jnp.int32, (table_ref.shape[1], rows), 0) == labels
+            bias = dot(table_ref[...], hot.astype(jnp.bfloat16)) * 0.5
+        if save:
+            saved[2][at : at + rows] = keys
+            saved[1][at : at + rows] = values
+            saved[0][:, at : at + rows] = bias
 
         lane = lax.broadcasted_iota(jnp.int32, (1, SPAN), 1) // head_size
         for block in range(width // SPAN):
@@ -162,7 +175,7 @@
 
 
 def on_device(
-    hist_events, query_events, hist_lengths, time_buckets, w_key, w_query, bias_table, out_gain, w_out, *, n
+    hist_events, query_events, hist_lengths, time_buckets, w_key, w_query, bias_table, out_gain, w_out, *, n, wide
 ):
     history, queries_in, buckets = hist_events[0], query_events[0], time_buckets
     shard_rows, width = history.shape
@@ -172,9 +185,13 @@
     rank, sources = routes(n)
     swap = [(z, z ^ 1) for z in range(n)]
 
-    def send(x, step):
+    def send(x, step, turn=None):
         pairs = [(source, z) for z, source in enumerate(sources[step]) if source != z]
-        return lax.ppermute(x, "narrow", pairs)
+        if turn is None:
+            return lax.ppermute(x, "narrow", pairs)
+        lines = [i * n for i in range(wide) if i % 2 == turn]
+        pairs = [(line + a, line + b) for line in lines for a, b in pairs]
+        return lax.ppermute(x, ("wide", "narrow"), pairs)
 
     half = shard_rows // 2
     pieces = [(step, at, half) for step in range(n // 2) for at in (0, half)]
@@ -210,9 +227,9 @@
         name="project_gates",
     )(queries_in, w_query, w_key)
     rest_own, gates = lax.optimization_barrier((rest_own, gates))
-    rest = send(rest_own, 0)
-
-    def absorb(states, indices, total, dtype, name, raw=False, keep=False):
+    rests = [send(rest_own, 0, 0)]
+
+    def absorb(states, indices, total, dtype, name, raw=False, keep=False, save=False, given=None):
         step = pieces[indices[0]][0]
         parts = [pieces[index][1:] for index in indices]
         operands = [hist_lengths]
@@ -220,10 +237,15 @@
         for at, _ in parts:
             if step == 0:
                 chosen = [int(sources[0][z] == z) for z in range(n)]
-                operands += [rest if at else head, rest_own if at else head_own, head, head_own]
-        if step:
+                operands += [*rests, rest_own] if at else [head, head_own]
+                operands += [head, head_own]
+        if given is not None:
+            operands += given
+        elif step:
             operands += received[step]
-        operands += [w_key, bias_table.T, states]
+        if given is None:
+            operands += [w_key, bias_table.T]
+        operands.append(states)
         if raw:
             operands.append(w_query)
         if total is not None:
@@ -238,37 +260,57 @@
             first=total is None,
             raw=raw,
             keep=keep,
+            save=save,
+            given=given is not None,
             scale=scale,
         )
         rows = sum(size for _, size in parts)
-        shape = jax.ShapeDtypeStruct((q_rows, width), dtype)
-        kept = jax.ShapeDtypeStruct((q_rows, width), jnp.bfloat16)
+        shapes = [jax.ShapeDtypeStruct((q_rows, width), dtype)]
+        if keep:
+            shapes.append(jax.ShapeDtypeStruct((q_rows, width), jnp.bfloat16))
+        if save:
+            shapes += [jax.ShapeDtypeStruct((rows, width), jnp.bfloat16)] * 2
+            shapes.append(jax.ShapeDtypeStruct((heads, rows), jnp.float32))
         return pl.pallas_call(
             body,
-            out_shape=(shape, kept) if keep else shape,
+            out_shape=shapes,
             in_specs=[SMEM] + [VMEM] * (len(operands) - 1),
-            out_specs=[VMEM] * 2 if keep else VMEM,
+            out_specs=[VMEM] * len(shapes),
             compiler_params=PARAMS,
             cost_estimate=cost(64 * q_rows * rows * width, *operands),
             name=name,
         )(*operands)
 
-    own = None
+    own, known = None, {}
     for step in range(1, n // 2):
-        own = absorb(
-            queries_in, [2 * step, 2 * step + 1], own, jnp.float32, f"own_far{step}", raw=True
+        own, *known[step] = absorb(
+            queries_in,
+            [2 * step, 2 * step + 1],
+            own,
+            jnp.float32,
+            f"own_far{step}",
+            raw=True,
+            save=True,
         )
-    other_queries, own = lax.optimization_barrier((other_queries, own))
+    rest_own, other_queries, own = lax.optimization_barrier((rest_own, other_queries, own))
+    rests.append(send(rest_own, 0, 1))
     theirs, other_states = absorb(
-        other_queries, [2, 3], None, jnp.float32, "theirs_far1", raw=True, keep=True
+        other_queries, [2, 3], None, jnp.float32, "theirs_far1", raw=True, keep=True, given=known[1]
     )
     for step in range(2, n // 2):
-        theirs = absorb(other_states, [2 * step, 2 * step + 1], theirs, jnp.float32, f"theirs_far{step}")
-    theirs = absorb(other_states, [0], theirs, jnp.float32, "theirs_near0")
-    theirs = absorb(other_states, [1], theirs, jnp.bfloat16, "theirs_near1")
-    theirs_sent, own, rest = lax.optimization_barrier((theirs, own, rest))
+        (theirs,) = absorb(
+            other_states,
+            [2 * step, 2 * step + 1],
+            theirs,
+            jnp.float32,
+            f"theirs_far{step}",
+            given=known[step],
+        )
+    (theirs,) = absorb(other_states, [0], theirs, jnp.float32, "theirs_near0")
+    (theirs,) = absorb(other_states, [1], theirs, jnp.bfloat16, "theirs_near1")
+    theirs_sent, own, rests[1] = lax.optimization_barrier((theirs, own, rests[1]))
     theirs = lax.ppermute(theirs_sent, "narrow", swap)
-    own = absorb(queries_in, [0, 1], own, jnp.float32, "own_near", raw=True)
+    (own,) = absorb(queries_in, [0, 1], own, jnp.float32, "own_near", raw=True)
     result = pl.pallas_call(
         finish,
         out_shape=jax.ShapeDtypeStruct((q_rows, width), jnp.bfloat16),
@@ -295,7 +337,7 @@
     )
     out_specs = P(("parts", "wide"), "narrow", None)
     return jax.shard_map(
-        functools.partial(on_device, n=mesh.shape["narrow"]),
+        functools.partial(on_device, n=mesh.shape["narrow"], wide=mesh.shape["wide"]),
         mesh=mesh,
         in_specs=in_specs,
         out_specs=out_specs,

time: 38.7 us -> 36.4 us (0.941)
  the two profiles are of different devices: /device:TPU:0 before, /device:TPU:1 now
where the time goes in v4:
time: 36.4 us; the launch traced here: 36.1 us
  starting transfers between devices  12.7 us (35%)
  Pallas kernels  10.9 us (30%)
  waiting for transfers between devices  8.16 us (22%)
  local copies, waits for them, and re-layouts  3.55 us (10%)
  between operations  0.79 us (2%)
    pallas_call x5, Pallas kernels, absorb(): pl.pallas_call(body, out_shape=shapes, in_specs=[SMEM] + [VMEM] * (len(op...  8.62 us
    ppermute x1, starting transfers between devices, on_device(): theirs = lax.ppermute(theirs_sent, 'narrow', swap)  5.9 us
    ppermute x3, starting transfers between devices, send(): return lax.ppermute(x, 'narrow', pairs)  5.15 us
    unnamed x18, local copies, waits for them, and re-layouts  3.55 us
    ppermute x1, waiting for transfers between devices, on_device(): other_queries = lax.ppermute(queries_out, 'narrow', swap)  3.18 us
    ppermute x3, waiting for transfers between devices, send(): return lax.ppermute(x, 'narrow', pairs)  2.68 us
    ppermute x1, waiting for transfers between devices, on_device(): theirs = lax.ppermute(theirs_sent, 'narrow', swap)  2.3 us
    ppermute x2, starting transfers between devices, send(): return lax.ppermute(x, ('wide', 'narrow'), pairs)  1.47 us
  transfers between devices with their start and end apart: 7, of which 3 were waited for; matrix products, arithmetic and copies ran while one was open for 0% of the time, Pallas kernels for 24%

profile of v4, /device:TPU:1, one launch (start us, length us, event | category | flops | bytes accessed | tf_op | source)
XLA Modules:
  0.0 36.1 jit_solution(10094447452078861724)
XLA Ops:
  0.0 3.1 %collective-permute-start.3 = (bf16[512,512]{1,0:T(8,128)(2,1)}, bf16[512,512]{1,0:T(8,128)(2,1)S(1)}, u32[]{:S(2)}, u32[]{:S(2)}) collective-permute-start(bf16[512,512]{1,0:T(8,128)(2,1)} %bitcast.10), channel_id=1, source_target_pairs={{1,0},{3,1},{0,2},{2,3},{5,4},{7,5},{4,6},{6,7},{9,8},{11,9},{8,10... | collective-permute-start | bytes 1572872 | tf_op jit(solution)/shard_map/ppermute | solution.py:191
  3.1 1.1 %copy-done.5 = bf16[1,512,512]{2,1,0:T(8,128)(2,1)S(1)} copy-done((bf16[1,512,512]{2,1,0:T(8,128)(2,1)S(1)}, bf16[1,512,512]{2,1,0:T(8,128)(2,1)}, u32[]{:S(2)}) %copy-start.5) | copy-done | bytes 524312
  4.2 0.7 %pack.1 = (bf16[272,512]{1,0:T(8,128)(2,1)S(1)}, bf16[256,512]{1,0:T(8,128)(2,1)S(1)}) custom-call(bf16[512,512]{1,0:T(8,128)(2,1)S(1)} %bitcast.11, s32[1,512]{1,0:T(1,128)} %labels_ref.1), custom_call_target="tpu_custom_call" | custom-call | tf_op jit(solution)/shard_map/pack/pallas_call | solution.py:200
  5.0 1.3 %collective-permute-start.4 = (s32[1,512]{1,0:T(1,128)}, s32[1,512]{1,0:T(1,128)S(1)}, u32[]{:S(2)}, u32[]{:S(2)}) collective-permute-start(s32[1,512]{1,0:T(1,128)} %labels_ref.1), channel_id=1, source_target_pairs={{1,0},{3,1},{0,2},{2,3},{5,4},{7,5},{4,6},{6,7},{9,8},{11,9},{8,10... | collective-permute-start | bytes 6152 | tf_op jit(solution)/shard_map/ppermute | solution.py:191
  6.3 0.2 collective-permute-start.2
  6.5 0.7 %collective-permute-start = (bf16[272,512]{1,0:T(8,128)(2,1)S(1)}, bf16[272,512]{1,0:T(8,128)(2,1)S(1)}, u32[]{:S(2)}, u32[]{:S(2)}) collective-permute-start(bf16[272,512]{1,0:T(8,128)(2,1)S(1)} %get-tuple-element.27.refs_1_.refs_3_.refs_4_.refs_8_), channel_id=1, source_target_pairs={{2,1},{1,2},{6,5},{5,6},{10,9},{9,10},{14,13},{13,14},{18,17},{17,... | collective-permute-start | bytes 835592 | tf_op jit(solution)/shard_map/ppermute | solution.py:191
  7.2 0.0 copy-start
  7.2 1.2 %copy-done = bf16[512,1024]{1,0:T(8,128)(2,1)S(1)} copy-done((bf16[512,1024]{1,0:T(8,128)(2,1)S(1)}, bf16[512,1024]{1,0:T(8,128)(2,1)}, u32[]{:S(2)}) %copy-start) | copy-done | bytes 1048600
  8.4 1.2 %copy-done.2 = bf16[512,1024]{1,0:T(8,128)(2,1)S(1)} copy-done((bf16[512,1024]{1,0:T(8,128)(2,1)S(1)}, bf16[512,1024]{1,0:T(8,128)(2,1)}, u32[]{:S(2)}) %copy-start.2) | copy-done | bytes 1048600
  9.6 0.3 project_gates.1.gates_ref
  9.9 0.0 copy-start.8
  10.0 0.8 %collective-permute-start.1 = (bf16[256,512]{1,0:T(8,128)(2,1)S(1)}, bf16[256,512]{1,0:T(8,128)(2,1)S(1)}, u32[]{:S(2)}, u32[]{:S(2)}) collective-permute-start(bf16[256,512]{1,0:T(8,128)(2,1)S(1)} %get-tuple-element.33.refs_2_.refs_6_), channel_id=1, source_target_pairs={{2,1},{1,2},{10,9},{9,10},{18,17},{17,18},{26,25},{25,26}} | collective-permute-start | bytes 786440 | tf_op jit(solution)/shard_map/ppermute | solution.py:194
  11.4 2.7 %collective-permute-done.4.refs_1_ = s32[1,512]{1,0:T(1,128)S(1)} collective-permute-done((s32[1,512]{1,0:T(1,128)}, s32[1,512]{1,0:T(1,128)S(1)}, u32[]{:S(2)}, u32[]{:S(2)}) %collective-permute-start.4) | collective-permute-done | bytes 2080 | tf_op jit(solution)/shard_map/ppermute | solution.py:191
  14.1 2.4 %own_far1.1 = (f32[256,512]{1,0:T(8,128)S(1)}, bf16[512,512]{1,0:T(8,128)(2,1)S(1)}, bf16[512,512]{1,0:T(8,128)(2,1)S(1)}, f32[8,512]{1,0:T(8,128)S(1)}) custom-call(s32[1]{0:T(128)S(6)} %copy.10.length_ref, bf16[512,512]{1,0:T(8,128)(2,1)S(1)} %collective-permute-done.3.refs_0_, s32[1,512]{1,0:T(1,128)S(1)} %collective-permute-done.4.refs_1_, ...), custom_call_target="tpu_custom_call" | custom-call | flops 4294967296 | bytes 2887684 | tf_op jit(solution)/shard_map/own_far1/pallas_call | solution.py:274
  16.5 3.2 %collective-permute-done.2.refs_3_ = bf16[256,512]{1,0:T(8,128)(2,1)S(1)} collective-permute-done((bf16[256,512]{1,0:T(8,128)(2,1)S(1)}, bf16[256,512]{1,0:T(8,128)(2,1)S(1)}, u32[]{:S(2)}, u32[]{:S(2)}) %collective-permute-start.2) | collective-permute-done | bytes 262176 | tf_op jit(solution)/shard_map/ppermute | solution.py:215
  19.6 0.7 %collective-permute-start.5 = (bf16[256,512]{1,0:T(8,128)(2,1)S(1)}, bf16[256,512]{1,0:T(8,128)(2,1)S(1)}, u32[]{:S(2)}, u32[]{:S(2)}) collective-permute-start(bf16[256,512]{1,0:T(8,128)(2,1)S(1)} %get-tuple-element.33.refs_2_.refs_6_), channel_id=1, source_target_pairs={{6,5},{5,6},{14,13},{13,14},{22,21},{21,22},{30,29},{29,30}} | collective-permute-start | bytes 786440 | tf_op jit(solution)/shard_map/ppermute | solution.py:194
  20.3 1.6 %theirs_far1.1 = (f32[256,512]{1,0:T(8,128)S(1)}, bf16[256,512]{1,0:T(8,128)(2,1)S(1)}) custom-call(s32[1]{0:T(128)S(6)} %copy.10.length_ref, bf16[512,512]{1,0:T(8,128)(2,1)S(1)} %get-tuple-element.34.refs_0_, bf16[512,512]{1,0:T(8,128)(2,1)S(1)} %get-tuple-element.35.refs_1_, f32[8,512]{1,0:T(8,128)S(1)} %get-tuple-element.36.refs_2_, ...), custom_call_target="tpu_custom_call" | custom-call | flops 4294967296 | bytes 2375684 | tf_op jit(solution)/shard_map/theirs_far1/pallas_call | solution.py:274
  21.9 1.1 %theirs_near0.1.refs_8_ = f32[256,512]{1,0:T(8,128)S(1)} custom-call(s32[1]{0:T(128)S(6)} %copy.10.length_ref, bf16[272,512]{1,0:T(8,128)(2,1)S(1)} %collective-permute-done.refs_0_.refs_2_.refs_3_.refs_7_, bf16[272,512]{1,0:T(8,128)(2,1)S(1)} %get-tuple-element.27.refs_1_.refs_3_.refs_4_.refs_8_, ...), custom_call_target="tpu_custom_call" | custom-call | flops 2147483648 | bytes 2951172 | tf_op jit(solution)/shard_map/theirs_near0/pallas_call | solution.py:274
  23.1 1.2 %theirs_near1.1 = bf16[256,512]{1,0:T(8,128)(2,1)S(1)} custom-call(s32[1]{0:T(128)S(6)} %copy.10.length_ref, bf16[256,512]{1,0:T(8,128)(2,1)S(1)} %collective-permute-done.1.refs_0_.refs_4_, bf16[256,512]{1,0:T(8,128)(2,1)S(1)} %collective-permute-done.5.refs_1_.refs_5_, bf16[256,512]{1,0:T(8,128)(2,1)S(1)} %get-tuple-element.33.refs_2_.refs_6_, ...), custom_call_target="tpu_custom_call" | custom-call | flops 2147483648 | bytes 3180548 | tf_op jit(solution)/shard_map/theirs_near1/pallas_call | solution.py:274
  24.3 0.0 copy-start.6
  24.3 5.9 %collective-permute-start.6 = (bf16[256,512]{1,0:T(8,128)(2,1)S(1)}, bf16[256,512]{1,0:T(8,128)(2,1)S(1)}, u32[]{:S(2)}, u32[]{:S(2)}) collective-permute-start(bf16[256,512]{1,0:T(8,128)(2,1)S(1)} %theirs_near1.1), channel_id=1, source_target_pairs={{0,1},{1,0},{2,3},{3,2},{4,5},{5,4},{6,7},{7,6},{8,9},{9,8},{10,11... | collective-permute-start | bytes 786440 | tf_op jit(solution)/shard_map/ppermute | solution.py:312
  30.2 2.4 %own_near.1.total_ref = f32[256,512]{1,0:T(8,128)S(1)} custom-call(s32[1]{0:T(128)S(6)} %copy.10.length_ref, bf16[272,512]{1,0:T(8,128)(2,1)S(1)} %collective-permute-done.refs_0_.refs_2_.refs_3_.refs_7_, bf16[272,512]{1,0:T(8,128)(2,1)S(1)} %get-tuple-element.27.refs_1_.refs_3_.refs_4_.refs_8_, ...), custom_call_target="tpu_custom_call" | custom-call | flops 4294967296 | bytes 5343236 | tf_op jit(solution)/shard_map/own_near/pallas_call | solution.py:274
  32.6 2.3 %collective-permute-done.6.other_ref = bf16[256,512]{1,0:T(8,128)(2,1)S(1)} collective-permute-done((bf16[256,512]{1,0:T(8,128)(2,1)S(1)}, bf16[256,512]{1,0:T(8,128)(2,1)S(1)}, u32[]{:S(2)}, u32[]{:S(2)}) %collective-permute-start.6) | collective-permute-done | bytes 262176 | tf_op jit(solution)/shard_map/ppermute | solution.py:312
  34.9 1.2 %finish.1 = bf16[256,512]{1,0:T(8,128)(2,1)} custom-call(f32[256,512]{1,0:T(8,128)S(1)} %own_near.1.total_ref, bf16[256,512]{1,0:T(8,128)(2,1)S(1)} %collective-permute-done.6.other_ref, f32[256,512]{1,0:T(8,128)S(1)} %project_gates.1.gates_ref, f32[1,512]{1,0:T(1,128)S(1)} %bitcast.12, bf16[512,512]{1,0:T(8,128)(2,1)S(1)} %copy-done.6, ...), custom_call_target="tpu_custom_call" | custom-call | flops 134217728 | bytes 1048576 | tf_op jit(solution)/shard_map/finish/pallas_call | solution.py:314
  (16 shorter events, 0.0 us)
Async XLA Ops:
  0.0 6.3 %copy-start.4 = (bf16[1,256,512]{2,1,0:T(8,128)(2,1)S(1)}, bf16[1,256,512]{2,1,0:T(8,128)(2,1)}, u32[]{:S(2)}) copy-start(bf16[1,256,512]{2,1,0:T(8,128)(2,1)} %param.10) | copy-start | bytes 786436
  0.0 14.1 %collective-permute-start.3 = (bf16[512,512]{1,0:T(8,128)(2,1)}, bf16[512,512]{1,0:T(8,128)(2,1)S(1)}, u32[]{:S(2)}, u32[]{:S(2)}) collective-permute-start(bf16[512,512]{1,0:T(8,128)(2,1)} %bitcast.10), channel_id=1, source_target_pairs={{1,0},{3,1},{0,2},{2,3},{5,4},{7,5},{4,6},{6,7},{9,8},{11,9},{8,10... | collective-permute-start | bytes 1572872 | tf_op jit(solution)/shard_map/ppermute | solution.py:191
  3.1 1.1 %copy-start.5 = (bf16[1,512,512]{2,1,0:T(8,128)(2,1)S(1)}, bf16[1,512,512]{2,1,0:T(8,128)(2,1)}, u32[]{:S(2)}) copy-start(bf16[1,512,512]{2,1,0:T(8,128)(2,1)} %param.9) | copy-start | bytes 1572868
  5.0 9.1 %collective-permute-start.4 = (s32[1,512]{1,0:T(1,128)}, s32[1,512]{1,0:T(1,128)S(1)}, u32[]{:S(2)}, u32[]{:S(2)}) collective-permute-start(s32[1,512]{1,0:T(1,128)} %labels_ref.1), channel_id=1, source_target_pairs={{1,0},{3,1},{0,2},{2,3},{5,4},{7,5},{4,6},{6,7},{9,8},{11,9},{8,10... | collective-permute-start | bytes 6152 | tf_op jit(solution)/shard_map/ppermute | solution.py:191
  6.3 13.3 %collective-permute-start.2 = (bf16[256,512]{1,0:T(8,128)(2,1)S(1)}, bf16[256,512]{1,0:T(8,128)(2,1)S(1)}, u32[]{:S(2)}, u32[]{:S(2)}) collective-permute-start(bf16[256,512]{1,0:T(8,128)(2,1)S(1)} %bitcast.5), channel_id=1, source_target_pairs={{0,1},{1,0},{2,3},{3,2},{4,5},{5,4},{6,7},{7,6},{8,9},{9,8},{10,11... | collective-permute-start | bytes 786440 | tf_op jit(solution)/shard_map/ppermute | solution.py:215
  6.5 15.4 %collective-permute-start = (bf16[272,512]{1,0:T(8,128)(2,1)S(1)}, bf16[272,512]{1,0:T(8,128)(2,1)S(1)}, u32[]{:S(2)}, u32[]{:S(2)}) collective-permute-start(bf16[272,512]{1,0:T(8,128)(2,1)S(1)} %get-tuple-element.27.refs_1_.refs_3_.refs_4_.refs_8_), channel_id=1, source_target_pairs={{2,1},{1,2},{6,5},{5,6},{10,9},{9,10},{14,13},{13,14},{18,17},{17,... | collective-permute-start | bytes 835592 | tf_op jit(solution)/shard_map/ppermute | solution.py:191
  7.2 1.2 %copy-start = (bf16[512,1024]{1,0:T(8,128)(2,1)S(1)}, bf16[512,1024]{1,0:T(8,128)(2,1)}, u32[]{:S(2)}) copy-start(bf16[512,1024]{1,0:T(8,128)(2,1)} %refs_9_.1) | copy-start | bytes 3145732
  8.4 1.2 %copy-start.2 = (bf16[512,1024]{1,0:T(8,128)(2,1)S(1)}, bf16[512,1024]{1,0:T(8,128)(2,1)}, u32[]{:S(2)}) copy-start(bf16[512,1024]{1,0:T(8,128)(2,1)} %refs_12_.1) | copy-start | bytes 3145732
  9.6 4.5 %copy-start.1 = (bf16[512,1024]{1,0:T(8,128)(2,1)S(1)}, bf16[512,1024]{1,0:T(8,128)(2,1)}, u32[]{:S(2)}) copy-start(bf16[512,1024]{1,0:T(8,128)(2,1)} %refs_9_.1) | copy-start | bytes 3145732
  9.6 4.5 %copy-start.3 = (bf16[512,1024]{1,0:T(8,128)(2,1)S(1)}, bf16[512,1024]{1,0:T(8,128)(2,1)}, u32[]{:S(2)}) copy-start(bf16[512,1024]{1,0:T(8,128)(2,1)} %refs_12_.1) | copy-start | bytes 3145732
  9.9 4.2 %copy-start.8 = (bf16[128,8]{0,1:T(8,128)(2,1)S(1)}, bf16[128,8]{0,1:T(8,128)(2,1)}, u32[]{:S(2)}) copy-start(bf16[128,8]{0,1:T(8,128)(2,1)} %param.15) | copy-start | bytes 6148
  10.0 13.1 %collective-permute-start.1 = (bf16[256,512]{1,0:T(8,128)(2,1)S(1)}, bf16[256,512]{1,0:T(8,128)(2,1)S(1)}, u32[]{:S(2)}, u32[]{:S(2)}) collective-permute-start(bf16[256,512]{1,0:T(8,128)(2,1)S(1)} %get-tuple-element.33.refs_2_.refs_6_), channel_id=1, source_target_pairs={{2,1},{1,2},{10,9},{9,10},{18,17},{17,18},{26,25},{25,26}} | collective-permute-start | bytes 786440 | tf_op jit(solution)/shard_map/ppermute | solution.py:194
  19.6 3.5 %collective-permute-start.5 = (bf16[256,512]{1,0:T(8,128)(2,1)S(1)}, bf16[256,512]{1,0:T(8,128)(2,1)S(1)}, u32[]{:S(2)}, u32[]{:S(2)}) collective-permute-start(bf16[256,512]{1,0:T(8,128)(2,1)S(1)} %get-tuple-element.33.refs_2_.refs_6_), channel_id=1, source_target_pairs={{6,5},{5,6},{14,13},{13,14},{22,21},{21,22},{30,29},{29,30}} | collective-permute-start | bytes 786440 | tf_op jit(solution)/shard_map/ppermute | solution.py:194
  24.3 10.6 %copy-start.6 = (bf16[512,512]{1,0:T(8,128)(2,1)S(1)}, bf16[512,512]{1,0:T(8,128)(2,1)}, u32[]{:S(2)}) copy-start(bf16[512,512]{1,0:T(8,128)(2,1)} %w_ref.3) | copy-start | bytes 1572868
  24.3 10.6 %collective-permute-start.6 = (bf16[256,512]{1,0:T(8,128)(2,1)S(1)}, bf16[256,512]{1,0:T(8,128)(2,1)S(1)}, u32[]{:S(2)}, u32[]{:S(2)}) collective-permute-start(bf16[256,512]{1,0:T(8,128)(2,1)S(1)} %theirs_near1.1), channel_id=1, source_target_pairs={{0,1},{1,0},{2,3},{3,2},{4,5},{5,4},{6,7},{7,6},{8,9},{9,8},{10,11... | collective-permute-start | bytes 786440 | tf_op jit(solution)/shard_map/ppermute | solution.py:312
  30.2 4.7 %copy-start.7 = (f32[512]{0:T(512)S(1)}, f32[512]{0:T(512)}, u32[]{:S(2)}) copy-start(f32[512]{0:T(512)} %param.16) | copy-start | bytes 6148

commit v5 on v4

--- a/solution.py
+++ b/solution.py
@@ -83,16 +83,17 @@
         else:
             take_own = pick(place, chosen) == 1
             hist = refs.pop(0)[:rows]
-            if at:
-                hist = jnp.where(lax.axis_index("wide") % 2 == 0, hist, refs.pop(0)[:rows])
+            even = lax.axis_index("wide") % 2 == 0
+            hist = jnp.where(even, hist, refs.pop(0)[:rows])
             hist = jnp.where(take_own, refs.pop(0)[:rows], hist)
             width = hist.shape[1]
-            labels_ref, own_labels_ref = refs.pop(0), refs.pop(0)
+            even_labels_ref, odd_labels_ref, own_labels_ref = [refs.pop(0) for _ in range(3)]
             where = (
                 slice(shard_rows // 2 + 16 * (at // width), shard_rows // 2 + 16 * (at // width) + 16),
                 slice(at % width, at % width + rows),
             )
-            labels = jnp.where(take_own, own_labels_ref[where], labels_ref[where])
+            labels = jnp.where(even, even_labels_ref[where], odd_labels_ref[where])
+            labels = jnp.where(take_own, own_labels_ref[where], labels)
             labels = labels.astype(jnp.float32)[:1].astype(jnp.int32)
         head_size = width // heads
         per_span = SPAN // head_size
@@ -215,7 +216,7 @@
     other_queries = lax.ppermute(queries_out, "narrow", swap)
     for step in range(1, n // 2):
         received[step].append(send(labels, step))
-    head = send(head_own, 0)
+    firsts = [send(head_own, 0, 0)]
 
     gates = pl.pallas_call(
         project_gates,
@@ -228,6 +229,8 @@
     )(queries_in, w_query, w_key)
     rest_own, gates = lax.optimization_barrier((rest_own, gates))
     rests = [send(rest_own, 0, 0)]
+    head_own, received[1][0] = lax.optimization_barrier((head_own, received[1][0]))
+    firsts.append(send(head_own, 0, 1))
 
     def absorb(states, indices, total, dtype, name, raw=False, keep=False, save=False, given=None):
         step = pieces[indices[0]][0]
@@ -237,8 +240,8 @@
         for at, _ in parts:
             if step == 0:
                 chosen = [int(sources[0][z] == z) for z in range(n)]
-                operands += [*rests, rest_own] if at else [head, head_own]
-                operands += [head, head_own]
+                operands += [*rests, rest_own] if at else [*firsts, head_own]
+                operands += [*firsts, head_own]
         if given is not None:
             operands += given
         elif step:
@@ -277,7 +280,7 @@
             in_specs=[SMEM] + [VMEM] * (len(operands) - 1),
             out_specs=[VMEM] * len(shapes),
             compiler_params=PARAMS,
-            cost_estimate=cost(64 * q_rows * rows * width, *operands),
+            cost_estimate=cost((12 if name.startswith('theirs') else 64) * q_rows * rows * width, *operands),
             name=name,
         )(*operands)
 
@@ -292,8 +295,9 @@
             raw=True,
             save=True,
         )
-    rest_own, other_queries, own = lax.optimization_barrier((rest_own, other_queries, own))
+    rest_own, own = lax.optimization_barrier((rest_own, own))
     rests.append(send(rest_own, 0, 1))
+    other_queries, own = lax.optimization_barrier((other_queries, own))
     theirs, other_states = absorb(
         other_queries, [2, 3], None, jnp.float32, "theirs_far1", raw=True, keep=True, given=known[1]
     )

time: 36.4 us -> 35.7 us (0.981)
  waiting for transfers between devices: 8.16 us -> 6.27 us
  starting transfers between devices: 12.7 us -> 13.9 us
    ppermute x1, waiting for transfers between devices: 3.18 us -> 1.79 us  [on_device(): other_queries = lax.ppermute(queries_out, 'narrow', swap)]
    ppermute x2 -> x4, starting transfers between devices: 1.47 us -> 2.82 us  [send(): return lax.ppermute(x, ('wide', 'narrow'), pairs)]
    ppermute x3 -> x2, starting transfers between devices: 5.15 us -> 4.49 us  [send(): return lax.ppermute(x, 'narrow', pairs)]
    ppermute x1, starting transfers between devices: 5.9 us -> 6.41 us  [on_device(): theirs = lax.ppermute(theirs_sent, 'narrow', swap)]
    ppermute x1, waiting for transfers between devices: 2.3 us -> 1.79 us  [on_device(): theirs = lax.ppermute(theirs_sent, 'narrow', swap)]
    ppermute x3 -> x2, waiting for transfers between devices: 2.68 us -> 2.67 us  [send(): return lax.ppermute(x, 'narrow', pairs)]
  transfers between devices with their start and end apart: 7 -> 8, of which waited for: 3 -> 3; matrix products, arithmetic and copies ran while one was open for 0% -> 0% of each run, Pallas kernels for 24% -> 24%
where the time goes in v5:
time: 35.7 us; the launch traced here: 35.4 us
  starting transfers between devices  13.9 us (39%)
  Pallas kernels  10.9 us (31%)
  waiting for transfers between devices  6.27 us (18%)
  local copies, waits for them, and re-layouts  3.55 us (10%)
  between operations  0.83 us (2%)
    pallas_call x5, Pallas kernels, absorb(): pl.pallas_call(body, out_shape=shapes, in_specs=[SMEM] + [VMEM] * (len(op...  8.61 us
    ppermute x1, starting transfers between devices, on_device(): theirs = lax.ppermute(theirs_sent, 'narrow', swap)  6.41 us
    ppermute x2, starting transfers between devices, send(): return lax.ppermute(x, 'narrow', pairs)  4.49 us
    unnamed x18, local copies, waits for them, and re-layouts  3.55 us
    ppermute x4, starting transfers between devices, send(): return lax.ppermute(x, ('wide', 'narrow'), pairs)  2.82 us
    ppermute x2, waiting for transfers between devices, send(): return lax.ppermute(x, 'narrow', pairs)  2.67 us
    ppermute x1, waiting for transfers between devices, on_device(): other_queries = lax.ppermute(queries_out, 'narrow', swap)  1.79 us
    ppermute x1, waiting for transfers between devices, on_device(): theirs = lax.ppermute(theirs_sent, 'narrow', swap)  1.79 us
  transfers between devices with their start and end apart: 8, of which 3 were waited for; matrix products, arithmetic and copies ran while one was open for 0% of the time, Pallas kernels for 24%

profile of v5, /device:TPU:1, one launch (start us, length us, event | category | flops | bytes accessed | tf_op | source)
XLA Modules:
  0.0 35.4 jit_solution(14441976073715368589)
XLA Ops:
  0.0 3.1 %collective-permute-start.1 = (bf16[512,512]{1,0:T(8,128)(2,1)}, bf16[512,512]{1,0:T(8,128)(2,1)S(1)}, u32[]{:S(2)}, u32[]{:S(2)}) collective-permute-start(bf16[512,512]{1,0:T(8,128)(2,1)} %bitcast.10), channel_id=1, source_target_pairs={{1,0},{3,1},{0,2},{2,3},{5,4},{7,5},{4,6},{6,7},{9,8},{11,9},{8,10... | collective-permute-start | bytes 1572872 | tf_op jit(solution)/shard_map/ppermute | solution.py:192
  3.1 1.1 %copy-done.5 = bf16[1,512,512]{2,1,0:T(8,128)(2,1)S(1)} copy-done((bf16[1,512,512]{2,1,0:T(8,128)(2,1)S(1)}, bf16[1,512,512]{2,1,0:T(8,128)(2,1)}, u32[]{:S(2)}) %copy-start.5) | copy-done | bytes 524312
  4.2 0.7 %pack.1 = (bf16[272,512]{1,0:T(8,128)(2,1)S(1)}, bf16[256,512]{1,0:T(8,128)(2,1)S(1)}) custom-call(bf16[512,512]{1,0:T(8,128)(2,1)S(1)} %bitcast.11, s32[1,512]{1,0:T(1,128)} %labels_ref.1), custom_call_target="tpu_custom_call" | custom-call | tf_op jit(solution)/shard_map/pack/pallas_call | solution.py:201
  5.0 1.3 %collective-permute-start.4 = (s32[1,512]{1,0:T(1,128)}, s32[1,512]{1,0:T(1,128)S(1)}, u32[]{:S(2)}, u32[]{:S(2)}) collective-permute-start(s32[1,512]{1,0:T(1,128)} %labels_ref.1), channel_id=1, source_target_pairs={{1,0},{3,1},{0,2},{2,3},{5,4},{7,5},{4,6},{6,7},{9,8},{11,9},{8,10... | collective-permute-start | bytes 6152 | tf_op jit(solution)/shard_map/ppermute | solution.py:192
  6.3 0.2 collective-permute-start.6
  6.5 0.7 %collective-permute-start = (bf16[272,512]{1,0:T(8,128)(2,1)S(1)}, bf16[272,512]{1,0:T(8,128)(2,1)S(1)}, u32[]{:S(2)}, u32[]{:S(2)}) collective-permute-start(bf16[272,512]{1,0:T(8,128)(2,1)S(1)} %get-tuple-element.31.refs_2_.refs_5_.refs_11_), channel_id=1, source_target_pairs={{2,1},{1,2},{10,9},{9,10},{18,17},{17,18},{26,25},{25,26}} | collective-permute-start | bytes 835592 | tf_op jit(solution)/shard_map/ppermute | solution.py:195
  7.2 0.0 copy-start
  7.2 1.2 %copy-done = bf16[512,1024]{1,0:T(8,128)(2,1)S(1)} copy-done((bf16[512,1024]{1,0:T(8,128)(2,1)S(1)}, bf16[512,1024]{1,0:T(8,128)(2,1)}, u32[]{:S(2)}) %copy-start) | copy-done | bytes 1048600
  8.4 1.2 %copy-done.2 = bf16[512,1024]{1,0:T(8,128)(2,1)S(1)} copy-done((bf16[512,1024]{1,0:T(8,128)(2,1)S(1)}, bf16[512,1024]{1,0:T(8,128)(2,1)}, u32[]{:S(2)}) %copy-start.2) | copy-done | bytes 1048600
  9.6 0.3 project_gates.1.gates_ref
  9.9 0.0 copy-start.7
  10.0 0.8 %collective-permute-start.3 = (bf16[256,512]{1,0:T(8,128)(2,1)S(1)}, bf16[256,512]{1,0:T(8,128)(2,1)S(1)}, u32[]{:S(2)}, u32[]{:S(2)}) collective-permute-start(bf16[256,512]{1,0:T(8,128)(2,1)S(1)} %get-tuple-element.37.refs_2_.refs_8_), channel_id=1, source_target_pairs={{2,1},{1,2},{10,9},{9,10},{18,17},{17,18},{26,25},{25,26}} | collective-permute-start | bytes 786440 | tf_op jit(solution)/shard_map/ppermute | solution.py:195
  11.4 2.7 %collective-permute-done.1.refs_0_ = bf16[512,512]{1,0:T(8,128)(2,1)S(1)} collective-permute-done((bf16[512,512]{1,0:T(8,128)(2,1)}, bf16[512,512]{1,0:T(8,128)(2,1)S(1)}, u32[]{:S(2)}, u32[]{:S(2)}) %collective-permute-start.1) | collective-permute-done | bytes 524320 | tf_op jit(solution)/shard_map/ppermute | solution.py:192
  14.1 0.7 %collective-permute-start.2 = (bf16[272,512]{1,0:T(8,128)(2,1)S(1)}, bf16[272,512]{1,0:T(8,128)(2,1)S(1)}, u32[]{:S(2)}, u32[]{:S(2)}) collective-permute-start(bf16[272,512]{1,0:T(8,128)(2,1)S(1)} %get-tuple-element.31.refs_2_.refs_5_.refs_11_), channel_id=1, source_target_pairs={{6,5},{5,6},{14,13},{13,14},{22,21},{21,22},{30,29},{29,30}} | collective-permute-start | bytes 835592 | tf_op jit(solution)/shard_map/ppermute | solution.py:195
  14.8 2.4 %own_far1.1 = (f32[256,512]{1,0:T(8,128)S(1)}, bf16[512,512]{1,0:T(8,128)(2,1)S(1)}, bf16[512,512]{1,0:T(8,128)(2,1)S(1)}, f32[8,512]{1,0:T(8,128)S(1)}) custom-call(s32[1]{0:T(128)S(6)} %copy.10.length_ref, bf16[512,512]{1,0:T(8,128)(2,1)S(1)} %collective-permute-done.1.refs_0_, s32[1,512]{1,0:T(1,128)S(1)} %collective-permute-done.4.refs_1_, ...), custom_call_target="tpu_custom_call" | custom-call | flops 4294967296 | bytes 2887684 | tf_op jit(solution)/shard_map/own_far1/pallas_call | solution.py:277
  17.2 0.7 %collective-permute-start.5 = (bf16[256,512]{1,0:T(8,128)(2,1)S(1)}, bf16[256,512]{1,0:T(8,128)(2,1)S(1)}, u32[]{:S(2)}, u32[]{:S(2)}) collective-permute-start(bf16[256,512]{1,0:T(8,128)(2,1)S(1)} %get-tuple-element.37.refs_2_.refs_8_), channel_id=1, source_target_pairs={{6,5},{5,6},{14,13},{13,14},{22,21},{21,22},{30,29},{29,30}} | collective-permute-start | bytes 786440 | tf_op jit(solution)/shard_map/ppermute | solution.py:195
  17.9 1.8 %collective-permute-done.6.refs_3_ = bf16[256,512]{1,0:T(8,128)(2,1)S(1)} collective-permute-done((bf16[256,512]{1,0:T(8,128)(2,1)S(1)}, bf16[256,512]{1,0:T(8,128)(2,1)S(1)}, u32[]{:S(2)}, u32[]{:S(2)}) %collective-permute-start.6) | collective-permute-done | bytes 262176 | tf_op jit(solution)/shard_map/ppermute | solution.py:216
  19.6 1.6 %theirs_far1.1 = (f32[256,512]{1,0:T(8,128)S(1)}, bf16[256,512]{1,0:T(8,128)(2,1)S(1)}) custom-call(s32[1]{0:T(128)S(6)} %copy.10.length_ref, bf16[512,512]{1,0:T(8,128)(2,1)S(1)} %get-tuple-element.38.refs_0_, bf16[512,512]{1,0:T(8,128)(2,1)S(1)} %get-tuple-element.39.refs_1_, f32[8,512]{1,0:T(8,128)S(1)} %get-tuple-element.40.refs_2_, ...), custom_call_target="tpu_custom_call" | custom-call | flops 805306368 | bytes 2375684 | tf_op jit(solution)/shard_map/theirs_far1/pallas_call | solution.py:277
  21.3 1.1 %theirs_near0.1.refs_9_ = f32[256,512]{1,0:T(8,128)S(1)} custom-call(s32[1]{0:T(128)S(6)} %copy.10.length_ref, bf16[272,512]{1,0:T(8,128)(2,1)S(1)} %collective-permute-done.refs_0_.refs_3_.refs_9_, bf16[272,512]{1,0:T(8,128)(2,1)S(1)} %collective-permute-done.2.refs_1_.refs_4_.refs_10_, bf16[272,512]{1,0:T(8,128)(2,1)S(1)} %get-tuple-element.31.refs_2_.refs_5_.refs_11_, ...), custom_call_target="tpu_custom_call" | custom-call | flops 402653184 | bytes 3508228 | tf_op jit(solution)/shard_map/theirs_near0/pallas_call | solution.py:277
  22.4 1.2 %theirs_near1.1 = bf16[256,512]{1,0:T(8,128)(2,1)S(1)} custom-call(s32[1]{0:T(128)S(6)} %copy.10.length_ref, bf16[256,512]{1,0:T(8,128)(2,1)S(1)} %collective-permute-done.3.refs_0_.refs_6_, bf16[256,512]{1,0:T(8,128)(2,1)S(1)} %collective-permute-done.5.refs_1_.refs_7_, bf16[256,512]{1,0:T(8,128)(2,1)S(1)} %get-tuple-element.37.refs_2_.refs_8_, ...), custom_call_target="tpu_custom_call" | custom-call | flops 402653184 | bytes 3459076 | tf_op jit(solution)/shard_map/theirs_near1/pallas_call | solution.py:277
  23.6 6.4 %collective-permute-start.7 = (bf16[256,512]{1,0:T(8,128)(2,1)S(1)}, bf16[256,512]{1,0:T(8,128)(2,1)S(1)}, u32[]{:S(2)}, u32[]{:S(2)}) collective-permute-start(bf16[256,512]{1,0:T(8,128)(2,1)S(1)} %theirs_near1.1), channel_id=1, source_target_pairs={{0,1},{1,0},{2,3},{3,2},{4,5},{5,4},{6,7},{7,6},{8,9},{9,8},{10,11... | collective-permute-start | bytes 786440 | tf_op jit(solution)/shard_map/ppermute | solution.py:316
  30.0 2.4 %own_near.1.total_ref = f32[256,512]{1,0:T(8,128)S(1)} custom-call(s32[1]{0:T(128)S(6)} %copy.10.length_ref, bf16[272,512]{1,0:T(8,128)(2,1)S(1)} %collective-permute-done.refs_0_.refs_3_.refs_9_, bf16[272,512]{1,0:T(8,128)(2,1)S(1)} %collective-permute-done.2.refs_1_.refs_4_.refs_10_, bf16[272,512]{1,0:T(8,128)(2,1)S(1)} %get-tuple-element.31.refs_2_.refs_5_.refs_11_, ...), custom_call_target="tpu_custom_call" | custom-call | flops 4294967296 | bytes 6178820 | tf_op jit(solution)/shard_map/own_near/pallas_call | solution.py:277
  32.4 1.8 %collective-permute-done.7.other_ref = bf16[256,512]{1,0:T(8,128)(2,1)S(1)} collective-permute-done((bf16[256,512]{1,0:T(8,128)(2,1)S(1)}, bf16[256,512]{1,0:T(8,128)(2,1)S(1)}, u32[]{:S(2)}, u32[]{:S(2)}) %collective-permute-start.7) | collective-permute-done | bytes 262176 | tf_op jit(solution)/shard_map/ppermute | solution.py:316
  34.2 1.2 %finish.1 = bf16[256,512]{1,0:T(8,128)(2,1)} custom-call(f32[256,512]{1,0:T(8,128)S(1)} %own_near.1.total_ref, bf16[256,512]{1,0:T(8,128)(2,1)S(1)} %collective-permute-done.7.other_ref, f32[256,512]{1,0:T(8,128)S(1)} %project_gates.1.gates_ref, f32[1,512]{1,0:T(1,128)S(1)} %bitcast.16, bf16[512,512]{1,0:T(8,128)(2,1)S(1)} %copy-done.6, ...), custom_call_target="tpu_custom_call" | custom-call | flops 134217728 | bytes 1048576 | tf_op jit(solution)/shard_map/finish/pallas_call | solution.py:318
  (18 shorter events, 0.0 us)
Async XLA Ops:
  0.0 6.3 %copy-start.4 = (bf16[1,256,512]{2,1,0:T(8,128)(2,1)S(1)}, bf16[1,256,512]{2,1,0:T(8,128)(2,1)}, u32[]{:S(2)}) copy-start(bf16[1,256,512]{2,1,0:T(8,128)(2,1)} %param.10) | copy-start | bytes 786436
  0.0 14.1 %collective-permute-start.1 = (bf16[512,512]{1,0:T(8,128)(2,1)}, bf16[512,512]{1,0:T(8,128)(2,1)S(1)}, u32[]{:S(2)}, u32[]{:S(2)}) collective-permute-start(bf16[512,512]{1,0:T(8,128)(2,1)} %bitcast.10), channel_id=1, source_target_pairs={{1,0},{3,1},{0,2},{2,3},{5,4},{7,5},{4,6},{6,7},{9,8},{11,9},{8,10... | collective-permute-start | bytes 1572872 | tf_op jit(solution)/shard_map/ppermute | solution.py:192
  3.1 1.1 %copy-start.5 = (bf16[1,512,512]{2,1,0:T(8,128)(2,1)S(1)}, bf16[1,512,512]{2,1,0:T(8,128)(2,1)}, u32[]{:S(2)}) copy-start(bf16[1,512,512]{2,1,0:T(8,128)(2,1)} %param.9) | copy-start | bytes 1572868
  5.0 9.8 %collective-permute-start.4 = (s32[1,512]{1,0:T(1,128)}, s32[1,512]{1,0:T(1,128)S(1)}, u32[]{:S(2)}, u32[]{:S(2)}) collective-permute-start(s32[1,512]{1,0:T(1,128)} %labels_ref.1), channel_id=1, source_target_pairs={{1,0},{3,1},{0,2},{2,3},{5,4},{7,5},{4,6},{6,7},{9,8},{11,9},{8,10... | collective-permute-start | bytes 6152 | tf_op jit(solution)/shard_map/ppermute | solution.py:192
  6.3 13.3 %collective-permute-start.6 = (bf16[256,512]{1,0:T(8,128)(2,1)S(1)}, bf16[256,512]{1,0:T(8,128)(2,1)S(1)}, u32[]{:S(2)}, u32[]{:S(2)}) collective-permute-start(bf16[256,512]{1,0:T(8,128)(2,1)S(1)} %bitcast.5), channel_id=1, source_target_pairs={{0,1},{1,0},{2,3},{3,2},{4,5},{5,4},{6,7},{7,6},{8,9},{9,8},{10,11... | collective-permute-start | bytes 786440 | tf_op jit(solution)/shard_map/ppermute | solution.py:216
  6.5 14.8 %collective-permute-start = (bf16[272,512]{1,0:T(8,128)(2,1)S(1)}, bf16[272,512]{1,0:T(8,128)(2,1)S(1)}, u32[]{:S(2)}, u32[]{:S(2)}) collective-permute-start(bf16[272,512]{1,0:T(8,128)(2,1)S(1)} %get-tuple-element.31.refs_2_.refs_5_.refs_11_), channel_id=1, source_target_pairs={{2,1},{1,2},{10,9},{9,10},{18,17},{17,18},{26,25},{25,26}} | collective-permute-start | bytes 835592 | tf_op jit(solution)/shard_map/ppermute | solution.py:195
  7.2 1.2 %copy-start = (bf16[512,1024]{1,0:T(8,128)(2,1)S(1)}, bf16[512,1024]{1,0:T(8,128)(2,1)}, u32[]{:S(2)}) copy-start(bf16[512,1024]{1,0:T(8,128)(2,1)} %refs_12_.1) | copy-start | bytes 3145732
  8.4 1.2 %copy-start.2 = (bf16[512,1024]{1,0:T(8,128)(2,1)S(1)}, bf16[512,1024]{1,0:T(8,128)(2,1)}, u32[]{:S(2)}) copy-start(bf16[512,1024]{1,0:T(8,128)(2,1)} %refs_15_.1) | copy-start | bytes 3145732
  9.6 5.2 %copy-start.1 = (bf16[512,1024]{1,0:T(8,128)(2,1)S(1)}, bf16[512,1024]{1,0:T(8,128)(2,1)}, u32[]{:S(2)}) copy-start(bf16[512,1024]{1,0:T(8,128)(2,1)} %refs_12_.1) | copy-start | bytes 3145732
  9.6 5.2 %copy-start.3 = (bf16[512,1024]{1,0:T(8,128)(2,1)S(1)}, bf16[512,1024]{1,0:T(8,128)(2,1)}, u32[]{:S(2)}) copy-start(bf16[512,1024]{1,0:T(8,128)(2,1)} %refs_15_.1) | copy-start | bytes 3145732
  9.9 4.9 %copy-start.7 = (bf16[128,8]{0,1:T(8,128)(2,1)S(1)}, bf16[128,8]{0,1:T(8,128)(2,1)}, u32[]{:S(2)}) copy-start(bf16[128,8]{0,1:T(8,128)(2,1)} %param.15) | copy-start | bytes 6148
  10.0 12.5 %collective-permute-start.3 = (bf16[256,512]{1,0:T(8,128)(2,1)S(1)}, bf16[256,512]{1,0:T(8,128)(2,1)S(1)}, u32[]{:S(2)}, u32[]{:S(2)}) collective-permute-start(bf16[256,512]{1,0:T(8,128)(2,1)S(1)} %get-tuple-element.37.refs_2_.refs_8_), channel_id=1, source_target_pairs={{2,1},{1,2},{10,9},{9,10},{18,17},{17,18},{26,25},{25,26}} | collective-permute-start | bytes 786440 | tf_op jit(solution)/shard_map/ppermute | solution.py:195
  14.1 7.2 %collective-permute-start.2 = (bf16[272,512]{1,0:T(8,128)(2,1)S(1)}, bf16[272,512]{1,0:T(8,128)(2,1)S(1)}, u32[]{:S(2)}, u32[]{:S(2)}) collective-permute-start(bf16[272,512]{1,0:T(8,128)(2,1)S(1)} %get-tuple-element.31.refs_2_.refs_5_.refs_11_), channel_id=1, source_target_pairs={{6,5},{5,6},{14,13},{13,14},{22,21},{21,22},{30,29},{29,30}} | collective-permute-start | bytes 835592 | tf_op jit(solution)/shard_map/ppermute | solution.py:195
  17.2 5.3 %collective-permute-start.5 = (bf16[256,512]{1,0:T(8,128)(2,1)S(1)}, bf16[256,512]{1,0:T(8,128)(2,1)S(1)}, u32[]{:S(2)}, u32[]{:S(2)}) collective-permute-start(bf16[256,512]{1,0:T(8,128)(2,1)S(1)} %get-tuple-element.37.refs_2_.refs_8_), channel_id=1, source_target_pairs={{6,5},{5,6},{14,13},{13,14},{22,21},{21,22},{30,29},{29,30}} | collective-permute-start | bytes 786440 | tf_op jit(solution)/shard_map/ppermute | solution.py:195
  23.6 10.6 %copy-start.6 = (bf16[512,512]{1,0:T(8,128)(2,1)S(1)}, bf16[512,512]{1,0:T(8,128)(2,1)}, u32[]{:S(2)}) copy-start(bf16[512,512]{1,0:T(8,128)(2,1)} %w_ref.3) | copy-start | bytes 1572868
  23.6 10.6 %collective-permute-start.7 = (bf16[256,512]{1,0:T(8,128)(2,1)S(1)}, bf16[256,512]{1,0:T(8,128)(2,1)S(1)}, u32[]{:S(2)}, u32[]{:S(2)}) collective-permute-start(bf16[256,512]{1,0:T(8,128)(2,1)S(1)} %theirs_near1.1), channel_id=1, source_target_pairs={{0,1},{1,0},{2,3},{3,2},{4,5},{5,4},{6,7},{7,6},{8,9},{9,8},{10,11... | collective-permute-start | bytes 786440 | tf_op jit(solution)/shard_map/ppermute | solution.py:316
  30.0 4.2 %copy-start.8 = (f32[512]{0:T(512)S(1)}, f32[512]{0:T(512)}, u32[]{:S(2)}) copy-start(f32[512]{0:T(512)} %param.16) | copy-start | bytes 6148

commit v6 on v5

--- a/solution.py
+++ b/solution.py
@@ -229,8 +229,11 @@
     )(queries_in, w_query, w_key)
     rest_own, gates = lax.optimization_barrier((rest_own, gates))
     rests = [send(rest_own, 0, 0)]
-    head_own, received[1][0] = lax.optimization_barrier((head_own, received[1][0]))
+    head_own, rest_own, received[1][0] = lax.optimization_barrier(
+        (head_own, rest_own, received[1][0])
+    )
     firsts.append(send(head_own, 0, 1))
+    rests.append(send(rest_own, 0, 1))
 
     def absorb(states, indices, total, dtype, name, raw=False, keep=False, save=False, given=None):
         step = pieces[indices[0]][0]
@@ -295,8 +298,6 @@
             raw=True,
             save=True,
         )
-    rest_own, own = lax.optimization_barrier((rest_own, own))
-    rests.append(send(rest_own, 0, 1))
     other_queries, own = lax.optimization_barrier((other_queries, own))
     theirs, other_states = absorb(
         other_queries, [2, 3], None, jnp.float32, "theirs_far1", raw=True, keep=True, given=known[1]

time: 35.7 us -> 35.7 us (level)
  no operation moved by 1% of the time
where the time goes in v6:
time: 35.7 us; the launch traced here: 35.4 us
  starting transfers between devices  13.6 us (38%)
  Pallas kernels  10.9 us (31%)
  waiting for transfers between devices  6.55 us (18%)
  local copies, waits for them, and re-layouts  3.55 us (10%)
  between operations  0.83 us (2%)
    pallas_call x5, Pallas kernels, absorb(): pl.pallas_call(body, out_shape=shapes, in_specs=[SMEM] + [VMEM] * (len(op...  8.61 us
    ppermute x1, starting transfers between devices, on_device(): theirs = lax.ppermute(theirs_sent, 'narrow', swap)  6.13 us
    ppermute x2, starting transfers between devices, send(): return lax.ppermute(x, 'narrow', pairs)  4.49 us
    unnamed x18, local copies, waits for them, and re-layouts  3.55 us
    ppermute x4, starting transfers between devices, send(): return lax.ppermute(x, ('wide', 'narrow'), pairs)  2.82 us
    ppermute x2, waiting for transfers between devices, send(): return lax.ppermute(x, 'narrow', pairs)  2.67 us
    ppermute x1, waiting for transfers between devices, on_device(): theirs = lax.ppermute(theirs_sent, 'narrow', swap)  2.07 us
    ppermute x1, waiting for transfers between devices, on_device(): other_queries = lax.ppermute(queries_out, 'narrow', swap)  1.79 us
  transfers between devices with their start and end apart: 8, of which 3 were waited for; matrix products, arithmetic and copies ran while one was open for 0% of the time, Pallas kernels for 24%

profile of v6, /device:TPU:1, one launch (start us, length us, event | category | flops | bytes accessed | tf_op | source)
XLA Modules:
  0.0 35.4 jit_solution(12804722058354954837)
XLA Ops:
  0.0 3.1 %collective-permute-start.1 = (bf16[512,512]{1,0:T(8,128)(2,1)}, bf16[512,512]{1,0:T(8,128)(2,1)S(1)}, u32[]{:S(2)}, u32[]{:S(2)}) collective-permute-start(bf16[512,512]{1,0:T(8,128)(2,1)} %bitcast.10), channel_id=1, source_target_pairs={{1,0},{3,1},{0,2},{2,3},{5,4},{7,5},{4,6},{6,7},{9,8},{11,9},{8,10... | collective-permute-start | bytes 1572872 | tf_op jit(solution)/shard_map/ppermute | solution.py:192
  3.1 1.1 %copy-done.5 = bf16[1,512,512]{2,1,0:T(8,128)(2,1)S(1)} copy-done((bf16[1,512,512]{2,1,0:T(8,128)(2,1)S(1)}, bf16[1,512,512]{2,1,0:T(8,128)(2,1)}, u32[]{:S(2)}) %copy-start.5) | copy-done | bytes 524312
  4.2 0.7 %pack.1 = (bf16[272,512]{1,0:T(8,128)(2,1)S(1)}, bf16[256,512]{1,0:T(8,128)(2,1)S(1)}) custom-call(bf16[512,512]{1,0:T(8,128)(2,1)S(1)} %bitcast.11, s32[1,512]{1,0:T(1,128)} %labels_ref.1), custom_call_target="tpu_custom_call" | custom-call | tf_op jit(solution)/shard_map/pack/pallas_call | solution.py:201
  5.0 1.3 %collective-permute-start.5 = (s32[1,512]{1,0:T(1,128)}, s32[1,512]{1,0:T(1,128)S(1)}, u32[]{:S(2)}, u32[]{:S(2)}) collective-permute-start(s32[1,512]{1,0:T(1,128)} %labels_ref.1), channel_id=1, source_target_pairs={{1,0},{3,1},{0,2},{2,3},{5,4},{7,5},{4,6},{6,7},{9,8},{11,9},{8,10... | collective-permute-start | bytes 6152 | tf_op jit(solution)/shard_map/ppermute | solution.py:192
  6.3 0.2 collective-permute-start.6
  6.5 0.7 %collective-permute-start = (bf16[272,512]{1,0:T(8,128)(2,1)S(1)}, bf16[272,512]{1,0:T(8,128)(2,1)S(1)}, u32[]{:S(2)}, u32[]{:S(2)}) collective-permute-start(bf16[272,512]{1,0:T(8,128)(2,1)S(1)} %get-tuple-element.32.refs_2_.refs_5_.refs_11_), channel_id=1, source_target_pairs={{2,1},{1,2},{10,9},{9,10},{18,17},{17,18},{26,25},{25,26}} | collective-permute-start | bytes 835592 | tf_op jit(solution)/shard_map/ppermute | solution.py:195
  7.2 1.2 %copy-done = bf16[512,1024]{1,0:T(8,128)(2,1)S(1)} copy-done((bf16[512,1024]{1,0:T(8,128)(2,1)S(1)}, bf16[512,1024]{1,0:T(8,128)(2,1)}, u32[]{:S(2)}) %copy-start) | copy-done | bytes 1048600
  8.4 1.2 %copy-done.2 = bf16[512,1024]{1,0:T(8,128)(2,1)S(1)} copy-done((bf16[512,1024]{1,0:T(8,128)(2,1)S(1)}, bf16[512,1024]{1,0:T(8,128)(2,1)}, u32[]{:S(2)}) %copy-start.2) | copy-done | bytes 1048600
  9.6 0.3 project_gates.1.gates_ref
  9.9 0.0 copy-start.7
  10.0 0.8 %collective-permute-start.3 = (bf16[256,512]{1,0:T(8,128)(2,1)S(1)}, bf16[256,512]{1,0:T(8,128)(2,1)S(1)}, u32[]{:S(2)}, u32[]{:S(2)}) collective-permute-start(bf16[256,512]{1,0:T(8,128)(2,1)S(1)} %get-tuple-element.33.refs_2_.refs_8_), channel_id=1, source_target_pairs={{2,1},{1,2},{10,9},{9,10},{18,17},{17,18},{26,25},{25,26}} | collective-permute-start | bytes 786440 | tf_op jit(solution)/shard_map/ppermute | solution.py:195
  11.4 2.7 %collective-permute-done.1.refs_0_ = bf16[512,512]{1,0:T(8,128)(2,1)S(1)} collective-permute-done((bf16[512,512]{1,0:T(8,128)(2,1)}, bf16[512,512]{1,0:T(8,128)(2,1)S(1)}, u32[]{:S(2)}, u32[]{:S(2)}) %collective-permute-start.1) | collective-permute-done | bytes 524320 | tf_op jit(solution)/shard_map/ppermute | solution.py:192
  14.1 0.7 %collective-permute-start.2 = (bf16[272,512]{1,0:T(8,128)(2,1)S(1)}, bf16[272,512]{1,0:T(8,128)(2,1)S(1)}, u32[]{:S(2)}, u32[]{:S(2)}) collective-permute-start(bf16[272,512]{1,0:T(8,128)(2,1)S(1)} %get-tuple-element.32.refs_2_.refs_5_.refs_11_), channel_id=1, source_target_pairs={{6,5},{5,6},{14,13},{13,14},{22,21},{21,22},{30,29},{29,30}} | collective-permute-start | bytes 835592 | tf_op jit(solution)/shard_map/ppermute | solution.py:195
  14.8 0.7 %collective-permute-start.4 = (bf16[256,512]{1,0:T(8,128)(2,1)S(1)}, bf16[256,512]{1,0:T(8,128)(2,1)S(1)}, u32[]{:S(2)}, u32[]{:S(2)}) collective-permute-start(bf16[256,512]{1,0:T(8,128)(2,1)S(1)} %get-tuple-element.33.refs_2_.refs_8_), channel_id=1, source_target_pairs={{6,5},{5,6},{14,13},{13,14},{22,21},{21,22},{30,29},{29,30}} | collective-permute-start | bytes 786440 | tf_op jit(solution)/shard_map/ppermute | solution.py:195
  15.5 2.4 %own_far1.1 = (f32[256,512]{1,0:T(8,128)S(1)}, bf16[512,512]{1,0:T(8,128)(2,1)S(1)}, bf16[512,512]{1,0:T(8,128)(2,1)S(1)}, f32[8,512]{1,0:T(8,128)S(1)}) custom-call(s32[1]{0:T(128)S(6)} %copy.10.length_ref, bf16[512,512]{1,0:T(8,128)(2,1)S(1)} %collective-permute-done.1.refs_0_, s32[1,512]{1,0:T(1,128)S(1)} %collective-permute-done.5.refs_1_, ...), custom_call_target="tpu_custom_call" | custom-call | flops 4294967296 | bytes 2887684 | tf_op jit(solution)/shard_map/own_far1/pallas_call | solution.py:280
  17.9 1.8 %collective-permute-done.6.refs_3_ = bf16[256,512]{1,0:T(8,128)(2,1)S(1)} collective-permute-done((bf16[256,512]{1,0:T(8,128)(2,1)S(1)}, bf16[256,512]{1,0:T(8,128)(2,1)S(1)}, u32[]{:S(2)}, u32[]{:S(2)}) %collective-permute-start.6) | collective-permute-done | bytes 262176 | tf_op jit(solution)/shard_map/ppermute | solution.py:216
  19.6 1.6 %theirs_far1.1 = (f32[256,512]{1,0:T(8,128)S(1)}, bf16[256,512]{1,0:T(8,128)(2,1)S(1)}) custom-call(s32[1]{0:T(128)S(6)} %copy.10.length_ref, bf16[512,512]{1,0:T(8,128)(2,1)S(1)} %get-tuple-element.36.refs_0_, bf16[512,512]{1,0:T(8,128)(2,1)S(1)} %get-tuple-element.37.refs_1_, f32[8,512]{1,0:T(8,128)S(1)} %get-tuple-element.38.refs_2_, ...), custom_call_target="tpu_custom_call" | custom-call | flops 805306368 | bytes 2375684 | tf_op jit(solution)/shard_map/theirs_far1/pallas_call | solution.py:280
  21.3 1.1 %theirs_near0.1.refs_9_ = f32[256,512]{1,0:T(8,128)S(1)} custom-call(s32[1]{0:T(128)S(6)} %copy.10.length_ref, bf16[272,512]{1,0:T(8,128)(2,1)S(1)} %collective-permute-done.refs_0_.refs_3_.refs_9_, bf16[272,512]{1,0:T(8,128)(2,1)S(1)} %collective-permute-done.2.refs_1_.refs_4_.refs_10_, bf16[272,512]{1,0:T(8,128)(2,1)S(1)} %get-tuple-element.32.refs_2_.refs_5_.refs_11_, ...), custom_call_target="tpu_custom_call" | custom-call | flops 402653184 | bytes 3508228 | tf_op jit(solution)/shard_map/theirs_near0/pallas_call | solution.py:280
  22.4 1.2 %theirs_near1.1 = bf16[256,512]{1,0:T(8,128)(2,1)S(1)} custom-call(s32[1]{0:T(128)S(6)} %copy.10.length_ref, bf16[256,512]{1,0:T(8,128)(2,1)S(1)} %collective-permute-done.3.refs_0_.refs_6_, bf16[256,512]{1,0:T(8,128)(2,1)S(1)} %collective-permute-done.4.refs_1_.refs_7_, bf16[256,512]{1,0:T(8,128)(2,1)S(1)} %get-tuple-element.33.refs_2_.refs_8_, ...), custom_call_target="tpu_custom_call" | custom-call | flops 402653184 | bytes 3459076 | tf_op jit(solution)/shard_map/theirs_near1/pallas_call | solution.py:280
  23.6 0.0 copy-start.6
  23.6 6.1 %collective-permute-start.7 = (bf16[256,512]{1,0:T(8,128)(2,1)S(1)}, bf16[256,512]{1,0:T(8,128)(2,1)S(1)}, u32[]{:S(2)}, u32[]{:S(2)}) collective-permute-start(bf16[256,512]{1,0:T(8,128)(2,1)S(1)} %theirs_near1.1), channel_id=1, source_target_pairs={{0,1},{1,0},{2,3},{3,2},{4,5},{5,4},{6,7},{7,6},{8,9},{9,8},{10,11... | collective-permute-start | bytes 786440 | tf_op jit(solution)/shard_map/ppermute | solution.py:317
  29.8 2.4 %own_near.1.total_ref = f32[256,512]{1,0:T(8,128)S(1)} custom-call(s32[1]{0:T(128)S(6)} %copy.10.length_ref, bf16[272,512]{1,0:T(8,128)(2,1)S(1)} %collective-permute-done.refs_0_.refs_3_.refs_9_, bf16[272,512]{1,0:T(8,128)(2,1)S(1)} %collective-permute-done.2.refs_1_.refs_4_.refs_10_, bf16[272,512]{1,0:T(8,128)(2,1)S(1)} %get-tuple-element.32.refs_2_.refs_5_.refs_11_, ...), custom_call_target="tpu_custom_call" | custom-call | flops 4294967296 | bytes 6178820 | tf_op jit(solution)/shard_map/own_near/pallas_call | solution.py:280
  32.1 2.1 %collective-permute-done.7.other_ref = bf16[256,512]{1,0:T(8,128)(2,1)S(1)} collective-permute-done((bf16[256,512]{1,0:T(8,128)(2,1)S(1)}, bf16[256,512]{1,0:T(8,128)(2,1)S(1)}, u32[]{:S(2)}, u32[]{:S(2)}) %collective-permute-start.7) | collective-permute-done | bytes 262176 | tf_op jit(solution)/shard_map/ppermute | solution.py:317
  34.2 1.2 %finish.1 = bf16[256,512]{1,0:T(8,128)(2,1)} custom-call(f32[256,512]{1,0:T(8,128)S(1)} %own_near.1.total_ref, bf16[256,512]{1,0:T(8,128)(2,1)S(1)} %collective-permute-done.7.other_ref, f32[256,512]{1,0:T(8,128)S(1)} %project_gates.1.gates_ref, f32[1,512]{1,0:T(1,128)S(1)} %bitcast.16, bf16[512,512]{1,0:T(8,128)(2,1)S(1)} %copy-done.6, ...), custom_call_target="tpu_custom_call" | custom-call | flops 134217728 | bytes 1048576 | tf_op jit(solution)/shard_map/finish/pallas_call | solution.py:319
  (18 shorter events, 0.0 us)
Async XLA Ops:
  0.0 6.3 %copy-start.4 = (bf16[1,256,512]{2,1,0:T(8,128)(2,1)S(1)}, bf16[1,256,512]{2,1,0:T(8,128)(2,1)}, u32[]{:S(2)}) copy-start(bf16[1,256,512]{2,1,0:T(8,128)(2,1)} %param.10) | copy-start | bytes 786436
  0.0 14.1 %collective-permute-start.1 = (bf16[512,512]{1,0:T(8,128)(2,1)}, bf16[512,512]{1,0:T(8,128)(2,1)S(1)}, u32[]{:S(2)}, u32[]{:S(2)}) collective-permute-start(bf16[512,512]{1,0:T(8,128)(2,1)} %bitcast.10), channel_id=1, source_target_pairs={{1,0},{3,1},{0,2},{2,3},{5,4},{7,5},{4,6},{6,7},{9,8},{11,9},{8,10... | collective-permute-start | bytes 1572872 | tf_op jit(solution)/shard_map/ppermute | solution.py:192
  3.1 1.1 %copy-start.5 = (bf16[1,512,512]{2,1,0:T(8,128)(2,1)S(1)}, bf16[1,512,512]{2,1,0:T(8,128)(2,1)}, u32[]{:S(2)}) copy-start(bf16[1,512,512]{2,1,0:T(8,128)(2,1)} %param.9) | copy-start | bytes 1572868
  5.0 9.8 %collective-permute-start.5 = (s32[1,512]{1,0:T(1,128)}, s32[1,512]{1,0:T(1,128)S(1)}, u32[]{:S(2)}, u32[]{:S(2)}) collective-permute-start(s32[1,512]{1,0:T(1,128)} %labels_ref.1), channel_id=1, source_target_pairs={{1,0},{3,1},{0,2},{2,3},{5,4},{7,5},{4,6},{6,7},{9,8},{11,9},{8,10... | collective-permute-start | bytes 6152 | tf_op jit(solution)/shard_map/ppermute | solution.py:192
  6.3 13.3 %collective-permute-start.6 = (bf16[256,512]{1,0:T(8,128)(2,1)S(1)}, bf16[256,512]{1,0:T(8,128)(2,1)S(1)}, u32[]{:S(2)}, u32[]{:S(2)}) collective-permute-start(bf16[256,512]{1,0:T(8,128)(2,1)S(1)} %bitcast.5), channel_id=1, source_target_pairs={{0,1},{1,0},{2,3},{3,2},{4,5},{5,4},{6,7},{7,6},{8,9},{9,8},{10,11... | collective-permute-start | bytes 786440 | tf_op jit(solution)/shard_map/ppermute | solution.py:216
  6.5 14.8 %collective-permute-start = (bf16[272,512]{1,0:T(8,128)(2,1)S(1)}, bf16[272,512]{1,0:T(8,128)(2,1)S(1)}, u32[]{:S(2)}, u32[]{:S(2)}) collective-permute-start(bf16[272,512]{1,0:T(8,128)(2,1)S(1)} %get-tuple-element.32.refs_2_.refs_5_.refs_11_), channel_id=1, source_target_pairs={{2,1},{1,2},{10,9},{9,10},{18,17},{17,18},{26,25},{25,26}} | collective-permute-start | bytes 835592 | tf_op jit(solution)/shard_map/ppermute | solution.py:195
  7.2 1.2 %copy-start = (bf16[512,1024]{1,0:T(8,128)(2,1)S(1)}, bf16[512,1024]{1,0:T(8,128)(2,1)}, u32[]{:S(2)}) copy-start(bf16[512,1024]{1,0:T(8,128)(2,1)} %refs_12_.1) | copy-start | bytes 3145732
  8.4 1.2 %copy-start.2 = (bf16[512,1024]{1,0:T(8,128)(2,1)S(1)}, bf16[512,1024]{1,0:T(8,128)(2,1)}, u32[]{:S(2)}) copy-start(bf16[512,1024]{1,0:T(8,128)(2,1)} %refs_15_.1) | copy-start | bytes 3145732
  9.6 5.8 %copy-start.1 = (bf16[512,1024]{1,0:T(8,128)(2,1)S(1)}, bf16[512,1024]{1,0:T(8,128)(2,1)}, u32[]{:S(2)}) copy-start(bf16[512,1024]{1,0:T(8,128)(2,1)} %refs_12_.1) | copy-start | bytes 3145732
  9.6 5.9 %copy-start.3 = (bf16[512,1024]{1,0:T(8,128)(2,1)S(1)}, bf16[512,1024]{1,0:T(8,128)(2,1)}, u32[]{:S(2)}) copy-start(bf16[512,1024]{1,0:T(8,128)(2,1)} %refs_15_.1) | copy-start | bytes 3145732
  9.9 5.5 %copy-start.7 = (bf16[128,8]{0,1:T(8,128)(2,1)S(1)}, bf16[128,8]{0,1:T(8,128)(2,1)}, u32[]{:S(2)}) copy-start(bf16[128,8]{0,1:T(8,128)(2,1)} %param.15) | copy-start | bytes 6148
  10.0 12.5 %collective-permute-start.3 = (bf16[256,512]{1,0:T(8,128)(2,1)S(1)}, bf16[256,512]{1,0:T(8,128)(2,1)S(1)}, u32[]{:S(2)}, u32[]{:S(2)}) collective-permute-start(bf16[256,512]{1,0:T(8,128)(2,1)S(1)} %get-tuple-element.33.refs_2_.refs_8_), channel_id=1, source_target_pairs={{2,1},{1,2},{10,9},{9,10},{18,17},{17,18},{26,25},{25,26}} | collective-permute-start | bytes 786440 | tf_op jit(solution)/shard_map/ppermute | solution.py:195
  14.1 7.2 %collective-permute-start.2 = (bf16[272,512]{1,0:T(8,128)(2,1)S(1)}, bf16[272,512]{1,0:T(8,128)(2,1)S(1)}, u32[]{:S(2)}, u32[]{:S(2)}) collective-permute-start(bf16[272,512]{1,0:T(8,128)(2,1)S(1)} %get-tuple-element.32.refs_2_.refs_5_.refs_11_), channel_id=1, source_target_pairs={{6,5},{5,6},{14,13},{13,14},{22,21},{21,22},{30,29},{29,30}} | collective-permute-start | bytes 835592 | tf_op jit(solution)/shard_map/ppermute | solution.py:195
  14.8 7.7 %collective-permute-start.4 = (bf16[256,512]{1,0:T(8,128)(2,1)S(1)}, bf16[256,512]{1,0:T(8,128)(2,1)S(1)}, u32[]{:S(2)}, u32[]{:S(2)}) collective-permute-start(bf16[256,512]{1,0:T(8,128)(2,1)S(1)} %get-tuple-element.33.refs_2_.refs_8_), channel_id=1, source_target_pairs={{6,5},{5,6},{14,13},{13,14},{22,21},{21,22},{30,29},{29,30}} | collective-permute-start | bytes 786440 | tf_op jit(solution)/shard_map/ppermute | solution.py:195
  23.6 10.6 %copy-start.6 = (bf16[512,512]{1,0:T(8,128)(2,1)S(1)}, bf16[512,512]{1,0:T(8,128)(2,1)}, u32[]{:S(2)}) copy-start(bf16[512,512]{1,0:T(8,128)(2,1)} %w_ref.3) | copy-start | bytes 1572868
  23.6 10.6 %collective-permute-start.7 = (bf16[256,512]{1,0:T(8,128)(2,1)S(1)}, bf16[256,512]{1,0:T(8,128)(2,1)S(1)}, u32[]{:S(2)}, u32[]{:S(2)}) collective-permute-start(bf16[256,512]{1,0:T(8,128)(2,1)S(1)} %theirs_near1.1), channel_id=1, source_target_pairs={{0,1},{1,0},{2,3},{3,2},{4,5},{5,4},{6,7},{7,6},{8,9},{9,8},{10,11... | collective-permute-start | bytes 786440 | tf_op jit(solution)/shard_map/ppermute | solution.py:317
  29.8 4.4 %copy-start.8 = (f32[512]{0:T(512)S(1)}, f32[512]{0:T(512)}, u32[]{:S(2)}) copy-start(f32[512]{0:T(512)} %param.16) | copy-start | bytes 6148

commit v7 on v6

--- a/solution.py
+++ b/solution.py
@@ -27,10 +27,10 @@
     return lax.dot_general(a, b, (dims, ((), ())), preferred_element_type=jnp.float32)
 
 
-def project_gates(events_ref, w_ref, w_key_ref, gates_ref):
+def project_gates(events_ref, w_ref, w_key_ref, gain_ref, gates_ref):
     del w_key_ref
     width = events_ref.shape[1]
-    gates_ref[...] = silu(dot(events_ref[...], w_ref[:, width:]))
+    gates_ref[...] = silu(dot(events_ref[...], w_ref[:, width:])) * gain_ref[...]
 
 
 def pack(history_ref, labels_ref, head_ref, rest_ref, sems):
@@ -133,13 +133,13 @@
         total = out_ref
 
 
-def finish(total_ref, other_ref, gates_ref, gain_ref, w_ref, events_ref, out_ref):
+def finish(total_ref, other_ref, gates_ref, w_ref, events_ref, out_ref):
     attended = total_ref[...] + other_ref[...].astype(jnp.float32)
     center = jnp.mean(attended, axis=-1, keepdims=True)
     away = attended - center
     spread = jnp.mean(away * away, axis=-1, keepdims=True)
     normed = away * lax.rsqrt(spread + 1e-05)
-    mixed = (normed * gain_ref[...] * gates_ref[...]).astype(jnp.bfloat16)
+    mixed = (normed * gates_ref[...]).astype(jnp.bfloat16)
     out_ref[...] = (events_ref[...].astype(jnp.float32) + dot(mixed, w_ref[...])).astype(jnp.bfloat16)
 
 
@@ -221,12 +221,12 @@
     gates = pl.pallas_call(
         project_gates,
         out_shape=jax.ShapeDtypeStruct((q_rows, width), jnp.float32),
-        in_specs=[VMEM] * 3,
+        in_specs=[VMEM] * 4,
         out_specs=VMEM,
         compiler_params=PARAMS,
         cost_estimate=cost(2 * q_rows * width * width, queries_in, w_query),
         name="project_gates",
-    )(queries_in, w_query, w_key)
+    )(queries_in, w_query, w_key, out_gain[None])
     rest_own, gates = lax.optimization_barrier((rest_own, gates))
     rests = [send(rest_own, 0, 0)]
     head_own, rest_own, received[1][0] = lax.optimization_barrier(
@@ -319,12 +319,12 @@
     result = pl.pallas_call(
         finish,
         out_shape=jax.ShapeDtypeStruct((q_rows, width), jnp.bfloat16),
-        in_specs=[VMEM] * 6,
+        in_specs=[VMEM] * 5,
         out_specs=VMEM,
         compiler_params=PARAMS,
         cost_estimate=cost(2 * q_rows * width * width, own, w_out),
         name="finish",
-    )(own, theirs, gates, out_gain[None], w_out, queries_in)
+    )(own, theirs, gates, w_out, queries_in)
     return result[None]
 
 

time: 35.7 us -> 35.7 us (level)
  no operation moved by 1% of the time
where the time goes in v7:
time: 35.7 us; the launch traced here: 35.4 us
  starting transfers between devices  13.6 us (38%)
  Pallas kernels  10.9 us (31%)
  waiting for transfers between devices  6.51 us (18%)
  local copies, waits for them, and re-layouts  3.55 us (10%)
  between operations  0.84 us (2%)
    pallas_call x5, Pallas kernels, absorb(): pl.pallas_call(body, out_shape=shapes, in_specs=[SMEM] + [VMEM] * (len(op...  8.61 us
    ppermute x1, starting transfers between devices, on_device(): theirs = lax.ppermute(theirs_sent, 'narrow', swap)  6.13 us
    ppermute x2, starting transfers between devices, send(): return lax.ppermute(x, 'narrow', pairs)  4.49 us
    unnamed x18, local copies, waits for them, and re-layouts  3.55 us
    ppermute x4, starting transfers between devices, send(): return lax.ppermute(x, ('wide', 'narrow'), pairs)  2.82 us
    ppermute x2, waiting for transfers between devices, send(): return lax.ppermute(x, 'narrow', pairs)  2.63 us
    ppermute x1, waiting for transfers between devices, on_device(): theirs = lax.ppermute(theirs_sent, 'narrow', swap)  2.07 us
    ppermute x1, waiting for transfers between devices, on_device(): other_queries = lax.ppermute(queries_out, 'narrow', swap)  1.79 us
  transfers between devices with their start and end apart: 8, of which 3 were waited for; matrix products, arithmetic and copies ran while one was open for 0% of the time, Pallas kernels for 24%

profile of v7, /device:TPU:1, one launch (start us, length us, event | category | flops | bytes accessed | tf_op | source)
XLA Modules:
  0.0 35.4 jit_solution(12475817340422859595)
XLA Ops:
  0.0 3.1 %collective-permute-start.1 = (bf16[512,512]{1,0:T(8,128)(2,1)}, bf16[512,512]{1,0:T(8,128)(2,1)S(1)}, u32[]{:S(2)}, u32[]{:S(2)}) collective-permute-start(bf16[512,512]{1,0:T(8,128)(2,1)} %bitcast.10), channel_id=1, source_target_pairs={{1,0},{3,1},{0,2},{2,3},{5,4},{7,5},{4,6},{6,7},{9,8},{11,9},{8,10... | collective-permute-start | bytes 1572872 | tf_op jit(solution)/shard_map/ppermute | solution.py:192
  3.1 1.1 %copy-done.5 = bf16[1,512,512]{2,1,0:T(8,128)(2,1)S(1)} copy-done((bf16[1,512,512]{2,1,0:T(8,128)(2,1)S(1)}, bf16[1,512,512]{2,1,0:T(8,128)(2,1)}, u32[]{:S(2)}) %copy-start.5) | copy-done | bytes 524312
  4.2 0.7 %pack.1 = (bf16[272,512]{1,0:T(8,128)(2,1)S(1)}, bf16[256,512]{1,0:T(8,128)(2,1)S(1)}) custom-call(bf16[512,512]{1,0:T(8,128)(2,1)S(1)} %bitcast.11, s32[1,512]{1,0:T(1,128)} %labels_ref.1), custom_call_target="tpu_custom_call" | custom-call | tf_op jit(solution)/shard_map/pack/pallas_call | solution.py:201
  5.0 1.3 %collective-permute-start.5 = (s32[1,512]{1,0:T(1,128)}, s32[1,512]{1,0:T(1,128)S(1)}, u32[]{:S(2)}, u32[]{:S(2)}) collective-permute-start(s32[1,512]{1,0:T(1,128)} %labels_ref.1), channel_id=1, source_target_pairs={{1,0},{3,1},{0,2},{2,3},{5,4},{7,5},{4,6},{6,7},{9,8},{11,9},{8,10... | collective-permute-start | bytes 6152 | tf_op jit(solution)/shard_map/ppermute | solution.py:192
  6.3 0.2 collective-permute-start.6
  6.5 0.7 %collective-permute-start = (bf16[272,512]{1,0:T(8,128)(2,1)S(1)}, bf16[272,512]{1,0:T(8,128)(2,1)S(1)}, u32[]{:S(2)}, u32[]{:S(2)}) collective-permute-start(bf16[272,512]{1,0:T(8,128)(2,1)S(1)} %get-tuple-element.32.refs_2_.refs_5_.refs_11_), channel_id=1, source_target_pairs={{2,1},{1,2},{10,9},{9,10},{18,17},{17,18},{26,25},{25,26}} | collective-permute-start | bytes 835592 | tf_op jit(solution)/shard_map/ppermute | solution.py:195
  7.2 1.2 %copy-done = bf16[512,1024]{1,0:T(8,128)(2,1)S(1)} copy-done((bf16[512,1024]{1,0:T(8,128)(2,1)S(1)}, bf16[512,1024]{1,0:T(8,128)(2,1)}, u32[]{:S(2)}) %copy-start) | copy-done | bytes 1048600
  8.4 1.2 %copy-done.3 = bf16[512,1024]{1,0:T(8,128)(2,1)S(1)} copy-done((bf16[512,1024]{1,0:T(8,128)(2,1)S(1)}, bf16[512,1024]{1,0:T(8,128)(2,1)}, u32[]{:S(2)}) %copy-start.3) | copy-done | bytes 1048600
  9.6 0.3 project_gates.1.gates_ref
  10.0 0.0 copy-start.7
  10.0 0.8 %collective-permute-start.3 = (bf16[256,512]{1,0:T(8,128)(2,1)S(1)}, bf16[256,512]{1,0:T(8,128)(2,1)S(1)}, u32[]{:S(2)}, u32[]{:S(2)}) collective-permute-start(bf16[256,512]{1,0:T(8,128)(2,1)S(1)} %get-tuple-element.33.refs_2_.refs_8_), channel_id=1, source_target_pairs={{2,1},{1,2},{10,9},{9,10},{18,17},{17,18},{26,25},{25,26}} | collective-permute-start | bytes 786440 | tf_op jit(solution)/shard_map/ppermute | solution.py:195
  11.5 2.6 %collective-permute-done.1.refs_0_ = bf16[512,512]{1,0:T(8,128)(2,1)S(1)} collective-permute-done((bf16[512,512]{1,0:T(8,128)(2,1)}, bf16[512,512]{1,0:T(8,128)(2,1)S(1)}, u32[]{:S(2)}, u32[]{:S(2)}) %collective-permute-start.1) | collective-permute-done | bytes 524320 | tf_op jit(solution)/shard_map/ppermute | solution.py:192
  14.1 0.7 %collective-permute-start.2 = (bf16[272,512]{1,0:T(8,128)(2,1)S(1)}, bf16[272,512]{1,0:T(8,128)(2,1)S(1)}, u32[]{:S(2)}, u32[]{:S(2)}) collective-permute-start(bf16[272,512]{1,0:T(8,128)(2,1)S(1)} %get-tuple-element.32.refs_2_.refs_5_.refs_11_), channel_id=1, source_target_pairs={{6,5},{5,6},{14,13},{13,14},{22,21},{21,22},{30,29},{29,30}} | collective-permute-start | bytes 835592 | tf_op jit(solution)/shard_map/ppermute | solution.py:195
  14.8 0.7 %collective-permute-start.4 = (bf16[256,512]{1,0:T(8,128)(2,1)S(1)}, bf16[256,512]{1,0:T(8,128)(2,1)S(1)}, u32[]{:S(2)}, u32[]{:S(2)}) collective-permute-start(bf16[256,512]{1,0:T(8,128)(2,1)S(1)} %get-tuple-element.33.refs_2_.refs_8_), channel_id=1, source_target_pairs={{6,5},{5,6},{14,13},{13,14},{22,21},{21,22},{30,29},{29,30}} | collective-permute-start | bytes 786440 | tf_op jit(solution)/shard_map/ppermute | solution.py:195
  15.5 2.4 %own_far1.1 = (f32[256,512]{1,0:T(8,128)S(1)}, bf16[512,512]{1,0:T(8,128)(2,1)S(1)}, bf16[512,512]{1,0:T(8,128)(2,1)S(1)}, f32[8,512]{1,0:T(8,128)S(1)}) custom-call(s32[1]{0:T(128)S(6)} %copy.10.length_ref, bf16[512,512]{1,0:T(8,128)(2,1)S(1)} %collective-permute-done.1.refs_0_, s32[1,512]{1,0:T(1,128)S(1)} %collective-permute-done.5.refs_1_, ...), custom_call_target="tpu_custom_call" | custom-call | flops 4294967296 | bytes 2887684 | tf_op jit(solution)/shard_map/own_far1/pallas_call | solution.py:280
  17.9 1.8 %collective-permute-done.6.refs_3_ = bf16[256,512]{1,0:T(8,128)(2,1)S(1)} collective-permute-done((bf16[256,512]{1,0:T(8,128)(2,1)S(1)}, bf16[256,512]{1,0:T(8,128)(2,1)S(1)}, u32[]{:S(2)}, u32[]{:S(2)}) %collective-permute-start.6) | collective-permute-done | bytes 262176 | tf_op jit(solution)/shard_map/ppermute | solution.py:216
  19.6 1.6 %theirs_far1.1 = (f32[256,512]{1,0:T(8,128)S(1)}, bf16[256,512]{1,0:T(8,128)(2,1)S(1)}) custom-call(s32[1]{0:T(128)S(6)} %copy.10.length_ref, bf16[512,512]{1,0:T(8,128)(2,1)S(1)} %get-tuple-element.36.refs_0_, bf16[512,512]{1,0:T(8,128)(2,1)S(1)} %get-tuple-element.37.refs_1_, f32[8,512]{1,0:T(8,128)S(1)} %get-tuple-element.38.refs_2_, ...), custom_call_target="tpu_custom_call" | custom-call | flops 805306368 | bytes 2375684 | tf_op jit(solution)/shard_map/theirs_far1/pallas_call | solution.py:280
  21.3 1.1 %theirs_near0.1.refs_9_ = f32[256,512]{1,0:T(8,128)S(1)} custom-call(s32[1]{0:T(128)S(6)} %copy.10.length_ref, bf16[272,512]{1,0:T(8,128)(2,1)S(1)} %collective-permute-done.refs_0_.refs_3_.refs_9_, bf16[272,512]{1,0:T(8,128)(2,1)S(1)} %collective-permute-done.2.refs_1_.refs_4_.refs_10_, bf16[272,512]{1,0:T(8,128)(2,1)S(1)} %get-tuple-element.32.refs_2_.refs_5_.refs_11_, ...), custom_call_target="tpu_custom_call" | custom-call | flops 402653184 | bytes 3508228 | tf_op jit(solution)/shard_map/theirs_near0/pallas_call | solution.py:280
  22.4 1.2 %theirs_near1.1 = bf16[256,512]{1,0:T(8,128)(2,1)S(1)} custom-call(s32[1]{0:T(128)S(6)} %copy.10.length_ref, bf16[256,512]{1,0:T(8,128)(2,1)S(1)} %collective-permute-done.3.refs_0_.refs_6_, bf16[256,512]{1,0:T(8,128)(2,1)S(1)} %collective-permute-done.4.refs_1_.refs_7_, bf16[256,512]{1,0:T(8,128)(2,1)S(1)} %get-tuple-element.33.refs_2_.refs_8_, ...), custom_call_target="tpu_custom_call" | custom-call | flops 402653184 | bytes 3459076 | tf_op jit(solution)/shard_map/theirs_near1/pallas_call | solution.py:280
  23.6 0.0 copy-start.6
  23.6 6.1 %collective-permute-start.7 = (bf16[256,512]{1,0:T(8,128)(2,1)S(1)}, bf16[256,512]{1,0:T(8,128)(2,1)S(1)}, u32[]{:S(2)}, u32[]{:S(2)}) collective-permute-start(bf16[256,512]{1,0:T(8,128)(2,1)S(1)} %theirs_near1.1), channel_id=1, source_target_pairs={{0,1},{1,0},{2,3},{3,2},{4,5},{5,4},{6,7},{7,6},{8,9},{9,8},{10,11... | collective-permute-start | bytes 786440 | tf_op jit(solution)/shard_map/ppermute | solution.py:317
  29.8 2.4 %own_near.1.total_ref = f32[256,512]{1,0:T(8,128)S(1)} custom-call(s32[1]{0:T(128)S(6)} %copy.10.length_ref, bf16[272,512]{1,0:T(8,128)(2,1)S(1)} %collective-permute-done.refs_0_.refs_3_.refs_9_, bf16[272,512]{1,0:T(8,128)(2,1)S(1)} %collective-permute-done.2.refs_1_.refs_4_.refs_10_, bf16[272,512]{1,0:T(8,128)(2,1)S(1)} %get-tuple-element.32.refs_2_.refs_5_.refs_11_, ...), custom_call_target="tpu_custom_call" | custom-call | flops 4294967296 | bytes 6178820 | tf_op jit(solution)/shard_map/own_near/pallas_call | solution.py:280
  32.1 2.1 %collective-permute-done.7.other_ref = bf16[256,512]{1,0:T(8,128)(2,1)S(1)} collective-permute-done((bf16[256,512]{1,0:T(8,128)(2,1)S(1)}, bf16[256,512]{1,0:T(8,128)(2,1)S(1)}, u32[]{:S(2)}, u32[]{:S(2)}) %collective-permute-start.7) | collective-permute-done | bytes 262176 | tf_op jit(solution)/shard_map/ppermute | solution.py:317
  34.2 1.2 %finish.1 = bf16[256,512]{1,0:T(8,128)(2,1)} custom-call(f32[256,512]{1,0:T(8,128)S(1)} %own_near.1.total_ref, bf16[256,512]{1,0:T(8,128)(2,1)S(1)} %collective-permute-done.7.other_ref, f32[256,512]{1,0:T(8,128)S(1)} %project_gates.1.gates_ref, bf16[512,512]{1,0:T(8,128)(2,1)S(1)} %copy-done.6, bf16[256,512]{1,0:T(8,128)(2,1)S(1)} %bitcast.9), custom_call_target="tpu_custom_call" | custom-call | flops 134217728 | bytes 1048576 | tf_op jit(solution)/shard_map/finish/pallas_call | solution.py:319
  (18 shorter events, 0.0 us)
Async XLA Ops:
  0.0 6.3 %copy-start.2 = (bf16[1,256,512]{2,1,0:T(8,128)(2,1)S(1)}, bf16[1,256,512]{2,1,0:T(8,128)(2,1)}, u32[]{:S(2)}) copy-start(bf16[1,256,512]{2,1,0:T(8,128)(2,1)} %param.10) | copy-start | bytes 786436
  0.0 14.1 %collective-permute-start.1 = (bf16[512,512]{1,0:T(8,128)(2,1)}, bf16[512,512]{1,0:T(8,128)(2,1)S(1)}, u32[]{:S(2)}, u32[]{:S(2)}) collective-permute-start(bf16[512,512]{1,0:T(8,128)(2,1)} %bitcast.10), channel_id=1, source_target_pairs={{1,0},{3,1},{0,2},{2,3},{5,4},{7,5},{4,6},{6,7},{9,8},{11,9},{8,10... | collective-permute-start | bytes 1572872 | tf_op jit(solution)/shard_map/ppermute | solution.py:192
  3.1 1.1 %copy-start.5 = (bf16[1,512,512]{2,1,0:T(8,128)(2,1)S(1)}, bf16[1,512,512]{2,1,0:T(8,128)(2,1)}, u32[]{:S(2)}) copy-start(bf16[1,512,512]{2,1,0:T(8,128)(2,1)} %param.9) | copy-start | bytes 1572868
  5.0 2.2 %copy-start.8 = (f32[512]{0:T(512)S(1)}, f32[512]{0:T(512)}, u32[]{:S(2)}) copy-start(f32[512]{0:T(512)} %param.16) | copy-start | bytes 6148
  5.0 9.8 %collective-permute-start.5 = (s32[1,512]{1,0:T(1,128)}, s32[1,512]{1,0:T(1,128)S(1)}, u32[]{:S(2)}, u32[]{:S(2)}) collective-permute-start(s32[1,512]{1,0:T(1,128)} %labels_ref.1), channel_id=1, source_target_pairs={{1,0},{3,1},{0,2},{2,3},{5,4},{7,5},{4,6},{6,7},{9,8},{11,9},{8,10... | collective-permute-start | bytes 6152 | tf_op jit(solution)/shard_map/ppermute | solution.py:192
  6.3 13.3 %collective-permute-start.6 = (bf16[256,512]{1,0:T(8,128)(2,1)S(1)}, bf16[256,512]{1,0:T(8,128)(2,1)S(1)}, u32[]{:S(2)}, u32[]{:S(2)}) collective-permute-start(bf16[256,512]{1,0:T(8,128)(2,1)S(1)} %bitcast.5), channel_id=1, source_target_pairs={{0,1},{1,0},{2,3},{3,2},{4,5},{5,4},{6,7},{7,6},{8,9},{9,8},{10,11... | collective-permute-start | bytes 786440 | tf_op jit(solution)/shard_map/ppermute | solution.py:216
  6.5 14.8 %collective-permute-start = (bf16[272,512]{1,0:T(8,128)(2,1)S(1)}, bf16[272,512]{1,0:T(8,128)(2,1)S(1)}, u32[]{:S(2)}, u32[]{:S(2)}) collective-permute-start(bf16[272,512]{1,0:T(8,128)(2,1)S(1)} %get-tuple-element.32.refs_2_.refs_5_.refs_11_), channel_id=1, source_target_pairs={{2,1},{1,2},{10,9},{9,10},{18,17},{17,18},{26,25},{25,26}} | collective-permute-start | bytes 835592 | tf_op jit(solution)/shard_map/ppermute | solution.py:195
  7.2 1.2 %copy-start = (bf16[512,1024]{1,0:T(8,128)(2,1)S(1)}, bf16[512,1024]{1,0:T(8,128)(2,1)}, u32[]{:S(2)}) copy-start(bf16[512,1024]{1,0:T(8,128)(2,1)} %refs_12_.1) | copy-start | bytes 3145732
  8.4 1.2 %copy-start.3 = (bf16[512,1024]{1,0:T(8,128)(2,1)S(1)}, bf16[512,1024]{1,0:T(8,128)(2,1)}, u32[]{:S(2)}) copy-start(bf16[512,1024]{1,0:T(8,128)(2,1)} %refs_15_.1) | copy-start | bytes 3145732
  9.6 5.8 %copy-start.1 = (bf16[512,1024]{1,0:T(8,128)(2,1)S(1)}, bf16[512,1024]{1,0:T(8,128)(2,1)}, u32[]{:S(2)}) copy-start(bf16[512,1024]{1,0:T(8,128)(2,1)} %refs_12_.1) | copy-start | bytes 3145732
  9.6 5.8 %copy-start.4 = (bf16[512,1024]{1,0:T(8,128)(2,1)S(1)}, bf16[512,1024]{1,0:T(8,128)(2,1)}, u32[]{:S(2)}) copy-start(bf16[512,1024]{1,0:T(8,128)(2,1)} %refs_15_.1) | copy-start | bytes 3145732
  10.0 5.5 %copy-start.7 = (bf16[128,8]{0,1:T(8,128)(2,1)S(1)}, bf16[128,8]{0,1:T(8,128)(2,1)}, u32[]{:S(2)}) copy-start(bf16[128,8]{0,1:T(8,128)(2,1)} %param.15) | copy-start | bytes 6148
  10.0 12.4 %collective-permute-start.3 = (bf16[256,512]{1,0:T(8,128)(2,1)S(1)}, bf16[256,512]{1,0:T(8,128)(2,1)S(1)}, u32[]{:S(2)}, u32[]{:S(2)}) collective-permute-start(bf16[256,512]{1,0:T(8,128)(2,1)S(1)} %get-tuple-element.33.refs_2_.refs_8_), channel_id=1, source_target_pairs={{2,1},{1,2},{10,9},{9,10},{18,17},{17,18},{26,25},{25,26}} | collective-permute-start | bytes 786440 | tf_op jit(solution)/shard_map/ppermute | solution.py:195
  14.1 7.2 %collective-permute-start.2 = (bf16[272,512]{1,0:T(8,128)(2,1)S(1)}, bf16[272,512]{1,0:T(8,128)(2,1)S(1)}, u32[]{:S(2)}, u32[]{:S(2)}) collective-permute-start(bf16[272,512]{1,0:T(8,128)(2,1)S(1)} %get-tuple-element.32.refs_2_.refs_5_.refs_11_), channel_id=1, source_target_pairs={{6,5},{5,6},{14,13},{13,14},{22,21},{21,22},{30,29},{29,30}} | collective-permute-start | bytes 835592 | tf_op jit(solution)/shard_map/ppermute | solution.py:195
  14.8 7.7 %collective-permute-start.4 = (bf16[256,512]{1,0:T(8,128)(2,1)S(1)}, bf16[256,512]{1,0:T(8,128)(2,1)S(1)}, u32[]{:S(2)}, u32[]{:S(2)}) collective-permute-start(bf16[256,512]{1,0:T(8,128)(2,1)S(1)} %get-tuple-element.33.refs_2_.refs_8_), channel_id=1, source_target_pairs={{6,5},{5,6},{14,13},{13,14},{22,21},{21,22},{30,29},{29,30}} | collective-permute-start | bytes 786440 | tf_op jit(solution)/shard_map/ppermute | solution.py:195
  23.6 10.6 %copy-start.6 = (bf16[512,512]{1,0:T(8,128)(2,1)S(1)}, bf16[512,512]{1,0:T(8,128)(2,1)}, u32[]{:S(2)}) copy-start(bf16[512,512]{1,0:T(8,128)(2,1)} %w_ref.3) | copy-start | bytes 1572868
  23.6 10.6 %collective-permute-start.7 = (bf16[256,512]{1,0:T(8,128)(2,1)S(1)}, bf16[256,512]{1,0:T(8,128)(2,1)S(1)}, u32[]{:S(2)}, u32[]{:S(2)}) collective-permute-start(bf16[256,512]{1,0:T(8,128)(2,1)S(1)} %theirs_near1.1), channel_id=1, source_target_pairs={{0,1},{1,0},{2,3},{3,2},{4,5},{5,4},{6,7},{7,6},{8,9},{9,8},{10,11... | collective-permute-start | bytes 786440 | tf_op jit(solution)/shard_map/ppermute | solution.py:317
